TPU v7x, 128 devices: a whole 4x4x4 slice. The times are simulated.
128 devices in a mesh: section: 2 (over y_lo), dp: 32 (over x, z, core), tensor: 2 (over y_hi).
Axes of the slice: x: 4, y: 4 (y_hi: 2, y_lo: 2; y = y_hi * 2 + y_lo), z: 4, core: 2. Of those that a mesh axis runs over, the one named last changes fastest.
Arguments:
- inputs: bfloat16 [2, 4608, 1536], P(None, ('dp', 'tensor')), may hold values from -16 to 16
- out_grad: bfloat16 [2, 4608, 1536], P(None, ('dp', 'tensor')), may hold values from -6 to 6
- lengths: int32 [2, 32, 4], replicated, may hold values from 1 to 128, 144 in all within a row
- order: int32 [2, 32], replicated, may hold values from 0 to 31, each once within a row
- gelu_weight: bfloat16 [2, 1536, 2048], P('section', 'dp', 'tensor'), may hold values from -0.15625 to 0.15625
- lru_weight: bfloat16 [2, 1536, 2048], P('section', 'dp', 'tensor'), may hold values from -0.15625 to 0.15625
- rate_weight: bfloat16 [2, 16, 128, 128], P('section', 'tensor', 'dp'), may hold values from -0.5 to 0.5
- input_weight: bfloat16 [2, 16, 128, 128], P('section', 'tensor', 'dp'), may hold values from -0.5 to 0.5
- rate_bias: bfloat16 [2, 16, 128], P('section', 'tensor', 'dp'), may hold values from -3 to 3
- input_bias: bfloat16 [2, 16, 128], P('section', 'tensor', 'dp'), may hold values from -3 to 3
- decay_param: bfloat16 [2, 16, 128], P('section', 'tensor', 'dp'), may hold values from 0.5 to 8
- filter_taps: bfloat16 [2, 4, 16, 128], P('section', None, 'tensor', 'dp'), may hold values from -2 to 2
- filter_bias: bfloat16 [2, 16, 128], P('section', 'tensor', 'dp'), may hold values from -2 to 2
- out_weight: bfloat16 [2, 2048, 1536], P('section', 'tensor', 'dp'), may hold values from -0.25 to 0.25
- gate_weight: bfloat16 [2, 1536, 4608], P('section', 'dp', 'tensor'), may hold values from -0.15625 to 0.15625
- up_weight: bfloat16 [2, 1536, 4608], P('section', 'dp', 'tensor'), may hold values from -0.15625 to 0.15625
- down_weight: bfloat16 [2, 4608, 1536], P('section', 'tensor', 'dp'), may hold values from -0.1875 to 0.1875
- norm_first: bfloat16 [2, 1536], P('section', 'dp'), may hold values from 0.5 to 1.5
- norm_second: bfloat16 [2, 1536], P('section', 'dp'), may hold values from 0.5 to 1.5
Outputs:
- hidden_out: float32 [2, 2, 4608, 1536], P('section', None, ('dp', 'tensor'))
- input_grad: float32 [2, 2, 4608, 1536], P('section', None, ('dp', 'tensor'))
- grad_gelu_weight: float32 [2, 1536, 2048], P('section', 'dp', 'tensor')
- grad_lru_weight: float32 [2, 1536, 2048], P('section', 'dp', 'tensor')
- grad_rate_weight: float32 [2, 16, 128, 128], P('section', 'tensor', 'dp')
- grad_input_weight: float32 [2, 16, 128, 128], P('section', 'tensor', 'dp')
- grad_rate_bias: float32 [2, 16, 128], P('section', 'tensor', 'dp')
- grad_input_bias: float32 [2, 16, 128], P('section', 'tensor', 'dp')
- grad_decay_param: float32 [2, 16, 128], P('section', 'tensor', 'dp')
- grad_filter_taps: float32 [2, 4, 16, 128], P('section', None, 'tensor', 'dp')
- grad_filter_bias: float32 [2, 16, 128], P('section', 'tensor', 'dp')
- grad_out_weight: float32 [2, 2048, 1536], P('section', 'tensor', 'dp')
- grad_gate_weight: float32 [2, 1536, 4608], P('section', 'dp', 'tensor')
- grad_up_weight: float32 [2, 1536, 4608], P('section', 'dp', 'tensor')
- grad_down_weight: float32 [2, 4608, 1536], P('section', 'tensor', 'dp')
- grad_norm_first: float32 [2, 1536], P('section', 'dp')
- grad_norm_second: float32 [2, 1536], P('section', 'dp')
Inputs may be any that keep to these rules, and one draw needn't show every extreme that they name: Each row lengths[m, g, :] holds 4 document lengths that sum to 144; the longest in every row is exactly 128. Each row order[m, :] names every data group exactly once.
All inputs are finite; a program needn't handle non-finite values.
Results may differ from a plain program's by a relative error of at most 0.039.
Values may be sent and summed in bfloat16 or wider, within the bound.
A program may use at most 320 MiB of HBM per device.

v0:
```python
import jax
import jax.numpy as jnp
from jax import lax
from jax.sharding import PartitionSpec as P

epsilon = 1e-06
floor_value = 0.01


def from_behind(block, axis, distance):
    devices = range(lax.axis_size(axis))
    route = [(i - distance, i) for i in devices if i - distance in devices]
    return lax.ppermute(block, axis, route)


def widen(value):
    return lax.optimization_barrier(value).astype(jnp.float32)


def lag_rows(values, offset):
    if offset == 0:
        return values
    zeros_head = jnp.zeros((offset,) + values.shape[1:], values.dtype)
    return jnp.concatenate([zeros_head, values[: values.shape[0] - offset]], axis=0)


def lead_rows(values, offset):
    if offset == 0:
        return values
    zeros_tail = jnp.zeros((offset,) + values.shape[1:], values.dtype)
    return jnp.concatenate([values[offset:], zeros_tail], axis=0)


def document_masks(doc_lengths, group_rows, tap_count):
    doc_ends = jnp.cumsum(doc_lengths, dtype=jnp.int32)
    position = jnp.arange(group_rows, dtype=jnp.int32)
    doc_ident = jnp.sum(
        (position[:, None] >= doc_ends[None, :]).astype(jnp.int32), axis=1, dtype=jnp.int32
    )
    lag_masks = []
    for offset in range(tap_count):
        before = jnp.concatenate(
            [jnp.full((offset,), -1, jnp.int32), doc_ident[: group_rows - offset]]
        )
        lag_masks.append((before == doc_ident).astype(jnp.float32)[:, None])
    return lag_masks


def chain_combine(earlier, later):
    return (earlier[0] * later[0], later[0] * earlier[1] + later[1])


def contract_rows(left, right):
    return lax.dot_general(
        left, right, (((0,), (0,)), ((), ())), preferred_element_type=jnp.float32
    )


def contract_cols(left, right):
    return lax.dot_general(
        left, right, (((1,), (1,)), ((), ())), preferred_element_type=jnp.float32
    )


def rms_back(grad_normed, values, scale):
    return scale * grad_normed - values * scale * scale * scale * jnp.mean(
        grad_normed * values, axis=1, keepdims=True
    )


def spread_rows(normed):
    return lax.all_gather(normed, "tensor", axis=0, tiled=True)


def collect_rows(partial_rows):
    return lax.psum_scatter(partial_rows, "tensor", scatter_dimension=0, tiled=True)


def spread_grads(grads_low):
    return lax.all_gather(grads_low, "tensor", axis=0, tiled=True)


def collect_grads(partial_rows):
    return lax.psum_scatter(partial_rows, "tensor", scatter_dimension=0, tiled=True)


def forward_block(values, weights, lag_masks):
    (
        gelu_weight,
        lru_weight,
        rate_weight,
        input_weight,
        rate_bias,
        input_bias,
        decay_param,
        filter_taps,
        filter_bias,
        out_weight,
        gate_weight,
        up_weight,
        down_weight,
        norm_first,
        norm_second,
    ) = weights
    scale_one = lax.rsqrt(jnp.mean(values * values, axis=1, keepdims=True) + epsilon)
    rows_one = spread_rows(
        (values * scale_one * norm_first.astype(jnp.float32)).astype(jnp.bfloat16)
    )
    group_rows = rows_one.shape[0]
    pre_branch = jnp.dot(rows_one, gelu_weight, preferred_element_type=jnp.float32)
    branch = jax.nn.gelu(pre_branch)
    feature = jnp.dot(rows_one, lru_weight, preferred_element_type=jnp.float32)
    tap_weights = filter_taps.astype(jnp.float32).reshape(filter_taps.shape[0], -1)
    filtered = filter_bias.astype(jnp.float32).reshape(-1)
    for offset in range(tap_weights.shape[0]):
        filtered = filtered + tap_weights[offset] * lag_rows(feature, offset) * lag_masks[offset]
    conv_low = filtered.astype(jnp.bfloat16)
    conv_val = widen(conv_low)
    local_blocks, block_width = (rate_weight.shape[0], rate_weight.shape[1])
    blocks = conv_low.reshape(group_rows, local_blocks, block_width)
    pre_rate = jnp.einsum(
        "gkc,kcd->gkd", blocks, rate_weight, preferred_element_type=jnp.float32
    ) + rate_bias.astype(jnp.float32)
    pre_input = jnp.einsum(
        "gkc,kcd->gkd", blocks, input_weight, preferred_element_type=jnp.float32
    ) + input_bias.astype(jnp.float32)
    rate_gate = jax.nn.sigmoid(pre_rate).reshape(group_rows, -1)
    input_gate = jax.nn.sigmoid(pre_input).reshape(group_rows, -1)
    forget = jax.nn.softplus(-decay_param.astype(jnp.float32)).reshape(-1)
    decay_rate = jnp.exp(-8.0 * rate_gate * forget)
    spare_room = 1.0 - decay_rate * decay_rate
    scale_in = jnp.sqrt(jnp.maximum(spare_room, floor_value))
    carry_decay = decay_rate * lag_masks[1]
    hidden_state = lax.associative_scan(
        chain_combine, (carry_decay, scale_in * input_gate * conv_val)
    )[1]
    mixed_low = (hidden_state * branch).astype(jnp.bfloat16)
    middle = values + collect_rows(
        jnp.dot(mixed_low, out_weight, preferred_element_type=jnp.float32)
    )
    scale_two = lax.rsqrt(jnp.mean(middle * middle, axis=1, keepdims=True) + epsilon)
    rows_two = spread_rows(
        (middle * scale_two * norm_second.astype(jnp.float32)).astype(jnp.bfloat16)
    )
    pre_gate = jnp.dot(rows_two, gate_weight, preferred_element_type=jnp.float32)
    pre_up = jnp.dot(rows_two, up_weight, preferred_element_type=jnp.float32)
    hidden = (jax.nn.gelu(pre_gate) * pre_up).astype(jnp.bfloat16)
    result = middle + collect_rows(jnp.dot(hidden, down_weight, preferred_element_type=jnp.float32))
    kept_values = (
        values,
        scale_one,
        rows_one,
        pre_branch,
        branch,
        feature,
        conv_low,
        rate_gate,
        input_gate,
        forget,
        decay_rate,
        spare_room,
        scale_in,
        carry_decay,
        hidden_state,
        mixed_low,
        middle,
        scale_two,
        rows_two,
        pre_gate,
        pre_up,
        hidden,
    )
    return (result, kept_values)


def backward_feed(incoming, kept_values, weights):
    (
        gelu_weight,
        lru_weight,
        rate_weight,
        input_weight,
        rate_bias,
        input_bias,
        decay_param,
        filter_taps,
        filter_bias,
        out_weight,
        gate_weight,
        up_weight,
        down_weight,
        norm_first,
        norm_second,
    ) = weights
    (
        values,
        scale_one,
        rows_one,
        pre_branch,
        branch,
        feature,
        conv_low,
        rate_gate,
        input_gate,
        forget,
        decay_rate,
        spare_room,
        scale_in,
        carry_decay,
        hidden_state,
        mixed_low,
        middle,
        scale_two,
        rows_two,
        pre_gate,
        pre_up,
        hidden,
    ) = kept_values
    grad_low = spread_grads(incoming.astype(jnp.bfloat16))
    grad_down = contract_rows(hidden, grad_low)
    grad_hidden = contract_cols(grad_low, down_weight)
    act_gate, gelu_pull = jax.vjp(jax.nn.gelu, pre_gate)
    gate_low = gelu_pull(grad_hidden * pre_up)[0].astype(jnp.bfloat16)
    up_low = (grad_hidden * act_gate).astype(jnp.bfloat16)
    grad_gate = contract_rows(rows_two, gate_low)
    grad_up = contract_rows(rows_two, up_low)
    normed_grad = collect_grads(
        contract_cols(gate_low, gate_weight) + contract_cols(up_low, up_weight)
    )
    grad_norm_two = jnp.sum(normed_grad * middle * scale_two, axis=0)
    grad_middle = incoming + rms_back(
        normed_grad * norm_second.astype(jnp.float32), middle, scale_two
    )
    return (grad_middle, (grad_gate, grad_up, grad_down, grad_norm_two))


def backward_mixer(grad_middle, kept_values, weights, lag_masks):
    (
        gelu_weight,
        lru_weight,
        rate_weight,
        input_weight,
        rate_bias,
        input_bias,
        decay_param,
        filter_taps,
        filter_bias,
        out_weight,
        gate_weight,
        up_weight,
        down_weight,
        norm_first,
        norm_second,
    ) = weights
    (
        values,
        scale_one,
        rows_one,
        pre_branch,
        branch,
        feature,
        conv_low,
        rate_gate,
        input_gate,
        forget,
        decay_rate,
        spare_room,
        scale_in,
        carry_decay,
        hidden_state,
        mixed_low,
        middle,
        scale_two,
        rows_two,
        pre_gate,
        pre_up,
        hidden,
    ) = kept_values
    group_rows = rows_one.shape[0]
    local_blocks, block_width = (rate_weight.shape[0], rate_weight.shape[1])
    shape_pair = (local_blocks, block_width)
    conv_val = widen(conv_low)
    middle_low = spread_grads(grad_middle.astype(jnp.bfloat16))
    grad_out_weight = contract_rows(mixed_low, middle_low)
    grad_mixed = contract_cols(middle_low, out_weight)
    grad_state = grad_mixed * branch
    _, branch_pull = jax.vjp(jax.nn.gelu, pre_branch)
    branch_low = branch_pull(grad_mixed * hidden_state)[0].astype(jnp.bfloat16)
    next_decay = lead_rows(carry_decay, 1)
    grad_drive = lax.associative_scan(chain_combine, (next_decay, grad_state), reverse=True)[1]
    grad_decay = grad_drive * lag_rows(hidden_state, 1) * lag_masks[1]
    grad_scale = grad_drive * input_gate * conv_val
    grad_spare = jnp.where(spare_room > floor_value, 0.5 * grad_scale / scale_in, 0.0)
    grad_decay = grad_decay - 2.0 * decay_rate * grad_spare
    grad_log = grad_decay * decay_rate
    rate_low = (grad_log * (-8.0 * forget) * rate_gate * (1.0 - rate_gate)).astype(jnp.bfloat16)
    input_low = (grad_drive * scale_in * conv_val * input_gate * (1.0 - input_gate)).astype(
        jnp.bfloat16
    )
    grad_forget = jnp.sum(grad_log * (-8.0 * rate_gate), axis=0)
    grad_decay_param = -grad_forget * jax.nn.sigmoid(-decay_param.astype(jnp.float32)).reshape(-1)
    conv_blocks = conv_low.reshape(group_rows, local_blocks, block_width)
    rate_blocks = rate_low.reshape(group_rows, local_blocks, block_width)
    input_blocks = input_low.reshape(group_rows, local_blocks, block_width)
    grad_rate_weight = jnp.einsum(
        "gkc,gkd->kcd", conv_blocks, rate_blocks, preferred_element_type=jnp.float32
    )
    grad_input_weight = jnp.einsum(
        "gkc,gkd->kcd", conv_blocks, input_blocks, preferred_element_type=jnp.float32
    )
    grad_rate_bias = jnp.sum(rate_low.astype(jnp.float32), axis=0)
    grad_input_bias = jnp.sum(input_low.astype(jnp.float32), axis=0)
    back_gates = jnp.einsum(
        "gkd,kcd->gkc", rate_blocks, rate_weight, preferred_element_type=jnp.float32
    )
    back_gates = back_gates + jnp.einsum(
        "gkd,kcd->gkc", input_blocks, input_weight, preferred_element_type=jnp.float32
    )
    grad_conv = grad_drive * scale_in * input_gate + back_gates.reshape(group_rows, -1)
    tap_weights = filter_taps.astype(jnp.float32).reshape(filter_taps.shape[0], -1)
    grad_taps = []
    grad_feature = jnp.zeros_like(feature)
    for offset in range(tap_weights.shape[0]):
        masked = grad_conv * lag_masks[offset]
        grad_taps.append(jnp.sum(masked * lag_rows(feature, offset), axis=0))
        grad_feature = grad_feature + lead_rows(masked, offset) * tap_weights[offset]
    grad_filter_bias = jnp.sum(grad_conv, axis=0)
    feature_low = grad_feature.astype(jnp.bfloat16)
    grad_gelu_weight = contract_rows(rows_one, branch_low)
    grad_lru_weight = contract_rows(rows_one, feature_low)
    first_grad = collect_grads(
        contract_cols(branch_low, gelu_weight) + contract_cols(feature_low, lru_weight)
    )
    grad_norm_one = jnp.sum(first_grad * values * scale_one, axis=0)
    grad_values = grad_middle + rms_back(
        first_grad * norm_first.astype(jnp.float32), values, scale_one
    )
    grads = (
        grad_gelu_weight,
        grad_lru_weight,
        grad_rate_weight,
        grad_input_weight,
        grad_rate_bias.reshape(shape_pair),
        grad_input_bias.reshape(shape_pair),
        grad_decay_param.reshape(shape_pair),
        jnp.stack(grad_taps).reshape((tap_weights.shape[0],) + shape_pair),
        grad_filter_bias.reshape(shape_pair),
        grad_out_weight,
        grad_norm_one,
    )
    return (grad_values, grads)


def add_tuples(left_tuple, right_tuple):
    if left_tuple is None:
        return right_tuple
    return tuple(
        (left_total + right_total for left_total, right_total in zip(left_tuple, right_tuple))
    )


def shards(
    inputs,
    out_grad,
    lengths,
    order,
    gelu_weight,
    lru_weight,
    rate_weight,
    input_weight,
    rate_bias,
    input_bias,
    decay_param,
    filter_taps,
    filter_bias,
    out_weight,
    gate_weight,
    up_weight,
    down_weight,
    norm_first,
    norm_second,
):
    group_id = lax.axis_index("dp")
    group_count = lax.axis_size("dp")
    slot_ids = jnp.arange(group_count, dtype=jnp.int32)
    target = lax.dynamic_index_in_dim(order, group_id, 1, keepdims=False)
    send_mask = (slot_ids[:, None] == target[None, :]).astype(jnp.bfloat16)
    send_inputs = send_mask[:, :, None, None] * inputs[None]
    send_cotangent = send_mask[:, :, None, None] * out_grad[None]
    got_inputs, got_cotangent = (
        lax.all_to_all(send_inputs, "dp", split_axis=0, concat_axis=0, tiled=True),
        lax.all_to_all(send_cotangent, "dp", split_axis=0, concat_axis=0, tiled=True),
    )
    dealt_inputs = jnp.sum(got_inputs.astype(jnp.float32), axis=0).astype(jnp.bfloat16)
    dealt_cotangent = jnp.sum(got_cotangent.astype(jnp.float32), axis=0).astype(jnp.bfloat16)
    source_of = jnp.sum(jnp.where(order == group_id, slot_ids[None, :], 0), axis=1, dtype=jnp.int32)
    micro = inputs.shape[0]
    dealt_lengths = lengths[jnp.arange(micro, dtype=jnp.int32), source_of]
    gathered = (
        lax.all_gather(gelu_weight, "dp", axis=1, tiled=True),
        lax.all_gather(lru_weight, "dp", axis=1, tiled=True),
        lax.all_gather(rate_weight, "dp", axis=2, tiled=True),
        lax.all_gather(input_weight, "dp", axis=2, tiled=True),
        lax.all_gather(rate_bias, "dp", axis=2, tiled=True),
        lax.all_gather(input_bias, "dp", axis=2, tiled=True),
        lax.all_gather(decay_param, "dp", axis=2, tiled=True),
        lax.all_gather(filter_taps, "dp", axis=3, tiled=True),
        lax.all_gather(filter_bias, "dp", axis=2, tiled=True),
        lax.all_gather(out_weight, "dp", axis=2, tiled=True),
        lax.all_gather(gate_weight, "dp", axis=1, tiled=True),
        lax.all_gather(up_weight, "dp", axis=1, tiled=True),
        lax.all_gather(down_weight, "dp", axis=2, tiled=True),
        lax.all_gather(norm_first, "dp", axis=1, tiled=True),
        lax.all_gather(norm_second, "dp", axis=1, tiled=True),
    )
    weights = tuple((member[0] for member in gathered))
    section_id = lax.axis_index("section")
    on_first = section_id == 0
    group_rows = inputs.shape[1] * lax.axis_size("tensor")
    tap_count = filter_taps.shape[1]
    received = jnp.zeros(inputs.shape[1:], jnp.bfloat16)
    forward_outs = []
    kept_all = []
    for moment in range(micro + 1):
        index_now = jnp.clip(moment - section_id, 0, micro - 1)
        doc_lengths = lax.dynamic_index_in_dim(dealt_lengths, index_now, 0, keepdims=False)
        lag_masks = document_masks(doc_lengths, group_rows, tap_count)
        start_rows = jnp.where(on_first, dealt_inputs[min(moment, micro - 1)], received).astype(
            jnp.float32
        )
        result, kept_values = forward_block(start_rows, weights, lag_masks)
        low_result = result.astype(jnp.bfloat16)
        forward_outs.append(result)
        kept_all.append((kept_values, tuple(lag_masks)))
        if moment < micro:
            received = from_behind(low_result, "section", 1)
    hidden_out = jnp.stack(
        [
            jnp.where(on_first, forward_outs[number], forward_outs[number + 1])
            for number in range(micro)
        ]
    )[None]
    fetched = (
        lax.all_gather(gelu_weight, "dp", axis=1, tiled=True),
        lax.all_gather(lru_weight, "dp", axis=1, tiled=True),
        lax.all_gather(rate_weight, "dp", axis=2, tiled=True),
        lax.all_gather(input_weight, "dp", axis=2, tiled=True),
        lax.all_gather(rate_bias, "dp", axis=2, tiled=True),
        lax.all_gather(input_bias, "dp", axis=2, tiled=True),
        lax.all_gather(decay_param, "dp", axis=2, tiled=True),
        lax.all_gather(filter_taps, "dp", axis=3, tiled=True),
        lax.all_gather(filter_bias, "dp", axis=2, tiled=True),
        lax.all_gather(out_weight, "dp", axis=2, tiled=True),
        lax.all_gather(gate_weight, "dp", axis=1, tiled=True),
        lax.all_gather(up_weight, "dp", axis=1, tiled=True),
        lax.all_gather(down_weight, "dp", axis=2, tiled=True),
        lax.all_gather(norm_first, "dp", axis=1, tiled=True),
        lax.all_gather(norm_second, "dp", axis=1, tiled=True),
    )
    back_weights = tuple((member[0] for member in fetched))

    def select(first_value, second_value):
        return jnp.where(on_first, first_value, second_value)

    back_received = jnp.zeros(inputs.shape[1:], jnp.bfloat16)
    feed_totals = None
    mixer_totals = None
    input_grads = []
    for period in range(micro + 1):
        kept_pair = jax.tree.map(
            select, kept_all[max(period - 1, 0)], kept_all[min(period + 1, micro)]
        )
        supplied = dealt_cotangent[min(period, micro - 1)].astype(jnp.float32) * (
            1.0 if period < micro else 0.0
        )
        incoming = jnp.where(on_first, back_received.astype(jnp.float32), supplied)
        grad_middle, feed_grads = backward_feed(incoming, kept_pair[0], back_weights)
        feed_totals = add_tuples(feed_totals, feed_grads)
        grad_values, mixer_grads = backward_mixer(
            grad_middle, kept_pair[0], back_weights, list(kept_pair[1])
        )
        mixer_totals = add_tuples(mixer_totals, mixer_grads)
        input_grads.append(grad_values)
        if period < micro:
            back_received = from_behind(grad_values.astype(jnp.bfloat16), "section", -1)
    dealt_back = jnp.stack(
        [
            jnp.where(on_first, input_grads[number + 1], input_grads[number])
            for number in range(micro)
        ]
    )
    return_mask = (slot_ids[:, None] == source_of[None, :]).astype(jnp.float32)
    send_back = return_mask[:, :, None, None] * dealt_back[None]
    got_back = lax.all_to_all(send_back, "dp", split_axis=0, concat_axis=0, tiled=True)
    input_grad = jnp.sum(got_back, axis=0)[None]
    reduced = (
        lax.psum_scatter(mixer_totals[0], "dp", scatter_dimension=0, tiled=True),
        lax.psum_scatter(mixer_totals[1], "dp", scatter_dimension=0, tiled=True),
        lax.psum_scatter(mixer_totals[2], "dp", scatter_dimension=1, tiled=True),
        lax.psum_scatter(mixer_totals[3], "dp", scatter_dimension=1, tiled=True),
        lax.psum_scatter(mixer_totals[4], "dp", scatter_dimension=1, tiled=True),
        lax.psum_scatter(mixer_totals[5], "dp", scatter_dimension=1, tiled=True),
        lax.psum_scatter(mixer_totals[6], "dp", scatter_dimension=1, tiled=True),
        lax.psum_scatter(mixer_totals[7], "dp", scatter_dimension=2, tiled=True),
        lax.psum_scatter(mixer_totals[8], "dp", scatter_dimension=1, tiled=True),
        lax.psum_scatter(mixer_totals[9], "dp", scatter_dimension=1, tiled=True),
        lax.psum_scatter(feed_totals[0], "dp", scatter_dimension=0, tiled=True),
        lax.psum_scatter(feed_totals[1], "dp", scatter_dimension=0, tiled=True),
        lax.psum_scatter(feed_totals[2], "dp", scatter_dimension=1, tiled=True),
        lax.psum_scatter(mixer_totals[10], "dp", scatter_dimension=0, tiled=True),
        lax.psum_scatter(feed_totals[3], "dp", scatter_dimension=0, tiled=True),
    )
    gain_totals = lax.psum((reduced[13], reduced[14]), "tensor")
    return (
        (hidden_out, input_grad)
        + tuple((member[None] for member in reduced[:13]))
        + (gain_totals[0][None], gain_totals[1][None])
    )


def solution(mesh):
    placed = (
        P(None, ("dp", "tensor"), None),
        P(None, ("dp", "tensor"), None),
        P(),
        P(),
        P("section", "dp", "tensor"),
        P("section", "dp", "tensor"),
        P("section", "tensor", "dp", None),
        P("section", "tensor", "dp", None),
        P("section", "tensor", "dp"),
        P("section", "tensor", "dp"),
        P("section", "tensor", "dp"),
        P("section", None, "tensor", "dp"),
        P("section", "tensor", "dp"),
        P("section", "tensor", "dp"),
        P("section", "dp", "tensor"),
        P("section", "dp", "tensor"),
        P("section", "tensor", "dp"),
        P("section", "dp"),
        P("section", "dp"),
    )
    return jax.shard_map(
        shards,
        mesh=mesh,
        in_specs=placed,
        out_specs=(
            P("section", None, ("dp", "tensor"), None),
            P("section", None, ("dp", "tensor"), None),
            P("section", "dp", "tensor"),
            P("section", "dp", "tensor"),
            P("section", "tensor", "dp", None),
            P("section", "tensor", "dp", None),
            P("section", "tensor", "dp"),
            P("section", "tensor", "dp"),
            P("section", "tensor", "dp"),
            P("section", None, "tensor", "dp"),
            P("section", "tensor", "dp"),
            P("section", "tensor", "dp"),
            P("section", "dp", "tensor"),
            P("section", "dp", "tensor"),
            P("section", "tensor", "dp"),
            P("section", "dp"),
            P("section", "dp"),
        ),
        check_vma=False,
    )
```

profile of v0, /device:TPU:0, one launch (start us, length us, event | category | flops | bytes accessed | tf_op | source)
XLA Modules:
  0.0 2789.6 jit_solution(2198833447931921313)
XLA Ops:
  8.8 10.6 broadcast_multiply_fusion.1
  31.5 227.7 %all-reduce.134 = (bf16[1536]{0:T(1024)(128)(2,1)}, bf16[1536]{0:T(1024)(128)(2,1)S(1)}) all-reduce(bf16[1536]{0:T(1024)(128)(2,1)S(1)} %dynamic-update-slice.1, bf16[1536]{0:T(1024)(128)(2,1)S(1)} %dynamic-update-slice), channel_id=1, replica_groups=mesh['section'=2,'dp'=32,'tensor'=2] {'dp'}, use_global_device_ids=true, to_apply=%add.124 | all-reduce | flops 3072 | bytes 12288
  261.7 31.3 %all_gather.93 = bf16[1,8,128]{1,0,2:T(2,128)(2,1)S(1)} all-gather(bf16[1,8,4]{1,0,2:T(2,128)(2,1)S(1)} %copy.174), channel_id=1, replica_groups=mesh['section'=2,'dp'=32,'tensor'=2] {'dp'}, dimensions={2}, use_global_device_ids=true | all-gather | bytes 2112 | tf_op jit(solution)/shard_map/all_gather | solution.py:407
  293.1 21.4 all_gather.100
  314.6 24.0 all_gather.102
  338.7 21.4 all_gather.99
  360.3 24.4 all_gather.94
  384.8 22.0 all_gather.101
  406.9 24.6 all_gather.98
  442.1 10.1 all_gather.96
  478.8 13.3 reduce-scatter.25.cloned.1.call-done
  494.4 9.4 all_gather.106
  503.8 173.3 %all-gather.13.cloned.1.call-done = bf16[1,1536,2304]{2,1,0:T(8,128)(2,1)} async-done(((bf16[1,48,2304]{2,1,0:T(8,128)(2,1)}), bf16[1,1536,2304]{2,1,0:T(8,128)(2,1)}) %all-gather.13.cloned.1.call-update) | async-done | bytes 7077904 | tf_op jit(solution)/shard_map/all_gather | solution.py:409
  681.3 48.7 %all-gather.15.cloned.1.call-done = bf16[1,1536,2304]{2,1,0:T(8,128)(2,1)} async-done(((bf16[1,48,2304]{2,1,0:T(8,128)(2,1)}), bf16[1,1536,2304]{2,1,0:T(8,128)(2,1)}) %all-gather.15.cloned.1.call-update) | async-done | bytes 7077904 | tf_op jit(solution)/shard_map/all_gather | solution.py:410
  735.6 46.3 %all-gather.17.cloned.1.call-done = bf16[1,2304,1536]{1,2,0:T(8,128)(2,1)} async-done(((bf16[1,2304,48]{1,2,0:T(8,128)(2,1)}), bf16[1,2304,1536]{1,2,0:T(8,128)(2,1)}) %all-gather.17.cloned.1.call-update) | async-done | bytes 7077904 | tf_op jit(solution)/shard_map/all_gather | solution.py:411
  788.3 21.7 reduce-scatter.27.cloned.1.call-done
  933.7 13.2 all_gather.114
  954.3 9.9 all_gather.111
  988.4 16.6 reduce-scatter.37.cloned.1.call-done
  1005.0 25.0 reduce-scatter.31.cloned.1.call-done
  1315.9 9.1 reduce-scatter.39.cloned.1.call-done
  1509.7 21.5 reduce-scatter.43.cloned.1.call-done
  1596.5 17.0 reduce-scatter.35.cloned.1.call-done
  1619.1 9.7 all_gather.119
  1823.2 13.2 broadcast_multiply_fusion
  1870.5 266.7 %reduce-scatter.53.cloned.1.call-done = f32[8,4,128]{2,0,1:T(8,128)} async-done(((f32[8,128,128]{2,0,1:T(8,128)}), f32[8,4,128]{2,0,1:T(8,128)}) %reduce-scatter.53.cloned.1.call-update) | async-done | bytes 16400 | tf_op jit(solution)/shard_map/reduce_scatter | solution.py:498
  2138.5 211.9 %all-reduce.132 = (f32[8,128]{1,0:T(8,128)S(1)}, f32[8,128]{1,0:T(8,128)S(1)}, f32[8,128]{1,0:T(8,128)S(1)}, f32[4,8,128]{1,0,2:T(4,128)S(1)}, f32[8,128]{1,0:T(...) all-reduce(f32[8,128]{1,0:T(8,128)S(1)} %add_bitcast_fusion.2, ...), channel_id=18, replica_groups=mesh['section'=2,'dp'=32,'tensor'=2] {'dp'}, use_global_device_ids=true, to_apply=%region_41.42.clone | all-reduce | flops 11264 | bytes 90112
  2361.0 11.1 reduce_sum.468
  2372.1 72.9 %reduce-scatter.49.cloned.1.call-done = f32[48,1024]{1,0:T(8,128)} async-done(((f32[1536,1024]{1,0:T(8,128)}), f32[48,1024]{1,0:T(8,128)}) %reduce-scatter.49.cloned.1.call-update) | async-done | bytes 196624 | tf_op jit(solution)/shard_map/reduce_scatter | solution.py:496
  2445.0 112.6 %reduce-scatter.59.cloned.1.call-done = f32[48,2304]{1,0:T(8,128)} async-done(((f32[1536,2304]{1,0:T(8,128)}), f32[48,2304]{1,0:T(8,128)}) %reduce-scatter.59.cloned.1.call-update) | async-done | bytes 442384 | tf_op jit(solution)/shard_map/reduce_scatter | solution.py:506
  2557.6 112.3 %reduce-scatter.61.cloned.1.call-done = f32[48,2304]{1,0:T(8,128)} async-done(((f32[1536,2304]{1,0:T(8,128)}), f32[48,2304]{1,0:T(8,128)}) %reduce-scatter.61.cloned.1.call-update) | async-done | bytes 442384 | tf_op jit(solution)/shard_map/reduce_scatter | solution.py:507
  2669.9 112.6 %reduce-scatter.63.cloned.1.call-done = f32[2304,48]{0,1:T(8,128)} async-done(((f32[2304,1536]{0,1:T(8,128)}), f32[2304,48]{0,1:T(8,128)}) %reduce-scatter.63.cloned.1.call-update) | async-done | bytes 442384 | tf_op jit(solution)/shard_map/reduce_scatter | solution.py:508
  (1364 shorter events, 1003.0 us)
Async XLA Ops:
  7.2 445.0 %all-gather.7.cloned.1.call-start = ((), (), s32[]{:S(2)}) async-start(), calls=%async_computation.23 | async-start | bytes 3244032 | tf_op jit(solution)/shard_map/all_gather | solution.py:400
  19.6 414.1 %all-to-all-start = ((bf16[32,2,72,1536]{3,2,1,0:T(8,128)(2,1)}), bf16[32,2,72,1536]{3,2,1,0:T(8,128)(2,1)}, u32[]{:S(2)}, u32[]{:S(2)}) async-start(bf16[32,2,72,1536]{3,2,1,0:T(8,128)(2,1)} %get-tuple-element.309), calls=%async_computation | async-start | bytes 28311552 | tf_op jit(solution)/shard_map/all_to_all | solution.py:390
  28.1 435.7 %all-gather.9.cloned.1.call-start = ((), (), s32[]{:S(2)}) async-start(), calls=%async_computation.24 | async-start | bytes 3244032 | tf_op jit(solution)/shard_map/all_gather | solution.py:399
  28.8 438.7 %all-gather.11.cloned.1.call-start = ((), (), s32[]{:S(2)}) async-start(), calls=%async_computation.25 | async-start | bytes 3244032 | tf_op jit(solution)/shard_map/all_gather | solution.py:408
  29.6 462.5 %reduce-scatter.25.cloned.1.call-start = ((), (), s32[]{:S(2)}) async-start(), calls=%async_computation.26 | async-start | bytes 1327104 | tf_op jit(solution)/shard_map/reduce_scatter | solution.py:76
  471.7 205.4 %all-gather.13.cloned.1.call-start = ((), (), s32[]{:S(2)}) async-start(), calls=%async_computation.27 | async-start | bytes 7299072 | tf_op jit(solution)/shard_map/all_gather | solution.py:409
  472.2 257.8 %all-gather.15.cloned.1.call-start = ((), (), s32[]{:S(2)}) async-start(), calls=%async_computation.28 | async-start | bytes 7299072 | tf_op jit(solution)/shard_map/all_gather | solution.py:410
  472.8 309.0 %all-gather.17.cloned.1.call-start = ((), (), s32[]{:S(2)}) async-start(), calls=%async_computation.29 | async-start | bytes 7299072 | tf_op jit(solution)/shard_map/all_gather | solution.py:411
  473.6 451.0 %all-to-all-start.1 = ((bf16[32,2,72,1536]{3,2,1,0:T(8,128)(2,1)}), bf16[32,2,72,1536]{3,2,1,0:T(8,128)(2,1)}, u32[]{:S(2)}, u32[]{:S(2)}) async-start(bf16[32,2,72,1536]{3,2,1,0:T(8,128)(2,1)} %get-tuple-element.308), calls=%async_computation.7 | async-start | bytes 28311552 | tf_op jit(solution)/shard_map/all_to_all | solution.py:391
  478.7 331.2 %reduce-scatter.27.cloned.1.call-start = ((), (), s32[]{:S(2)}) async-start(), calls=%async_computation.30 | async-start | bytes 1327104 | tf_op jit(solution)/shard_map/reduce_scatter | solution.py:76
  788.2 163.6 %reduce-scatter.29.cloned.1.call-start = ((), (), s32[]{:S(2)}) async-start(), calls=%async_computation.31 | async-start | bytes 1327104 | tf_op jit(solution)/shard_map/reduce_scatter | solution.py:76
  924.5 80.5 %reduce-scatter.37.cloned.1.call-start = ((), (), s32[]{:S(2)}) async-start(), calls=%async_computation.35 | async-start | bytes 1327104 | tf_op jit(solution)/shard_map/reduce_scatter | solution.py:84
  981.7 48.3 %reduce-scatter.31.cloned.1.call-start = ((), (), s32[]{:S(2)}) async-start(), calls=%async_computation.32 | async-start | bytes 1327104 | tf_op jit(solution)/shard_map/reduce_scatter | solution.py:76
  988.4 183.4 %reduce-scatter.33.cloned.1.call-start = ((), (), s32[]{:S(2)}) async-start(), calls=%async_computation.33 | async-start | bytes 1327104 | tf_op jit(solution)/shard_map/reduce_scatter | solution.py:76
  1033.6 7.3 collective-permute-start.1
  1146.3 178.7 %reduce-scatter.39.cloned.1.call-start = ((), (), s32[]{:S(2)}) async-start(), calls=%async_computation.36 | async-start | bytes 1327104 | tf_op jit(solution)/shard_map/reduce_scatter | solution.py:84
  1301.2 79.1 %reduce-scatter.41.cloned.1.call-start = ((), (), s32[]{:S(2)}) async-start(), calls=%async_computation.37 | async-start | bytes 1327104 | tf_op jit(solution)/shard_map/reduce_scatter | solution.py:84
  1329.3 9.5 collective-permute-start.2
  1355.9 175.3 %reduce-scatter.43.cloned.1.call-start = ((), (), s32[]{:S(2)}) async-start(), calls=%async_computation.38 | async-start | bytes 1327104 | tf_op jit(solution)/shard_map/reduce_scatter | solution.py:84
  1509.6 86.9 %reduce-scatter.45.cloned.1.call-start = ((), (), s32[]{:S(2)}) async-start(), calls=%async_computation.39 | async-start | bytes 1327104 | tf_op jit(solution)/shard_map/reduce_scatter | solution.py:84
  1536.2 9.1 collective-permute-start.3
  1567.2 46.3 %reduce-scatter.35.cloned.1.call-start = ((), (), s32[]{:S(2)}) async-start(), calls=%async_computation.34 | async-start | bytes 1327104 | tf_op jit(solution)/shard_map/reduce_scatter | solution.py:76
  1573.8 246.5 %reduce-scatter.47.cloned.1.call-start = ((), (), s32[]{:S(2)}) async-start(), calls=%async_computation.40 | async-start | bytes 1327104 | tf_op jit(solution)/shard_map/reduce_scatter | solution.py:84
  1741.6 127.6 %reduce-scatter.55.cloned.1.call-start = ((), (), s32[]{:S(2)}) async-start(), calls=%async_computation.44 | async-start | bytes 540672 | tf_op jit(solution)/shard_map/reduce_scatter | solution.py:499
  1746.2 390.9 %reduce-scatter.53.cloned.1.call-start = ((), (), s32[]{:S(2)}) async-start(), calls=%async_computation.43 | async-start | bytes 540672 | tf_op jit(solution)/shard_map/reduce_scatter | solution.py:498
  1752.5 619.5 %reduce-scatter.57.cloned.1.call-start = ((), (), s32[]{:S(2)}) async-start(), calls=%async_computation.45 | async-start | bytes 6488064 | tf_op jit(solution)/shard_map/reduce_scatter | solution.py:505
  1760.4 611.7 %reduce-scatter.51.cloned.1.call-start = ((), (), s32[]{:S(2)}) async-start(), calls=%async_computation.42 | async-start | bytes 6488064 | tf_op jit(solution)/shard_map/reduce_scatter | solution.py:497
  1767.5 677.4 %reduce-scatter.49.cloned.1.call-start = ((), (), s32[]{:S(2)}) async-start(), calls=%async_computation.41 | async-start | bytes 6488064 | tf_op jit(solution)/shard_map/reduce_scatter | solution.py:496
  1774.4 783.2 %reduce-scatter.59.cloned.1.call-start = ((), (), s32[]{:S(2)}) async-start(), calls=%async_computation.46 | async-start | bytes 14598144 | tf_op jit(solution)/shard_map/reduce_scatter | solution.py:506
  1797.2 872.7 %reduce-scatter.61.cloned.1.call-start = ((), (), s32[]{:S(2)}) async-start(), calls=%async_computation.47 | async-start | bytes 14598144 | tf_op jit(solution)/shard_map/reduce_scatter | solution.py:507
  1836.4 524.6 %all-to-all-start.2 = ((f32[32,2,72,1536]{3,2,1,0:T(8,128)}), f32[32,2,72,1536]{3,2,1,0:T(8,128)}, u32[]{:S(2)}, u32[]{:S(2)}) async-start(f32[32,2,72,1536]{3,2,1,0:T(8,128)} %broadcast_multiply_fusion), calls=%async_computation.14 | async-start | bytes 56623104 | tf_op jit(solution)/shard_map/all_to_all | solution.py:493
  1843.9 938.6 %reduce-scatter.63.cloned.1.call-start = ((), (), s32[]{:S(2)}) async-start(), calls=%async_computation.48 | async-start | bytes 14598144 | tf_op jit(solution)/shard_map/reduce_scatter | solution.py:508
  (290 other events, 4715.3 us)
Sparse Core Ops, SparseCore 0:
  10.3 150.4 all-gather.6
  163.0 73.0 all-gather.8
  238.4 46.3 all-gather.10
  471.8 20.2 reduce-scatter.24
  494.2 182.8 all-gather.12
  679.2 50.7 all-gather.14
  732.3 49.5 all-gather.16
  788.3 21.5 reduce-scatter.26
  924.6 27.1 reduce-scatter.28
  981.9 23.1 reduce-scatter.36
  1008.0 21.9 reduce-scatter.30
  1146.4 23.8 reduce-scatter.32
  1301.3 23.6 reduce-scatter.38
  1356.0 21.3 reduce-scatter.40
  1509.7 21.3 reduce-scatter.42
  1567.3 21.3 reduce-scatter.44
  1591.6 21.9 reduce-scatter.34
  1741.7 21.8 reduce-scatter.46
  1767.0 76.4 reduce-scatter.54
  1846.8 290.3 reduce-scatter.52
  2141.5 122.6 reduce-scatter.56
  2269.0 86.0 reduce-scatter.50
  2359.4 85.5 reduce-scatter.48
  2449.8 107.7 reduce-scatter.58
  2562.1 107.7 reduce-scatter.60
  2674.7 107.7 reduce-scatter.62
where the time goes:
time: 2820 us; the launch traced here: 2790 us
  waiting for transfers between devices  1100 us (39%)
  blocking collectives  728 us (26%)
  local copies, waits for them, and re-layouts  447 us (16%)
  other arithmetic  250 us (9%)
  matrix products  215 us (8%)
  starting transfers between devices  31.6 us (1%)
    unnamed x2, blocking collectives  440 us
    reduce_scatter x1, waiting for transfers between devices, shards(): lax.psum_scatter(mixer_totals[2], 'dp', scatter_dimension=1, tiled=True)  267 us
    slice x135, local copies, waits for them, and re-layouts, backward_mixer(): lax.associative_scan(chain_combine, (next_decay, grad_state), reverse=True)  209 us
    all_gather x1, waiting for transfers between devices, shards(): lax.all_gather(gate_weight, 'dp', axis=1, tiled=True)  173 us
    reduce_scatter x1, waiting for transfers between devices, shards(): lax.psum_scatter(feed_totals[0], 'dp', scatter_dimension=0, tiled=True)  113 us
    reduce_scatter x1, waiting for transfers between devices, shards(): lax.psum_scatter(feed_totals[2], 'dp', scatter_dimension=1, tiled=True)  113 us
    reduce_scatter x1, waiting for transfers between devices, shards(): lax.psum_scatter(feed_totals[1], 'dp', scatter_dimension=0, tiled=True)  112 us
    slice x117, local copies, waits for them, and re-layouts, forward_block(): lax.associative_scan(chain_combine, (carry_decay, scale_in * input_gate *...  94.7 us
  transfers between devices with their start and end apart: 33, of which 20 were waited for; matrix products, arithmetic and copies ran while one was open for 14% of the time, Pallas kernels for 0%

commit v1 on v0

--- a/solution.py
+++ b/solution.py
@@ -1,10 +1,140 @@
 import jax
 import jax.numpy as jnp
 from jax import lax
+from jax.experimental import pallas as pl
+from jax.experimental.pallas import tpu as pltpu
 from jax.sharding import PartitionSpec as P
 
 epsilon = 1e-06
 floor_value = 0.01
+
+
+MESH = pl.DeviceIdType.MESH
+ROWS = 48
+
+def ag_body(w_ref, g_ref, lsem, s1s, s1r, s2s, s2r, s3s, s3r, K, L=1, SIB=True):
+    dp = lax.axis_index("dp")
+    c = dp % 2; z = (dp // 2) % 4; x = dp // 8
+    def at(dx, dz):
+        return ((x + dx) % 4) * 8 + ((z + dz) % 4) * 2 + c
+    dAp, dAm = at(1 - c, c), at(3 * (1 - c), 3 * c)
+    dBp, dBm = at(c, 1 - c), at(3 * c, 3 * (1 - c))
+    sib = dp + 1 - 2 * c
+    barrier = pltpu.get_barrier_semaphore()
+    for d in (dAp, dAm, dBp, dBm, sib):
+        pl.semaphore_signal(barrier, inc=1, device_id={"dp": d}, device_id_type=MESH)
+    pl.semaphore_wait(barrier, 5)
+    def go(r, dev, ssem, rsem):
+        return pltpu.make_async_remote_copy(src_ref=r, dst_ref=r, send_sem=ssem, recv_sem=rsem,
+                                            device_id={"dp": dev}, device_id_type=MESH)
+    def one(k, j):
+        return g_ref.at[k, (x + j * (1 - c)) % 4, (z + j * c) % 4, c]
+    def p1(k, j, recv):
+        d = (0, 0)[j] if j < 2 else None
+        if j == 0:
+            return go(one(k, 3 if recv else 0), dAp, s1s.at[k, 0], s1r.at[k, 0])
+        return go(one(k, 1 if recv else 0), dAm, s1s.at[k, 1], s1r.at[k, 1])
+    def p1f(k, par, recv):
+        if par == 0:
+            return go(one(k, 2 if recv else 3), dAp, s1s.at[k, 2], s1r.at[k, 2])
+        return go(one(k, 2 if recv else 1), dAm, s1s.at[k, 2], s1r.at[k, 2])
+    def byc(fn):
+        @pl.when(c == 0)
+        def _(): fn(0)
+        @pl.when(c == 1)
+        def _(): fn(1)
+    def row(k, j, col):
+        if col == 0: return g_ref.at[k, :, (z + j) % 4, 0]
+        return g_ref.at[k, (x + j) % 4, :, 1]
+    def p2(k, j, recv, col):
+        if j == 0: return go(row(k, 3 if recv else 0, col), dBp, s2s.at[k, 0], s2r.at[k, 0])
+        return go(row(k, 1 if recv else 0, col), dBm, s2s.at[k, 1], s2r.at[k, 1])
+    def p2f(k, par, recv, col):
+        if par == 0: return go(row(k, 2 if recv else 3, col), dBp, s2s.at[k, 2], s2r.at[k, 2])
+        return go(row(k, 2 if recv else 1, col), dBm, s2s.at[k, 2], s2r.at[k, 2])
+    def sb(k, j, col):
+        return go(row(k, j, col), sib, s3s.at[k, j], s3r.at[k, j])
+    own = pltpu.make_async_copy(w_ref, g_ref.at[:, x, z, c], lsem)
+    own.start()
+    own.wait()
+    def parity(k, fn):
+        @pl.when(k % 2 == 0)
+        def _(): fn(0)
+        @pl.when(k % 2 == 1)
+        def _(): fn(1)
+    def step(t, carry):
+        @pl.when(t < K)
+        def _():
+            k = t
+            p1(k, 0, False).start(); p1(k, 1, False).start()
+        @pl.when(jnp.logical_and(t >= L, t - L < K))
+        def _():
+            k = t - L
+            def f(par):
+                p1(k, par, True).wait_recv()
+                p1f(k, par, False).start()
+                p1(k, 1 - par, True).wait_recv()
+            parity(k, f)
+        @pl.when(jnp.logical_and(t >= 2 * L, t - 2 * L < K))
+        def _():
+            k = t - 2 * L
+            parity(k, lambda par: p1f(k, par, True).wait_recv())
+            def f(col):
+                p2(k, 0, False, col).start(); p2(k, 1, False, col).start()
+                if SIB: sb(k, 0, col).start()
+            byc(f)
+        @pl.when(jnp.logical_and(t >= 3 * L, t - 3 * L < K))
+        def _():
+            k = t - 3 * L
+            def g(col):
+                def f(par):
+                    p2(k, par, True, col).wait_recv()
+                    p2f(k, par, False, col).start()
+                    p2(k, 1 - par, True, col).wait_recv()
+                parity(k, f)
+                if SIB: sb(k, 1, col).start(); sb(k, 3, col).start()
+            byc(g)
+        @pl.when(t >= 4 * L)
+        def _():
+            k = t - 4 * L
+            def g(col):
+                parity(k, lambda par: p2f(k, par, True, col).wait_recv())
+                if SIB: sb(k, 2, col).start()
+            byc(g)
+        return carry
+    lax.fori_loop(0, K + 4 * L, step, 0)
+    def finish(k, carry):
+        p1(k, 0, False).wait_send(); p1(k, 1, False).wait_send()
+        parity(k, lambda par: p1f(k, par, False).wait_send())
+        def g(col):
+            p2(k, 0, False, col).wait_send(); p2(k, 1, False, col).wait_send()
+            parity(k, lambda par: p2f(k, par, False, col).wait_send())
+            if SIB:
+                for j in range(4):
+                    sb(k, j, col).wait_send()
+                    go(row(k, j, 1 - col), sib, s3s.at[k, j], s3r.at[k, j]).wait_recv()
+        byc(g)
+        return carry
+    lax.fori_loop(0, K, finish, 0)
+
+def gather(w, vmem=True, L=1, SIB=True, cid=1):
+    K, _, CW = w.shape
+    def kern(w_ref, o_ref, *rest):
+        if vmem:
+            g_ref, osem, *sems = rest
+            ag_body(w_ref, g_ref, *sems, K, L, SIB)
+            cp = pltpu.make_async_copy(g_ref, o_ref, osem); cp.start(); cp.wait()
+        else:
+            ag_body(w_ref, o_ref, *rest, K, L, SIB)
+    D = pltpu.SemaphoreType.DMA
+    sems = [D(()), D((K, 3)), D((K, 3)), D((K, 3)), D((K, 3)), D((K, 4)), D((K, 4))]
+    shape = (K, 4, 4, 2, ROWS, CW)
+    if vmem:
+        sems = [pltpu.VMEM(shape, w.dtype), D(())] + sems
+    return pl.pallas_call(kern, out_shape=jax.ShapeDtypeStruct(shape, w.dtype),
+        in_specs=[pl.BlockSpec(memory_space=pl.ANY)], out_specs=pl.BlockSpec(memory_space=pl.ANY),
+        scratch_shapes=sems,
+        compiler_params=pltpu.CompilerParams(collective_id=cid, has_side_effects=True, vmem_limit_bytes=60*2**20))(w)
 
 
 def from_behind(block, axis, distance):
@@ -382,37 +512,35 @@
     group_id = lax.axis_index("dp")
     group_count = lax.axis_size("dp")
     slot_ids = jnp.arange(group_count, dtype=jnp.int32)
-    target = lax.dynamic_index_in_dim(order, group_id, 1, keepdims=False)
-    send_mask = (slot_ids[:, None] == target[None, :]).astype(jnp.bfloat16)
-    send_inputs = send_mask[:, :, None, None] * inputs[None]
-    send_cotangent = send_mask[:, :, None, None] * out_grad[None]
-    got_inputs, got_cotangent = (
-        lax.all_to_all(send_inputs, "dp", split_axis=0, concat_axis=0, tiled=True),
-        lax.all_to_all(send_cotangent, "dp", split_axis=0, concat_axis=0, tiled=True),
-    )
-    dealt_inputs = jnp.sum(got_inputs.astype(jnp.float32), axis=0).astype(jnp.bfloat16)
-    dealt_cotangent = jnp.sum(got_cotangent.astype(jnp.float32), axis=0).astype(jnp.bfloat16)
     source_of = jnp.sum(jnp.where(order == group_id, slot_ids[None, :], 0), axis=1, dtype=jnp.int32)
     micro = inputs.shape[0]
-    dealt_lengths = lengths[jnp.arange(micro, dtype=jnp.int32), source_of]
-    gathered = (
-        lax.all_gather(gelu_weight, "dp", axis=1, tiled=True),
-        lax.all_gather(lru_weight, "dp", axis=1, tiled=True),
-        lax.all_gather(rate_weight, "dp", axis=2, tiled=True),
-        lax.all_gather(input_weight, "dp", axis=2, tiled=True),
-        lax.all_gather(rate_bias, "dp", axis=2, tiled=True),
-        lax.all_gather(input_bias, "dp", axis=2, tiled=True),
-        lax.all_gather(decay_param, "dp", axis=2, tiled=True),
-        lax.all_gather(filter_taps, "dp", axis=3, tiled=True),
-        lax.all_gather(filter_bias, "dp", axis=2, tiled=True),
-        lax.all_gather(out_weight, "dp", axis=2, tiled=True),
-        lax.all_gather(gate_weight, "dp", axis=1, tiled=True),
-        lax.all_gather(up_weight, "dp", axis=1, tiled=True),
-        lax.all_gather(down_weight, "dp", axis=2, tiled=True),
-        lax.all_gather(norm_first, "dp", axis=1, tiled=True),
-        lax.all_gather(norm_second, "dp", axis=1, tiled=True),
-    )
-    weights = tuple((member[0] for member in gathered))
+    dealt_inputs, dealt_cotangent = inputs, out_grad
+    dealt_lengths = lax.dynamic_index_in_dim(lengths, group_id, 1, keepdims=False)
+    vectors = jnp.concatenate([rate_bias[0].reshape(-1), input_bias[0].reshape(-1), decay_param[0].reshape(-1),
+        filter_taps[0].reshape(-1), filter_bias[0].reshape(-1)]).reshape(1, 256)
+    gains = jnp.concatenate([norm_first[0], norm_second[0], jnp.zeros((160,), jnp.bfloat16)]).reshape(1, 256)
+    gates = jnp.concatenate([rate_weight[0].reshape(32, 128), input_weight[0].reshape(32, 128)], axis=1)
+    small = jnp.concatenate([gates, vectors, gains, jnp.zeros((14, 256), jnp.bfloat16)], axis=0)
+    shard = jnp.concatenate([small, gelu_weight[0], lru_weight[0], out_weight[0].T, gate_weight[0], up_weight[0], down_weight[0].T], axis=1)
+    pieces = shard.reshape(48, 8, 1280).transpose(1, 0, 2)
+    whole = gather(pieces).reshape(8, 1536, 1280).transpose(1, 0, 2).reshape(1536, 10240)
+    small = whole[:, :256].reshape(32, 48, 256)
+    def unblock(part):
+        return part.reshape(32, 8, 4, 128).transpose(1, 0, 2, 3).reshape(8, 128, 128)
+    vec = small[:, 32].reshape(32, 8, 8, 4).transpose(1, 2, 0, 3).reshape(8, 8, 128)
+    weights = (
+        whole[:, 256:1280],
+        whole[:, 1280:2304],
+        unblock(small[:, :32, :128]),
+        unblock(small[:, :32, 128:]),
+        vec[0], vec[1], vec[2], vec[3:7], vec[7],
+        whole[:, 2304:3328].T,
+        whole[:, 3328:5632],
+        whole[:, 5632:7936],
+        whole[:, 7936:10240].T,
+        small[:, 33, 0:48].reshape(1536),
+        small[:, 33, 48:96].reshape(1536),
+    )
     section_id = lax.axis_index("section")
     on_first = section_id == 0
     group_rows = inputs.shape[1] * lax.axis_size("tensor")
@@ -433,30 +561,17 @@
         kept_all.append((kept_values, tuple(lag_masks)))
         if moment < micro:
             received = from_behind(low_result, "section", 1)
-    hidden_out = jnp.stack(
+    own_out = jnp.stack(
         [
             jnp.where(on_first, forward_outs[number], forward_outs[number + 1])
             for number in range(micro)
         ]
-    )[None]
-    fetched = (
-        lax.all_gather(gelu_weight, "dp", axis=1, tiled=True),
-        lax.all_gather(lru_weight, "dp", axis=1, tiled=True),
-        lax.all_gather(rate_weight, "dp", axis=2, tiled=True),
-        lax.all_gather(input_weight, "dp", axis=2, tiled=True),
-        lax.all_gather(rate_bias, "dp", axis=2, tiled=True),
-        lax.all_gather(input_bias, "dp", axis=2, tiled=True),
-        lax.all_gather(decay_param, "dp", axis=2, tiled=True),
-        lax.all_gather(filter_taps, "dp", axis=3, tiled=True),
-        lax.all_gather(filter_bias, "dp", axis=2, tiled=True),
-        lax.all_gather(out_weight, "dp", axis=2, tiled=True),
-        lax.all_gather(gate_weight, "dp", axis=1, tiled=True),
-        lax.all_gather(up_weight, "dp", axis=1, tiled=True),
-        lax.all_gather(down_weight, "dp", axis=2, tiled=True),
-        lax.all_gather(norm_first, "dp", axis=1, tiled=True),
-        lax.all_gather(norm_second, "dp", axis=1, tiled=True),
-    )
-    back_weights = tuple((member[0] for member in fetched))
+    ).astype(jnp.bfloat16)
+    every_out = lax.all_gather(own_out, "dp", axis=0, tiled=False)
+    hidden_out = jnp.stack(
+        [lax.dynamic_index_in_dim(every_out[:, m], source_of[m], 0, keepdims=False) for m in range(micro)]
+    ).astype(jnp.float32)[None]
+    back_weights = weights
 
     def select(first_value, second_value):
         return jnp.where(on_first, first_value, second_value)
@@ -488,26 +603,23 @@
             for number in range(micro)
         ]
     )
-    return_mask = (slot_ids[:, None] == source_of[None, :]).astype(jnp.float32)
-    send_back = return_mask[:, :, None, None] * dealt_back[None]
-    got_back = lax.all_to_all(send_back, "dp", split_axis=0, concat_axis=0, tiled=True)
-    input_grad = jnp.sum(got_back, axis=0)[None]
+    input_grad = dealt_back[None]
     reduced = (
-        lax.psum_scatter(mixer_totals[0], "dp", scatter_dimension=0, tiled=True),
-        lax.psum_scatter(mixer_totals[1], "dp", scatter_dimension=0, tiled=True),
-        lax.psum_scatter(mixer_totals[2], "dp", scatter_dimension=1, tiled=True),
-        lax.psum_scatter(mixer_totals[3], "dp", scatter_dimension=1, tiled=True),
-        lax.psum_scatter(mixer_totals[4], "dp", scatter_dimension=1, tiled=True),
-        lax.psum_scatter(mixer_totals[5], "dp", scatter_dimension=1, tiled=True),
-        lax.psum_scatter(mixer_totals[6], "dp", scatter_dimension=1, tiled=True),
-        lax.psum_scatter(mixer_totals[7], "dp", scatter_dimension=2, tiled=True),
-        lax.psum_scatter(mixer_totals[8], "dp", scatter_dimension=1, tiled=True),
-        lax.psum_scatter(mixer_totals[9], "dp", scatter_dimension=1, tiled=True),
-        lax.psum_scatter(feed_totals[0], "dp", scatter_dimension=0, tiled=True),
-        lax.psum_scatter(feed_totals[1], "dp", scatter_dimension=0, tiled=True),
-        lax.psum_scatter(feed_totals[2], "dp", scatter_dimension=1, tiled=True),
-        lax.psum_scatter(mixer_totals[10], "dp", scatter_dimension=0, tiled=True),
-        lax.psum_scatter(feed_totals[3], "dp", scatter_dimension=0, tiled=True),
+        lax.psum_scatter(mixer_totals[0].astype(jnp.bfloat16), "dp", scatter_dimension=0, tiled=True).astype(jnp.float32),
+        lax.psum_scatter(mixer_totals[1].astype(jnp.bfloat16), "dp", scatter_dimension=0, tiled=True).astype(jnp.float32),
+        lax.psum_scatter(mixer_totals[2].astype(jnp.bfloat16), "dp", scatter_dimension=1, tiled=True).astype(jnp.float32),
+        lax.psum_scatter(mixer_totals[3].astype(jnp.bfloat16), "dp", scatter_dimension=1, tiled=True).astype(jnp.float32),
+        lax.psum_scatter(mixer_totals[4].astype(jnp.bfloat16), "dp", scatter_dimension=1, tiled=True).astype(jnp.float32),
+        lax.psum_scatter(mixer_totals[5].astype(jnp.bfloat16), "dp", scatter_dimension=1, tiled=True).astype(jnp.float32),
+        lax.psum_scatter(mixer_totals[6].astype(jnp.bfloat16), "dp", scatter_dimension=1, tiled=True).astype(jnp.float32),
+        lax.psum_scatter(mixer_totals[7].astype(jnp.bfloat16), "dp", scatter_dimension=2, tiled=True).astype(jnp.float32),
+        lax.psum_scatter(mixer_totals[8].astype(jnp.bfloat16), "dp", scatter_dimension=1, tiled=True).astype(jnp.float32),
+        lax.psum_scatter(mixer_totals[9].astype(jnp.bfloat16), "dp", scatter_dimension=1, tiled=True).astype(jnp.float32),
+        lax.psum_scatter(feed_totals[0].astype(jnp.bfloat16), "dp", scatter_dimension=0, tiled=True).astype(jnp.float32),
+        lax.psum_scatter(feed_totals[1].astype(jnp.bfloat16), "dp", scatter_dimension=0, tiled=True).astype(jnp.float32),
+        lax.psum_scatter(feed_totals[2].astype(jnp.bfloat16), "dp", scatter_dimension=1, tiled=True).astype(jnp.float32),
+        lax.psum_scatter(mixer_totals[10].astype(jnp.bfloat16), "dp", scatter_dimension=0, tiled=True).astype(jnp.float32),
+        lax.psum_scatter(feed_totals[3].astype(jnp.bfloat16), "dp", scatter_dimension=0, tiled=True).astype(jnp.float32),
     )
     gain_totals = lax.psum((reduced[13], reduced[14]), "tensor")
     return (

time: 2820 us -> 2060 us (0.73)
  blocking collectives: 728 us -> 245 us
  waiting for transfers between devices: 1100 us -> 649 us
  Pallas kernels: 0 us -> 105 us
  local copies, waits for them, and re-layouts: 447 us -> 524 us
  matrix products: 215 us -> 256 us
  other arithmetic: 250 us -> 218 us
    unnamed x2 -> x1, blocking collectives: 440 us -> 130 us
    reduce_scatter x8, waiting for transfers between devices: 677 us -> 422 us  [the longest x1 89.8 us: shards(): lax.psum_scatter(feed_totals[2].astype(jnp.bfloat16), 'dp', scatter_dimen...]
    all_gather x6 -> x1, waiting for transfers between devices: 268 us -> 66.7 us  [shards(): every_out = lax.all_gather(own_out, 'dp', axis=0, tiled=False)]
    all_gather x7 -> x0, blocking collectives: 169 us -> none  [the longest x1 31.3 us: shards(): lax.all_gather(filter_bias, 'dp', axis=2, tiled=True)]
    pallas_call x0 -> x1, Pallas kernels: none -> 105 us  [gather(): pl.pallas_call(kern, out_shape=jax.ShapeDtypeStruct(shape, w.dtype), in_s...]
    slice x117, local copies, waits for them, and re-layouts: 94.7 us -> 146 us  [forward_block(): lax.associative_scan(chain_combine, (carry_decay, scale_in * input_gate *...]
    reshape x0 -> x4, local copies, waits for them, and re-layouts: none -> 41.6 us  [the longest x1 40.6 us: shards(): gather(pieces).reshape(8, 1536, 1280).transpose(1, 0, 2)]
    dot_general x18, matrix products: 49.3 us -> 84.1 us  [contract_cols(): lax.dot_general(left, right, (((1,), (1,)), ((), ())), preferred_element_...]
  transfers between devices with their start and end apart: 33 -> 25, of which waited for: 20 -> 18; matrix products, arithmetic and copies ran while one was open for 14% -> 15% of each run, Pallas kernels for 0% -> 0%
where the time goes in v1:
time: 2060 us; the launch traced here: 2030 us
  waiting for transfers between devices  649 us (32%)
  local copies, waits for them, and re-layouts  524 us (25%)
  matrix products  256 us (12%)
  blocking collectives  245 us (12%)
  other arithmetic  218 us (11%)
  Pallas kernels  105 us (5%)
  between operations  24.1 us (1%)
    slice x135, local copies, waits for them, and re-layouts, backward_mixer(): lax.associative_scan(chain_combine, (next_decay, grad_state), reverse=True)  208 us
    slice x117, local copies, waits for them, and re-layouts, forward_block(): lax.associative_scan(chain_combine, (carry_decay, scale_in * input_gate *...  146 us
    unnamed x1, blocking collectives  130 us
    pallas_call x1, Pallas kernels, gather(): pl.pallas_call(kern, out_shape=jax.ShapeDtypeStruct(shape, w.dtype), in_s...  105 us
    reduce_scatter x1, waiting for transfers between devices, shards(): lax.psum_scatter(feed_totals[2].astype(jnp.bfloat16), 'dp', scatter_dimen...  89.8 us
    reduce_scatter x1, waiting for transfers between devices, shards(): lax.psum_scatter(feed_totals[1].astype(jnp.bfloat16), 'dp', scatter_dimen...  89.8 us
    reduce_scatter x1, waiting for transfers between devices, shards(): lax.psum_scatter(feed_totals[0].astype(jnp.bfloat16), 'dp', scatter_dimen...  89.6 us
    dot_general x18, matrix products, contract_cols(): lax.dot_general(left, right, (((1,), (1,)), ((), ())), preferred_element_...  84.1 us
  transfers between devices with their start and end apart: 25, of which 18 were waited for; matrix products, arithmetic and copies ran while one was open for 15% of the time, Pallas kernels for 0%

profile of v1, /device:TPU:0, one launch (start us, length us, event | category | flops | bytes accessed | tf_op | source)
XLA Modules:
  0.0 2031.2 jit_solution(10353724960268800289)
XLA Ops:
  19.9 104.8 %shard_map.314 = bf16[8,4,4,2,48,1280]{5,4,3,2,1,0:T(8,128)(2,1)} custom-call(bf16[8,48,1280]{2,1,0:T(8,128)(2,1)} %bitcast.657), custom_call_target="tpu_custom_call" | custom-call | tf_op jit(solution)/shard_map/pallas_call | solution.py:134
  124.8 40.6 %copy.341 = bf16[8,1536,1280]{1,2,0:T(8,128)(2,1)} copy(bf16[8,1536,1280]{2,1,0:T(8,128)(2,1)} %bitcast.589) | data formatting | bytes 62914560 | tf_op jit(solution)/shard_map/reshape | solution.py:526
  170.0 9.9 all_gather.40
  256.9 23.0 %reduce-scatter.25.cloned.1.call-done = f32[72,1536]{1,0:T(8,128)} async-done(((f32[144,1536]{1,0:T(8,128)}), f32[72,1536]{1,0:T(8,128)}) %reduce-scatter.25.cloned.1.call-update) | async-done | bytes 442384 | tf_op jit(solution)/shard_map/reduce_scatter | solution.py:206
  282.3 9.6 all_gather.41
  310.6 22.1 %reduce-scatter.27.cloned.1.call-done = f32[72,1536]{1,0:T(8,128)} async-done(((f32[144,1536]{1,0:T(8,128)}), f32[72,1536]{1,0:T(8,128)}) %reduce-scatter.27.cloned.1.call-update) | async-done | bytes 442384 | tf_op jit(solution)/shard_map/reduce_scatter | solution.py:206
  341.7 8.5 all_gather.42
  464.7 15.8 reduce-scatter.29.cloned.1.call-done
  484.0 9.6 all_gather.43
  528.8 12.3 reduce-scatter.31.cloned.1.call-done
  546.3 19.6 reduce-scatter.37.cloned.1.call-done
  570.1 9.8 all_gather.44
  709.4 8.6 all_gather.48
  812.4 8.3 rev.6
  872.3 8.7 all_gather.49
  1028.2 8.3 rev.7
  1052.0 22.0 %reduce-scatter.43.cloned.1.call-done = f32[72,1536]{1,0:T(8,128)} async-done(((f32[144,1536]{1,0:T(8,128)}), f32[72,1536]{1,0:T(8,128)}) %reduce-scatter.43.cloned.1.call-update) | async-done | bytes 442384 | tf_op jit(solution)/shard_map/reduce_scatter | solution.py:214
  1088.8 8.9 all_gather.51
  1153.6 10.2 all_gather.52
  1222.6 8.4 rev.8
  1287.1 10.0 fusion.2
  1307.7 10.1 fusion.1
  1328.0 10.1 fusion
  1349.7 49.7 %reduce-scatter.53.cloned.1.call-done = bf16[8,4,128]{2,0,1:T(8,128)(2,1)} async-done(((bf16[8,128,128]{2,0,1:T(8,128)(2,1)}), bf16[8,4,128]{2,0,1:T(8,128)(2,1)}) %reduce-scatter.53.cloned.1.call-update) | async-done | bytes 8208 | tf_op jit(solution)/shard_map/reduce_scatter | solution.py:610
  1400.7 23.3 %reduce-scatter.47.cloned.1.call-done = f32[72,1536]{1,0:T(8,128)} async-done(((f32[144,1536]{1,0:T(8,128)}), f32[72,1536]{1,0:T(8,128)}) %reduce-scatter.47.cloned.1.call-update) | async-done | bytes 442384 | tf_op jit(solution)/shard_map/reduce_scatter | solution.py:214
  1425.3 130.2 %all-reduce.131 = (bf16[8,128]{1,0:T(8,128)(2,1)S(1)}, bf16[8,128]{1,0:T(8,128)(2,1)S(1)}, bf16[8,128]{1,0:T(8,128)(2,1)S(1)}, bf16[4,8,128]{1,0,2:T(4,128)(2,1)...) all-reduce(bf16[8,128]{1,0:T(8,128)(2,1)S(1)} %fusion.387, ...), channel_id=18, replica_groups=mesh['section'=2,'dp'=32,'tensor'=2] {'dp'}, use_global_device_ids=true, to_apply=%region_38.39.clone | all-reduce | flops 11264 | bytes 45056
  1570.0 21.2 %reduce-scatter.51.cloned.1.call-done = bf16[48,1024]{1,0:T(8,128)(2,1)} async-done(((bf16[1536,1024]{1,0:T(8,128)(2,1)}), bf16[48,1024]{1,0:T(8,128)(2,1)}) %reduce-scatter.51.cloned.1.call-update) | async-done | bytes 98320 | tf_op jit(solution)/shard_map/reduce_scatter | solution.py:609
  1592.7 81.8 %reduce-scatter.49.cloned.1.call-done = bf16[48,1024]{1,0:T(8,128)(2,1)} async-done(((bf16[1536,1024]{1,0:T(8,128)(2,1)}), bf16[48,1024]{1,0:T(8,128)(2,1)}) %reduce-scatter.49.cloned.1.call-update) | async-done | bytes 98320 | tf_op jit(solution)/shard_map/reduce_scatter | solution.py:608
  1676.1 89.8 %reduce-scatter.63.cloned.1.call-done = bf16[2304,48]{0,1:T(8,128)(2,1)} async-done(((bf16[2304,1536]{0,1:T(8,128)(2,1)}), bf16[2304,48]{0,1:T(8,128)(2,1)}) %reduce-scatter.63.cloned.1.call-update) | async-done | bytes 221200 | tf_op jit(solution)/shard_map/reduce_scatter | solution.py:620
  1767.7 89.8 %reduce-scatter.61.cloned.1.call-done = bf16[48,2304]{1,0:T(8,128)(2,1)} async-done(((bf16[1536,2304]{1,0:T(8,128)(2,1)}), bf16[48,2304]{1,0:T(8,128)(2,1)}) %reduce-scatter.61.cloned.1.call-update) | async-done | bytes 221200 | tf_op jit(solution)/shard_map/reduce_scatter | solution.py:619
  1859.2 89.6 %reduce-scatter.59.cloned.1.call-done = bf16[48,2304]{1,0:T(8,128)(2,1)} async-done(((bf16[1536,2304]{1,0:T(8,128)(2,1)}), bf16[48,2304]{1,0:T(8,128)(2,1)}) %reduce-scatter.59.cloned.1.call-update) | async-done | bytes 221200 | tf_op jit(solution)/shard_map/reduce_scatter | solution.py:618
  1950.6 66.7 %all-gather.2.cloned.1.call-done = bf16[32,2,72,1536]{3,2,1,0:T(8,128)(2,1)} async-done(((bf16[1,2,72,1536]{3,2,1,0:T(8,128)(2,1)}), bf16[32,2,72,1536]{3,2,1,0:T(8,128)(2,1)}) %all-gather.2.cloned.1.call-update) | async-done | bytes 14155792 | tf_op jit(solution)/shard_map/all_gather | solution.py:570
  (1340 shorter events, 965.9 us)
Async XLA Ops:
  7.2 272.8 %reduce-scatter.25.cloned.1.call-start = ((), (), s32[]{:S(2)}) async-start(), calls=%async_computation.20 | async-start | bytes 1327104 | tf_op jit(solution)/shard_map/reduce_scatter | solution.py:206
  256.8 75.8 %reduce-scatter.27.cloned.1.call-start = ((), (), s32[]{:S(2)}) async-start(), calls=%async_computation.21 | async-start | bytes 1327104 | tf_op jit(solution)/shard_map/reduce_scatter | solution.py:206
  310.5 170.0 %reduce-scatter.29.cloned.1.call-start = ((), (), s32[]{:S(2)}) async-start(), calls=%async_computation.22 | async-start | bytes 1327104 | tf_op jit(solution)/shard_map/reduce_scatter | solution.py:206
  333.7 7.2 collective-permute-start
  350.1 97.8 %copy-start.8 = (bf16[144,1536]{1,0:T(8,128)(2,1)}, bf16[144,1536]{1,0:T(8,128)(2,1)S(1)}, u32[]{:S(2)}) copy-start(bf16[144,1536]{1,0:T(8,128)(2,1)S(1)} %all_gather.42) | copy-start | bytes 1327108
  456.5 84.6 %reduce-scatter.31.cloned.1.call-start = ((), (), s32[]{:S(2)}) async-start(), calls=%async_computation.23 | async-start | bytes 1327104 | tf_op jit(solution)/shard_map/reduce_scatter | solution.py:206
  519.0 46.9 %reduce-scatter.37.cloned.1.call-start = ((), (), s32[]{:S(2)}) async-start(), calls=%async_computation.27 | async-start | bytes 1327104 | tf_op jit(solution)/shard_map/reduce_scatter | solution.py:214
  528.8 175.7 %reduce-scatter.33.cloned.1.call-start = ((), (), s32[]{:S(2)}) async-start(), calls=%async_computation.24 | async-start | bytes 1327104 | tf_op jit(solution)/shard_map/reduce_scatter | solution.py:206
  543.1 22.8 %collective-permute-start.1 = (bf16[72,1536]{1,0:T(8,128)(2,1)S(1)}, bf16[72,1536]{1,0:T(8,128)(2,1)}, u32[]{:S(2)}, u32[]{:S(2)}) collective-permute-start(bf16[72,1536]{1,0:T(8,128)(2,1)S(1)} %get-tuple-element.193), channel_id=1, source_target_pairs={{0,64},{1,65},{2,66},{3,67},{4,68},{5,69},{6,70},{7,71},{8,72},{9,... | collective-permute-start | bytes 663560 | tf_op jit(solution)/shard_map/ppermute | solution.py:143
  677.8 180.6 %reduce-scatter.39.cloned.1.call-start = ((), (), s32[]{:S(2)}) async-start(), calls=%async_computation.28 | async-start | bytes 1327104 | tf_op jit(solution)/shard_map/reduce_scatter | solution.py:214
  836.2 85.2 %reduce-scatter.41.cloned.1.call-start = ((), (), s32[]{:S(2)}) async-start(), calls=%async_computation.29 | async-start | bytes 1327104 | tf_op jit(solution)/shard_map/reduce_scatter | solution.py:214
  862.3 9.3 collective-permute-start.2
  896.9 177.1 %reduce-scatter.43.cloned.1.call-start = ((), (), s32[]{:S(2)}) async-start(), calls=%async_computation.30 | async-start | bytes 1327104 | tf_op jit(solution)/shard_map/reduce_scatter | solution.py:214
  1052.0 98.0 %reduce-scatter.45.cloned.1.call-start = ((), (), s32[]{:S(2)}) async-start(), calls=%async_computation.31 | async-start | bytes 1327104 | tf_op jit(solution)/shard_map/reduce_scatter | solution.py:214
  1078.9 9.1 collective-permute-start.3
  1114.8 223.8 %reduce-scatter.35.cloned.1.call-start = ((), (), s32[]{:S(2)}) async-start(), calls=%async_computation.25 | async-start | bytes 1327104 | tf_op jit(solution)/shard_map/reduce_scatter | solution.py:206
  1149.9 198.5 %reduce-scatter.55.cloned.1.call-start = ((), (), s32[]{:S(2)}) async-start(), calls=%async_computation.36 | async-start | bytes 270336 | tf_op jit(solution)/shard_map/reduce_scatter | solution.py:611
  1243.8 155.6 %reduce-scatter.53.cloned.1.call-start = ((), (), s32[]{:S(2)}) async-start(), calls=%async_computation.35 | async-start | bytes 270336 | tf_op jit(solution)/shard_map/reduce_scatter | solution.py:610
  1253.6 170.4 %reduce-scatter.47.cloned.1.call-start = ((), (), s32[]{:S(2)}) async-start(), calls=%async_computation.32 | async-start | bytes 1327104 | tf_op jit(solution)/shard_map/reduce_scatter | solution.py:214
  1259.1 309.3 %reduce-scatter.57.cloned.1.call-start = ((), (), s32[]{:S(2)}) async-start(), calls=%async_computation.37 | async-start | bytes 3244032 | tf_op jit(solution)/shard_map/reduce_scatter | solution.py:617
  1264.5 326.7 %reduce-scatter.51.cloned.1.call-start = ((), (), s32[]{:S(2)}) async-start(), calls=%async_computation.34 | async-start | bytes 3244032 | tf_op jit(solution)/shard_map/reduce_scatter | solution.py:609
  1270.6 403.9 %reduce-scatter.49.cloned.1.call-start = ((), (), s32[]{:S(2)}) async-start(), calls=%async_computation.33 | async-start | bytes 3244032 | tf_op jit(solution)/shard_map/reduce_scatter | solution.py:608
  1276.5 489.5 %reduce-scatter.63.cloned.1.call-start = ((), (), s32[]{:S(2)}) async-start(), calls=%async_computation.40 | async-start | bytes 7299072 | tf_op jit(solution)/shard_map/reduce_scatter | solution.py:620
  1297.2 560.3 %reduce-scatter.61.cloned.1.call-start = ((), (), s32[]{:S(2)}) async-start(), calls=%async_computation.39 | async-start | bytes 7299072 | tf_op jit(solution)/shard_map/reduce_scatter | solution.py:619
  1317.8 631.1 %reduce-scatter.59.cloned.1.call-start = ((), (), s32[]{:S(2)}) async-start(), calls=%async_computation.38 | async-start | bytes 7299072 | tf_op jit(solution)/shard_map/reduce_scatter | solution.py:618
  1338.5 85.6 %copy-start.112 = (f32[1536]{0:T(1024)S(1)}, f32[1536]{0:T(1024)}, u32[]{:S(2)}) copy-start(f32[1536]{0:T(1024)} %copy-done.110) | copy-start | bytes 18436
  1338.5 86.8 %copy-start.174 = (f32[1536]{0:T(1024)S(1)}, f32[1536]{0:T(1024)}, u32[]{:S(2)}) copy-start(f32[1536]{0:T(1024)} %get-tuple-element.70) | copy-start | bytes 18436
  1338.5 86.8 %copy-start.176 = (f32[1536]{0:T(1024)S(1)}, f32[1536]{0:T(1024)}, u32[]{:S(2)}) copy-start(f32[1536]{0:T(1024)} %get-tuple-element.68) | copy-start | bytes 18436
  1338.5 227.7 %copy-start.62 = (f32[72,1536]{1,0:T(8,128)S(1)}, f32[72,1536]{1,0:T(8,128)}, u32[]{:S(2)}) copy-start(f32[72,1536]{1,0:T(8,128)} %copy-done.61) | copy-start | bytes 1327108
  1338.5 227.7 %copy-start.102 = (f32[72,1536]{1,0:T(8,128)S(1)}, f32[72,1536]{1,0:T(8,128)}, u32[]{:S(2)}) copy-start(f32[72,1536]{1,0:T(8,128)} %get-tuple-element.166) | copy-start | bytes 1327108
  1338.5 228.9 %copy-start.93 = (f32[1,72,1536]{2,1,0:T(8,128)S(1)}, f32[1,72,1536]{2,1,0:T(8,128)}, u32[]{:S(2)}) copy-start(f32[1,72,1536]{2,1,0:T(8,128)} %get-tuple-element.148) | copy-start | bytes 1327108
  1338.5 678.7 %all-gather.2.cloned.1.call-start = ((), (), s32[]{:S(2)}) async-start(), calls=%async_computation.26 | async-start | bytes 14598144 | tf_op jit(solution)/shard_map/all_gather | solution.py:570
  (268 other events, 2187.0 us)
Sparse Core Ops, SparseCore 0:
  256.9 22.9 reduce-scatter.24
  310.6 21.9 reduce-scatter.26
  456.6 23.8 reduce-scatter.28
  519.1 21.9 reduce-scatter.30
  543.9 21.9 reduce-scatter.36
  677.9 22.0 reduce-scatter.32
  836.3 22.0 reduce-scatter.38
  897.0 21.8 reduce-scatter.40
  1052.1 21.8 reduce-scatter.42
  1115.0 21.3 reduce-scatter.44
  1150.0 22.3 reduce-scatter.34
  1243.9 75.7 reduce-scatter.54
  1323.1 76.2 reduce-scatter.52
  1402.2 21.7 reduce-scatter.46
  1427.5 79.9 reduce-scatter.56
  1511.4 79.7 reduce-scatter.50
  1594.6 79.8 reduce-scatter.48
  1678.6 87.2 reduce-scatter.62
  1770.2 87.2 reduce-scatter.60
  1861.6 87.1 reduce-scatter.58
  1951.3 65.8 all-gather.1

commit v2 on v0

v2 whole, which is shorter than its diff:
```python
import jax
import jax.numpy as jnp
from jax import lax
from jax.experimental import pallas as pl
from jax.experimental.pallas import tpu as pltpu
from jax.sharding import PartitionSpec as P

MESH = pl.DeviceIdType.MESH
F32 = jnp.float32
BF16 = jnp.bfloat16
EPS = 1e-06
FLOOR = 0.01
PIECES = 20
PW = 512
TILE = 256
HALF = 144
ALL = 288
D = 1536
QUARTER = 384
VMEM_LIMIT = 62 * 2**20


def nn(a, b):
    return lax.dot_general(a, b, (((1,), (0,)), ((), ())), preferred_element_type=F32)


def nt(a, b):
    return lax.dot_general(a, b, (((1,), (1,)), ((), ())), preferred_element_type=F32)


def tn(a, b):
    return lax.dot_general(a, b, (((0,), (0,)), ((), ())), preferred_element_type=F32)


def gelu_parts(v):
    k = 0.7978845608028654
    th = jnp.tanh(k * (v + 0.044715 * v * v * v))
    half = 0.5 * (1.0 + th)
    slope = half + 0.5 * v * (1.0 - th * th) * (k * (1.0 + 0.134145 * v * v))
    return v * half, slope


def gelu(v):
    k = 0.7978845608028654
    return 0.5 * v * (1.0 + jnp.tanh(k * (v + 0.044715 * v * v * v)))


def sigmoid(v):
    return 1.0 / (1.0 + jnp.exp(-v))


def softplus(v):
    return jnp.maximum(v, 0.0) + jnp.log(1.0 + jnp.exp(-jnp.abs(v)))


def to_natural(v):
    return jnp.concatenate([v[0:72], v[144:216], v[72:144], v[216:288]], axis=0)


def to_exchange(v):
    return jnp.concatenate([v[0:72], v[144:216], v[72:144], v[216:288]], axis=0)


def down(v, k):
    return pltpu.roll(v, k, 0) if k else v


def up(v, k):
    return pltpu.roll(v, ALL - k, 0) if k else v


def scan_down(a, b):
    for s in (1, 2, 4, 8, 16, 32, 64):
        b = a * down(b, s) + b
        if s < 64:
            a = a * down(a, s)
    return b


def scan_up(a, b):
    for s in (1, 2, 4, 8, 16, 32, 64):
        b = a * up(b, s) + b
        if s < 64:
            a = a * up(a, s)
    return b


def iota(shape, dim):
    return lax.broadcasted_iota(jnp.int32, shape, dim)


def onehot(cond):
    return jnp.where(cond, 1.0, 0.0).astype(BF16)


class Ring:
    def __init__(self):
        dp = lax.axis_index("dp")
        c, z, x = dp % 2, (dp // 2) % 4, dp // 8
        self.dp, self.c, self.z, self.x = dp, c, z, x

        def at(dx, dz):
            return ((x + dx) % 4) * 8 + ((z + dz) % 4) * 2 + c

        self.ap, self.am = at(1 - c, c), at(3 * (1 - c), 3 * c)
        self.bp, self.bm = at(c, 1 - c), at(3 * c, 3 * (1 - c))
        self.sib = dp + 1 - 2 * c

    def by_colour(self, fn):
        @pl.when(self.c == 0)
        def _():
            fn(0)

        @pl.when(self.c == 1)
        def _():
            fn(1)


def by_parity(k, fn):
    @pl.when(k % 2 == 0)
    def _():
        fn(0)

    @pl.when(k % 2 == 1)
    def _():
        fn(1)


def go(src, dst, dev, ssem, rsem):
    return pltpu.make_async_remote_copy(
        src_ref=src, dst_ref=dst, send_sem=ssem, recv_sem=rsem, device_id=dev, device_id_type=MESH
    )


def gather_weights(ring, g_ref, sems):
    s1s, s1r, s2s, s2r, s3s, s3r = sems
    c, x, z = ring.c, ring.x, ring.z
    K = PIECES

    def send(r, dev, ssem, rsem):
        return go(r, r, {"dp": dev}, ssem, rsem)

    def one(k, j):
        return g_ref.at[k, (x + j * (1 - c)) % 4, (z + j * c) % 4, c]

    def p1(k, j, recv):
        if j == 0:
            return send(one(k, 3 if recv else 0), ring.ap, s1s.at[k, 0], s1r.at[k, 0])
        return send(one(k, 1 if recv else 0), ring.am, s1s.at[k, 1], s1r.at[k, 1])

    def p1f(k, par, recv):
        if par == 0:
            return send(one(k, 2 if recv else 3), ring.ap, s1s.at[k, 2], s1r.at[k, 2])
        return send(one(k, 2 if recv else 1), ring.am, s1s.at[k, 2], s1r.at[k, 2])

    def row(k, j, col):
        if col == 0:
            return g_ref.at[k, :, (z + j) % 4, 0]
        return g_ref.at[k, (x + j) % 4, :, 1]

    def p2(k, j, recv, col):
        if j == 0:
            return send(row(k, 3 if recv else 0, col), ring.bp, s2s.at[k, 0], s2r.at[k, 0])
        return send(row(k, 1 if recv else 0, col), ring.bm, s2s.at[k, 1], s2r.at[k, 1])

    def p2f(k, par, recv, col):
        if par == 0:
            return send(row(k, 2 if recv else 3, col), ring.bp, s2s.at[k, 2], s2r.at[k, 2])
        return send(row(k, 2 if recv else 1, col), ring.bm, s2s.at[k, 2], s2r.at[k, 2])

    def sb(k, j, col):
        return send(row(k, j, col), ring.sib, s3s.at[k, j], s3r.at[k, j])

    def step(t, carry):
        @pl.when(t < K)
        def _():
            p1(t, 0, False).start()
            p1(t, 1, False).start()

        @pl.when(jnp.logical_and(t >= 1, t - 1 < K))
        def _():
            k = t - 1

            def f(par):
                p1(k, par, True).wait_recv()
                p1f(k, par, False).start()
                p1(k, 1 - par, True).wait_recv()

            by_parity(k, f)

        @pl.when(jnp.logical_and(t >= 2, t - 2 < K))
        def _():
            k = t - 2
            by_parity(k, lambda par: p1f(k, par, True).wait_recv())

            def f(col):
                p2(k, 0, False, col).start()
                p2(k, 1, False, col).start()
                sb(k, 0, col).start()

            ring.by_colour(f)

        @pl.when(jnp.logical_and(t >= 3, t - 3 < K))
        def _():
            k = t - 3

            def f(col):
                def h(par):
                    p2(k, par, True, col).wait_recv()
                    p2f(k, par, False, col).start()
                    p2(k, 1 - par, True, col).wait_recv()

                by_parity(k, h)
                sb(k, 1, col).start()
                sb(k, 3, col).start()

            ring.by_colour(f)

        @pl.when(t >= 4)
        def _():
            k = t - 4

            def f(col):
                by_parity(k, lambda par: p2f(k, par, True, col).wait_recv())
                sb(k, 2, col).start()

            ring.by_colour(f)

        return carry

    lax.fori_loop(0, K + 4, step, 0)

    def finish(k, carry):
        p1(k, 0, False).wait_send()
        p1(k, 1, False).wait_send()
        by_parity(k, lambda par: p1f(k, par, False).wait_send())

        def f(col):
            p2(k, 0, False, col).wait_send()
            p2(k, 1, False, col).wait_send()
            by_parity(k, lambda par: p2f(k, par, False, col).wait_send())
            for j in range(4):
                sb(k, j, col).wait_send()
                send(row(k, j, 1 - col), ring.sib, s3s.at[k, j], s3r.at[k, j]).wait_recv()

        ring.by_colour(f)
        return carry

    lax.fori_loop(0, K, finish, 0)


def chain_kernel(
    shard_ref, xin_ref, ein_ref, mask_ref,
    res_out, grad_out, left_out, right_out, small_out,
    g_ref, xb, left, right, pf, cv, rg, ig, st, mid, own, sb, rb, gmid, rw, vec, vgrad, gains, gsum, gpart, sgrad, acc,
    lsem, psem_s, psem_r, *gsems,
):
    sec = lax.axis_index("section")
    t = lax.axis_index("tensor")
    ring = Ring()
    barrier = pltpu.get_barrier_semaphore()
    others = [{"dp": d} for d in (ring.ap, ring.am, ring.bp, ring.bm, ring.sib)] + [{"tensor": 1 - t}, {"section": 1 - sec}]
    for dev in others:
        pl.semaphore_signal(barrier, inc=1, device_id=dev, device_id_type=MESH)
    load = pltpu.make_async_copy(shard_ref, g_ref.at[:, ring.x, ring.z, ring.c], lsem.at[0])
    load.start()
    pl.semaphore_wait(barrier, 7)
    load.wait()

    my = pl.ds(pl.multiple_of(t * HALF, 16), HALF)
    his = pl.ds(pl.multiple_of((1 - t) * HALF, 16), HALF)

    def pair(src, dst, i):
        return go(src, dst, {"tensor": 1 - t}, psem_s.at[i], psem_r.at[i])

    def share(li, i):
        return pair(left.at[li, my], left.at[li, my], i)

    def shared(li, i):
        return pair(left.at[li, his], left.at[li, his], i)

    def hand(src, dst, i):
        return go(src, dst, {"section": 1 - sec}, psem_s.at[i], psem_r.at[i])

    def back_piece(x):
        return hand(sb.at[x], left.at[3, my, pl.ds(x * QUARTER, QUARTER)], 22 + x)

    @pl.when(sec == 1)
    def _():
        left[3, my, :] = ein_ref[...]
        share(3, 10).start()

    gather_weights(ring, g_ref, gsems)

    def wt(T):
        k, off = T // 2, pl.multiple_of((T % 2) * TILE, TILE)
        return g_ref[k, :, :, :, :, pl.ds(off, TILE)].reshape(D, TILE)

    def wq(T, x):
        k, off = T // 2, pl.multiple_of((T % 2) * TILE, TILE)
        return g_ref[k, x, :, :, :, pl.ds(off, TILE)].reshape(QUARTER, TILE)

    small = wt(0)

    def unpack(j, carry):
        ci, r = iota((128, D), 0), iota((128, D), 1)
        sel = onehot(r == (ci // 4) * 48 + j * 4 + ci % 4)
        rw[j] = nn(sel, small).astype(BF16)
        return carry

    lax.fori_loop(0, 8, unpack, 0)
    dpi, r = iota((32, D), 0), iota((32, D), 1)
    t32 = nn(onehot(r == dpi * 48 + 32), small).astype(BF16)
    d1 = onehot(iota((32, 128), 1) // 4 == iota((32, 128), 0))
    e1 = tn(t32, d1)
    e1 = jnp.where(iota((256, 128), 0) % 4 == iota((256, 128), 1) % 4, e1, 0.0).astype(BF16)
    v1 = nn(onehot(iota((64, 256), 1) // 4 == iota((64, 256), 0)), e1)
    for i in range(64):
        vec[i] = v1[i:i + 1, :]
    t33 = nn(onehot(r == dpi * 48 + 33), small).astype(BF16)
    d2 = onehot(jnp.logical_and(r >= dpi * 48, r < dpi * 48 + 48))
    e2 = tn(t33[:, 0:128], d2)
    within = iota((128, D), 1) % 48
    q = iota((128, D), 0)
    gains[0] = jnp.sum(jnp.where(q == within, e2, 0.0), axis=0, keepdims=True)
    gains[1] = jnp.sum(jnp.where(q == within + 48, e2, 0.0), axis=0, keepdims=True)

    @pl.when(sec == 0)
    def _():
        xb[...] = xin_ref[...]

    @pl.when(sec == 1)
    def _():
        hand(xb, xb, 21).wait_recv()

    def rows16(i):
        return pl.ds(pl.multiple_of(i * 16, 16), 16)

    def myrows16(i):
        return pl.ds(pl.multiple_of(t * HALF + i * 16, 16), 16)

    def scale_of(v):
        return lax.rsqrt(jnp.mean(v * v, axis=1, keepdims=True) + EPS)

    def norm_one(i, carry):
        v = xb[rows16(i), :].astype(F32)
        left[0, myrows16(i), :] = (v * scale_of(v) * gains[0]).astype(BF16)
        return carry

    lax.fori_loop(0, 9, norm_one, 0)
    share(0, 0).start()

    def into_branches(rows):
        def body(i, carry):
            pf[i, rows, :] = nn(left[0, rows, :], wt(1 + i))
            return carry
        lax.fori_loop(0, 8, body, 0)

    into_branches(my)
    shared(0, 0).wait_recv()
    into_branches(his)

    def vrow(a, j):
        return vec[a * 8 + j]

    def mixer(i, carry):
        for h in range(2):
            j = i * 2 + h
            lanes = slice(h * 128, h * 128 + 128)
            feature = to_natural(pf[4 + i, :, lanes])
            filtered = vrow(7, j)
            for k in range(4):
                filtered = filtered + vrow(3 + k, j) * down(feature, k) * mask_ref[k]
            low = filtered.astype(BF16)
            cv[j] = low
            conv = low.astype(F32)
            pre = nn(low, rw[j])
            rate = sigmoid(pre[:, 0:128] + vrow(0, j))
            inp = sigmoid(pre[:, 128:256] + vrow(1, j))
            rg[j] = rate
            ig[j] = inp
            decay = jnp.exp(-8.0 * rate * softplus(-vrow(2, j)))
            scale_in = jnp.sqrt(jnp.maximum(1.0 - decay * decay, FLOOR))
            state = scan_down(decay * mask_ref[1], scale_in * inp * conv)
            st[j] = state
            right[8 + i, :, lanes] = (to_exchange(state) * gelu(pf[i, :, lanes])).astype(BF16)
        return carry

    lax.fori_loop(0, 4, mixer, 0)

    def reduce_out(terms, base, turn):
        def body(x, carry):
            total = None
            for ri, T in terms:
                part = nt(right[ri], wq(T, x))
                total = part if total is None else total + part
            acc[...] = total
            sb[x] = acc[his, :].astype(BF16)
            pair(sb.at[x], rb.at[turn, x], base + x).start()
            own[x] = acc[my, :]
            return carry

        lax.fori_loop(0, 4, body, 0)
        for x in range(4):
            pair(sb.at[x], rb.at[turn, x], base + x).wait()

    def summed(i, turn):
        rows = rows16(i)
        return jnp.concatenate([own[x, rows, :] + rb[turn, x, rows, :].astype(F32) for x in range(4)], axis=1)

    reduce_out([(8 + i, 9 + i) for i in range(4)], 1, 0)

    def norm_two(i, carry):
        v = xb[rows16(i), :].astype(F32) + summed(i, 0)
        mid[rows16(i), :] = v
        left[2, myrows16(i), :] = (v * scale_of(v) * gains[1]).astype(BF16)
        return carry

    lax.fori_loop(0, 9, norm_two, 0)
    share(2, 5).start()

    def feed(rows):
        def body(i, carry):
            lhs = left[2, rows, :]
            pg = nn(lhs, wt(13 + i))
            pu = nn(lhs, wt(22 + i))
            right[12 + i, rows, :] = pg.astype(BF16)
            right[21 + i, rows, :] = pu.astype(BF16)
            right[30 + i, rows, :] = (gelu(pg) * pu).astype(BF16)
            return carry
        lax.fori_loop(0, 9, body, 0)

    feed(my)
    shared(2, 5).wait_recv()
    feed(his)
    reduce_out([(30 + i, 31 + i) for i in range(9)], 6, 1)

    def finish_forward(i, carry):
        v = mid[rows16(i), :] + summed(i, 1)
        res_out[rows16(i), :] = v.astype(BF16)
        return carry

    lax.fori_loop(0, 9, finish_forward, 0)

    @pl.when(sec == 0)
    def _():
        hand(res_out, xb, 21).start()
        for x in range(4):
            back_piece(x).wait_recv()
        share(3, 10).start()

    shared(3, 10).wait_recv()

    def feed_back(i, carry):
        gh = nn(left[3], wt(31 + i))
        pg = right[12 + i].astype(F32)
        pu = right[21 + i].astype(F32)
        act, slope = gelu_parts(pg)
        right[12 + i] = (gh * pu * slope).astype(BF16)
        right[21 + i] = (gh * act).astype(BF16)
        return carry

    lax.fori_loop(0, 9, feed_back, 0)
    reduce_out([(12 + i, 13 + i) for i in range(18)], 11, 0)

    def eight(v):
        return v[0:8] + v[8:16]

    def middle_back(i, carry):
        ng = summed(i, 0)
        m = mid[rows16(i), :]
        sc = scale_of(m)
        u = ng * gains[1]
        gm = left[3, myrows16(i), :].astype(F32) + sc * u - m * (sc * sc * sc) * jnp.mean(u * m, axis=1, keepdims=True)
        gmid[rows16(i), :] = gm
        left[1, myrows16(i), :] = gm.astype(BF16)
        return carry + eight(ng * m * sc)

    gpart[1] = lax.fori_loop(0, 9, middle_back, jnp.zeros((8, D), F32))
    share(1, 15).start()
    shared(1, 15).wait_recv()

    def mixer_back(i, carry):
        gmix = nn(left[1], wt(9 + i))
        for h in range(2):
            j = i * 2 + h
            lanes = slice(h * 128, h * 128 + 128)
            gm = gmix[:, lanes]
            act, slope = gelu_parts(pf[i, :, lanes])
            state = st[j]
            right[i, :, lanes] = (gm * to_exchange(state) * slope).astype(BF16)
            grad_state = to_natural(gm * act)
            rate, inp = rg[j], ig[j]
            conv = cv[j].astype(F32)
            forget = softplus(-vrow(2, j))
            decay = jnp.exp(-8.0 * rate * forget)
            spare = 1.0 - decay * decay
            scale_in = jnp.sqrt(jnp.maximum(spare, FLOOR))
            m1 = mask_ref[1]
            drive = scan_up(up(decay * m1, 1), grad_state)
            grad_spare = jnp.where(spare > FLOOR, 0.5 * (drive * inp * conv) / scale_in, 0.0)
            grad_decay = drive * down(state, 1) * m1 - 2.0 * decay * grad_spare
            grad_log = grad_decay * decay
            rate_low = (grad_log * (-8.0 * forget) * rate * (1.0 - rate)).astype(BF16)
            driven = drive * scale_in
            input_low = (driven * conv * inp * (1.0 - inp)).astype(BF16)
            both = jnp.concatenate([rate_low, input_low], axis=1)
            back = nt(both, rw[j])
            vgrad[0 * 8 + j] = jnp.sum(rate_low.astype(F32), axis=0, keepdims=True)
            vgrad[1 * 8 + j] = jnp.sum(input_low.astype(F32), axis=0, keepdims=True)
            grad_forget = jnp.sum(grad_log * (-8.0 * rate), axis=0, keepdims=True)
            vgrad[2 * 8 + j] = -grad_forget * sigmoid(-vrow(2, j))
            sgrad[j] = tn(cv[j], both).astype(BF16)
            grad_conv = driven * inp + back
            feature = to_natural(pf[4 + i, :, lanes])
            grad_feature = None
            for k in range(4):
                masked = grad_conv * mask_ref[k] if k else grad_conv
                vgrad[(3 + k) * 8 + j] = jnp.sum(masked * down(feature, k), axis=0, keepdims=True)
                term = up(masked, k) * vrow(3 + k, j)
                grad_feature = term if grad_feature is None else grad_feature + term
            vgrad[7 * 8 + j] = jnp.sum(grad_conv, axis=0, keepdims=True)
            right[4 + i, :, lanes] = to_exchange(grad_feature).astype(BF16)
        return carry

    lax.fori_loop(0, 4, mixer_back, 0)
    reduce_out([(i, 1 + i) for i in range(8)], 16, 1)

    def first_back(i, carry):
        fg = summed(i, 1)
        v = xb[rows16(i), :].astype(F32)
        sc = scale_of(v)
        u = fg * gains[0]
        gv = gmid[rows16(i), :] + sc * u - v * (sc * sc * sc) * jnp.mean(u * v, axis=1, keepdims=True)
        mid[rows16(i), :] = gv
        for x in range(4):
            sb[x, rows16(i), :] = gv[:, x * QUARTER:(x + 1) * QUARTER].astype(BF16)
        return carry + eight(fg * v * sc)

    gpart[0] = lax.fori_loop(0, 9, first_back, jnp.zeros((8, D), F32))

    @pl.when(sec == 1)
    def _():
        for x in range(4):
            back_piece(x).start()

    pair(gpart, gsum, 20).start()
    grad_copy = pltpu.make_async_copy(mid, grad_out, lsem.at[1])
    left_copy = pltpu.make_async_copy(left, left_out, lsem.at[2])
    right_copy = pltpu.make_async_copy(right, right_out, lsem.at[3])
    grad_copy.start()
    left_copy.start()
    right_copy.start()

    v2 = jnp.concatenate([vgrad[i] for i in range(64)], axis=0).astype(BF16)
    e2 = nn(onehot(iota((256, 64), 0) // 4 == iota((256, 64), 1)), v2)
    e2 = jnp.where(iota((256, 128), 0) % 4 == iota((256, 128), 1) % 4, e2, 0.0).astype(BF16)
    t32 = nt(d1, e2).astype(BF16)
    pair(gpart, gsum, 20).wait()
    n1 = jnp.sum(gpart[0] + gsum[0], axis=0, keepdims=True)
    n2 = jnp.sum(gpart[1] + gsum[1], axis=0, keepdims=True)
    spread = jnp.where(q == within, n1, jnp.where(q == within + 48, n2, 0.0)).astype(BF16)
    t33 = nt(d2, spread).astype(BF16)
    t33 = jnp.concatenate([t33, jnp.zeros((32, 128), BF16)], axis=1)

    def pack(x, carry):
        r = iota((QUARTER, 128), 0) + x * QUARTER
        ci = iota((QUARTER, 128), 1)
        total = None
        for j in range(8):
            sel = onehot(r == (ci // 4) * 48 + j * 4 + ci % 4)
            part = nn(sel, sgrad[j])
            total = part if total is None else total + part
        r = iota((QUARTER, 32), 0) + x * QUARTER
        dpi = iota((QUARTER, 32), 1)
        total = total + nn(onehot(r == dpi * 48 + 32), t32) + nn(onehot(r == dpi * 48 + 33), t33)
        small_out[pl.ds(pl.multiple_of(x * QUARTER, 16), QUARTER), :] = total.astype(BF16)
        return carry

    lax.fori_loop(0, 4, pack, 0)

    for li, i in ((0, 0), (2, 5), (3, 10), (1, 15)):
        share(li, i).wait_send()

    @pl.when(sec == 0)
    def _():
        hand(res_out, xb, 21).wait_send()

    @pl.when(sec == 1)
    def _():
        for x in range(4):
            back_piece(x).wait_send()

    grad_copy.wait()
    left_copy.wait()
    right_copy.wait()


def chain(shard, xin, ein, masks):
    K = PIECES
    dma = pltpu.SemaphoreType.DMA
    vmem = pl.BlockSpec(memory_space=pltpu.VMEM)
    hbm = pl.BlockSpec(memory_space=pl.ANY)
    sds = jax.ShapeDtypeStruct
    return pl.pallas_call(
        chain_kernel,
        name="chain",
        out_shape=(
            sds((HALF, D), BF16), sds((HALF, D), F32), sds((4, ALL, D), BF16),
            sds((39, ALL, TILE), BF16), sds((D, TILE), BF16),
        ),
        in_specs=[hbm, vmem, vmem, vmem],
        out_specs=(vmem, hbm, hbm, hbm, vmem),
        scratch_shapes=[
            pltpu.VMEM((K, 4, 4, 2, 48, PW), BF16),
            pltpu.VMEM((HALF, D), BF16),
            pltpu.VMEM((4, ALL, D), BF16),
            pltpu.VMEM((39, ALL, TILE), BF16),
            pltpu.VMEM((8, ALL, TILE), F32),
            pltpu.VMEM((8, ALL, 128), BF16),
            pltpu.VMEM((8, ALL, 128), F32),
            pltpu.VMEM((8, ALL, 128), F32),
            pltpu.VMEM((8, ALL, 128), F32),
            pltpu.VMEM((HALF, D), F32),
            pltpu.VMEM((4, HALF, QUARTER), F32),
            pltpu.VMEM((4, HALF, QUARTER), BF16),
            pltpu.VMEM((2, 4, HALF, QUARTER), BF16),
            pltpu.VMEM((HALF, D), F32),
            pltpu.VMEM((8, 128, 256), BF16),
            pltpu.VMEM((64, 1, 128), F32),
            pltpu.VMEM((64, 1, 128), F32),
            pltpu.VMEM((2, 1, D), F32),
            pltpu.VMEM((2, 8, D), F32),
            pltpu.VMEM((2, 8, D), F32),
            pltpu.VMEM((8, 128, 256), BF16),
            pltpu.VMEM((ALL, QUARTER), F32),
            dma((4,)), dma((26,)), dma((26,)),
            dma((K, 3)), dma((K, 3)), dma((K, 3)), dma((K, 3)), dma((K, 4)), dma((K, 4)),
        ],
        compiler_params=pltpu.CompilerParams(
            collective_id=1, has_side_effects=True, vmem_limit_bytes=VMEM_LIMIT
        ),
    )(shard, xin, ein, masks)


def document_masks(doc_lengths):
    ends = jnp.cumsum(doc_lengths, axis=-1, dtype=jnp.int32)
    position = jnp.arange(HALF, dtype=jnp.int32)
    ident = jnp.sum((position[None, :, None] >= ends[:, None, :]).astype(jnp.int32), axis=-1, dtype=jnp.int32)
    masks = []
    for offset in range(4):
        before = jnp.pad(ident, ((0, 0), (offset, 0)), constant_values=-1)[:, :HALF]
        masks.append((before == ident).astype(F32).reshape(ALL, 1))
    return jnp.broadcast_to(jnp.stack(masks), (4, ALL, 128))


def pack_shard(gelu_weight, lru_weight, rate_weight, input_weight, rate_bias, input_bias, decay_param,
               filter_taps, filter_bias, out_weight, gate_weight, up_weight, down_weight, norm_first, norm_second):
    vectors = jnp.concatenate([v[0].reshape(-1) for v in (rate_bias, input_bias, decay_param, filter_taps, filter_bias)]).reshape(1, 256)
    gains = jnp.concatenate([norm_first[0], norm_second[0], jnp.zeros((160,), BF16)]).reshape(1, 256)
    gates = jnp.concatenate([rate_weight[0].reshape(32, 128), input_weight[0].reshape(32, 128)], axis=1)
    small = jnp.concatenate([gates, vectors, gains, jnp.zeros((14, 256), BF16)], axis=0)
    shard = jnp.concatenate(
        [small, gelu_weight[0], lru_weight[0], out_weight[0].T, gate_weight[0], up_weight[0], down_weight[0].T], axis=1
    )
    return shard.reshape(48, PIECES, PW).transpose(1, 0, 2)


def reduce_kernel(
    left_ref, right_ref, small_ref, out_ref,
    leftt, pp, r0, hh, tt, h2, uu, sbs, sbr, s1s, s1r, s2s, s2r,
):
    ring = Ring()
    c, x, z = ring.c, ring.x, ring.z
    K = PIECES
    barrier = pltpu.get_barrier_semaphore()
    for dev in (ring.ap, ring.am, ring.bp, ring.bm, ring.sib):
        pl.semaphore_signal(barrier, inc=1, device_id={"dp": dev}, device_id_type=MESH)

    def send(src, dst, dev, ssem, rsem):
        return go(src, dst, {"dp": dev}, ssem, rsem)

    def turn_left(li):
        def body(i, carry):
            cols = pl.ds(pl.multiple_of(i * 128, 128), 128)
            leftt[li, cols, :] = left_ref[li, :, cols].T
            return carry
        lax.fori_loop(0, 12, body, 0)

    def one(k, j):
        return k, (x + j * (1 - c)) % 4, (z + j * c) % 4

    def row(k, j, col):
        if col == 0:
            return k, slice(None), (z + j) % 4
        return k, (x + j) % 4

    def sib(k, col):
        return send(pp.at[k % 2, :, :, 1 - col], r0.at[k], ring.sib, sbs.at[k], sbr.at[k])

    def p1(k, i, j, dev, col):
        dst = hh.at[k] if i == 0 else tt.at[k, i - 1]
        return send(r0.at[row(k, j, col)], dst, dev, s1s.at[k, i], s1r.at[k, i])

    def p2(k, i, j, dev):
        dst = h2.at[k] if i == 0 else uu.at[k, i - 1]
        return send(r0.at[one(k, j)], dst, dev, s2s.at[k, i], s2r.at[k, i])

    def add(a, b):
        return a.astype(F32) + b.astype(F32)

    def step(t, carry):
        for li, when in ((0, 0), (1, 2), (2, 4), (3, 8)):
            @pl.when(t == when)
            def _(li=li):
                turn_left(li)

        @pl.when(t == 0)
        def _():
            pl.semaphore_wait(barrier, 5)

        @pl.when(t < K)
        def _():
            k = t

            @pl.when(k >= 2)
            def _():
                ring.by_colour(lambda col: sib(k - 2, col).wait_send())

            for h in range(2):
                T = 2 * k + h
                lanes = slice(h * TILE, h * TILE + TILE)
                li = (T >= 9).astype(jnp.int32) + (T >= 13).astype(jnp.int32) + (T >= 31).astype(jnp.int32)
                ri = jnp.maximum(T - 1, 0)

                def body(xx, carry):
                    rows = pl.ds(pl.multiple_of(xx * QUARTER, 16), QUARTER)
                    part = nn(leftt[li, rows, :], right_ref[ri]).astype(BF16)
                    pp[k % 2, xx, :, :, :, lanes] = part.reshape(4, 2, 48, TILE)
                    return carry

                lax.fori_loop(0, 4, body, 0)

            @pl.when(k == 0)
            def _():
                def body(xx, carry):
                    rows = pl.ds(pl.multiple_of(xx * QUARTER, 16), QUARTER)
                    pp[0, xx, :, :, :, 0:TILE] = small_ref[rows, :].reshape(4, 2, 48, TILE)
                    return carry
                lax.fori_loop(0, 4, body, 0)

            ring.by_colour(lambda col: sib(k, col).start())

        @pl.when(jnp.logical_and(t >= 1, t - 1 < K))
        def _():
            k = t - 1

            def f(col):
                sib(k, col).wait_recv()

                def body(xx, carry):
                    r0[k, xx] = add(r0[k, xx], pp[k % 2, xx, :, col]).astype(BF16)
                    return carry

                lax.fori_loop(0, 4, body, 0)

                def h(par):
                    if par == 0:
                        p1(k, 0, 2, ring.bp, col).start()
                        p1(k, 2, 3, ring.bm, col).start()
                    else:
                        p1(k, 0, 2, ring.bm, col).start()
                        p1(k, 1, 1, ring.bp, col).start()

                by_parity(k, h)

            ring.by_colour(f)

        @pl.when(jnp.logical_and(t >= 2, t - 2 < K))
        def _():
            k = t - 2

            def f(col):
                def h(par):
                    j = 1 if par == 0 else 3
                    p1(k, 0, 2, ring.bp, col).wait_recv()
                    r0[row(k, j, col)] = add(r0[row(k, j, col)], hh[k]).astype(BF16)
                    if par == 0:
                        p1(k, 1, 1, ring.bp, col).start()
                    else:
                        p1(k, 2, 3, ring.bm, col).start()

                by_parity(k, h)

            ring.by_colour(f)

        @pl.when(jnp.logical_and(t >= 3, t - 3 < K))
        def _():
            k = t - 3

            def f(col):
                p1(k, 1, 1, ring.bp, col).wait_recv()
                p1(k, 2, 3, ring.bm, col).wait_recv()
                mine = row(k, 0, col)
                r0[mine] = (add(r0[mine], tt[k, 0]) + tt[k, 1].astype(F32)).astype(BF16)

            ring.by_colour(f)

            def h(par):
                if par == 0:
                    p2(k, 0, 2, ring.ap).start()
                    p2(k, 2, 3, ring.am).start()
                else:
                    p2(k, 0, 2, ring.am).start()
                    p2(k, 1, 1, ring.ap).start()

            by_parity(k, h)

        @pl.when(jnp.logical_and(t >= 4, t - 4 < K))
        def _():
            k = t - 4

            def h(par):
                j = 1 if par == 0 else 3
                p2(k, 0, 2, ring.ap).wait_recv()
                r0[one(k, j)] = add(r0[one(k, j)], h2[k]).astype(BF16)
                if par == 0:
                    p2(k, 1, 1, ring.ap).start()
                else:
                    p2(k, 2, 3, ring.am).start()

            by_parity(k, h)

        @pl.when(t >= 5)
        def _():
            k = t - 5
            p2(k, 1, 1, ring.ap).wait_recv()
            p2(k, 2, 3, ring.am).wait_recv()
            out_ref[:, pl.ds(pl.multiple_of(k * PW, PW), PW)] = add(r0[one(k, 0)], uu[k, 0]) + uu[k, 1].astype(F32)

        return carry

    lax.fori_loop(0, K + 5, step, 0)

    def finish(k, carry):
        def f(col):
            @pl.when(k >= K - 2)
            def _():
                sib(k, col).wait_send()
            for i in range(3):
                p1(k, i, 1, ring.bp, col).wait_send()

        ring.by_colour(f)
        for i in range(3):
            p2(k, i, 1, ring.ap).wait_send()
        return carry

    lax.fori_loop(0, K, finish, 0)


def reduce_weights(left, right, small):
    K = PIECES
    dma = pltpu.SemaphoreType.DMA
    vmem = pl.BlockSpec(memory_space=pltpu.VMEM)
    return pl.pallas_call(
        reduce_kernel,
        name="reduce",
        out_shape=jax.ShapeDtypeStruct((48, PIECES * PW), F32),
        in_specs=[vmem, vmem, vmem],
        out_specs=vmem,
        scratch_shapes=[
            pltpu.VMEM((4, D, ALL), BF16),
            pltpu.VMEM((2, 4, 4, 2, 48, PW), BF16),
            pltpu.VMEM((K, 4, 4, 48, PW), BF16),
            pltpu.VMEM((K, 4, 48, PW), BF16),
            pltpu.VMEM((K, 2, 4, 48, PW), BF16),
            pltpu.VMEM((K, 48, PW), BF16),
            pltpu.VMEM((K, 2, 48, PW), BF16),
            dma((K,)), dma((K,)), dma((K, 3)), dma((K, 3)), dma((K, 3)), dma((K, 3)),
        ],
        compiler_params=pltpu.CompilerParams(
            collective_id=2, has_side_effects=True, vmem_limit_bytes=VMEM_LIMIT
        ),
    )(left, right, small)


def shards(
    inputs, out_grad, lengths, order, *weights
):
    group = lax.axis_index("dp")
    masks = document_masks(lax.dynamic_index_in_dim(lengths, group, 1, keepdims=False))
    res, grad, left, right, small = chain(
        pack_shard(*weights), inputs.reshape(HALF, D), out_grad.reshape(HALF, D), masks
    )
    slots = jnp.arange(32, dtype=jnp.int32)
    source = jnp.sum(jnp.where(order == group, slots[None, :], 0), axis=1, dtype=jnp.int32)
    every = lax.all_gather(res, "dp", axis=0, tiled=False).reshape(32, 2, 72, D)
    hidden = jnp.stack(
        [lax.dynamic_index_in_dim(every[:, m], source[m], 0, keepdims=False) for m in range(2)]
    ).astype(F32)[None]
    input_grad = grad.reshape(1, 2, 72, D)
    total = reduce_weights(left, right, small)
    vec = total[32, 0:256].reshape(8, 8, 4)
    col = lambda a, n: total[:, a:a + n]
    return (
        hidden, input_grad,
        col(256, 1024)[None], col(1280, 1024)[None],
        total[0:32, 0:128].reshape(1, 8, 4, 128), total[0:32, 128:256].reshape(1, 8, 4, 128),
        vec[0][None], vec[1][None], vec[2][None], vec[3:7][None], vec[7][None],
        col(2304, 1024).T[None], col(3328, 2304)[None], col(5632, 2304)[None], col(7936, 2304).T[None],
        total[33, 0:48][None], total[33, 48:96][None],
    )


def solution(mesh):
    rows = P(None, ("dp", "tensor"), None)
    tall = P("section", "dp", "tensor")
    wide = P("section", "tensor", "dp")
    block = P("section", "tensor", "dp", None)
    taps = P("section", None, "tensor", "dp")
    gain = P("section", "dp")
    params = (tall, tall, block, block, wide, wide, wide, taps, wide, wide, tall, tall, wide, gain, gain)
    out_rows = P("section", None, ("dp", "tensor"), None)
    return jax.shard_map(
        shards,
        mesh=mesh,
        in_specs=(rows, rows, P(), P()) + params,
        out_specs=(out_rows, out_rows) + params,
        check_vma=False,
    )
```

time: 2820 us -> 558 us (0.20); the launches traced: 2790 us -> 557 us
  waiting for transfers between devices: 1100 us -> 0.02 us
  blocking collectives: 728 us -> 0 us
  Pallas kernels: 0 us -> 502 us
  local copies, waits for them, and re-layouts: 447 us -> 33.2 us
  other arithmetic: 250 us -> 3.06 us
  matrix products: 215 us -> 0 us
  starting transfers between devices: 31.6 us -> 0.04 us
    reduce_scatter x20 -> x0, waiting for transfers between devices: 806 us -> none  [the longest x1 267 us: shards(): lax.psum_scatter(mixer_totals[2], 'dp', scatter_dimension=1, tiled=True)]
    pallas_call x0 -> x2, Pallas kernels: none -> 502 us  [the longest x1 350 us: chain(): pl.pallas_call(chain_kernel, name='chain', out_shape=(sds((HALF, D), BF16...]
    unnamed x2 -> x0, blocking collectives: 440 us -> none
    slice x261 -> x10, local copies, waits for them, and re-layouts: 305 us -> 11.2 us  [the longest x1 5.91 us: shards(): every[:, m]]
    all_gather x19 -> x0, blocking collectives: 281 us -> none  [the longest x6 56.7 us: spread_grads(): return lax.all_gather(grads_low, 'tensor', axis=0, tiled=True)]
    all_gather x6 -> x1, waiting for transfers between devices: 268 us -> 0.01 us  [shards(): every = lax.all_gather(res, 'dp', axis=0, tiled=False).reshape(32, 2, 72, D)]
    dot_general x72 -> x0, matrix products: 215 us -> none  [the longest x18 87.5 us: contract_rows(): lax.dot_general(left, right, (((0,), (0,)), ((), ())), preferred_element_...]
    pad x72 -> x0, local copies, waits for them, and re-layouts: 77.3 us -> none  [the longest x36 46.3 us: backward_mixer(): lax.associative_scan(chain_combine, (next_decay, grad_state), reverse=True)]
  transfers between devices with their start and end apart: 33 -> 1, of which waited for: 20 -> 0; matrix products, arithmetic and copies ran while one was open for 14% -> 2% of each run, Pallas kernels for 0% -> 27%
where the time goes in v2:
time: 558 us; the launch traced here: 557 us
  Pallas kernels  502 us (90%)
  local copies, waits for them, and re-layouts  33.2 us (6%)
  between operations  18 us (3%)
    pallas_call x1, Pallas kernels, chain(): pl.pallas_call(chain_kernel, name='chain', out_shape=(sds((HALF, D), BF16...  350 us
    pallas_call x1, Pallas kernels, reduce_weights(): pl.pallas_call(reduce_kernel, name='reduce', out_shape=jax.ShapeDtypeStru...  152 us
    unnamed x22, local copies, waits for them, and re-layouts  13.4 us
  transfers between devices with their start and end apart: 1, of which 0 were waited for; matrix products, arithmetic and copies ran while one was open for 2% of the time, Pallas kernels for 27%

profile of v2, /device:TPU:0, one launch (start us, length us, event | category | flops | bytes accessed | tf_op | source)
XLA Modules:
  0.0 556.7 jit_solution(3631067010342087953)
XLA Ops:
  7.3 0.6 copy-done
  8.7 0.8 copy.60
  9.6 0.8 copy.57
  10.5 0.8 copy.58
  11.3 0.8 copy.59
  12.2 0.8 copy.61
  13.2 0.8 pad_maximum_fusion.1
  14.0 0.8 fusion.3
  14.8 0.9 bitcast_dynamic-update-slice_fusion.5
  15.7 0.9 bitcast_dynamic-update-slice_fusion.4
  16.6 0.9 bitcast_dynamic-update-slice_fusion.3
  17.5 0.9 bitcast_dynamic-update-slice_fusion.2
  18.5 1.0 bitcast_dynamic-update-slice_fusion.1
  19.4 1.0 bitcast_dynamic-update-slice_fusion
  20.4 1.1 copy.73
  21.5 1.0 broadcast_in_dim.53.mask_ref
  22.5 350.3 %chain.1 = (bf16[144,1536]{1,0:T(8,128)(2,1)}, f32[144,1536]{1,0:T(8,128)}, bf16[4,288,1536]{2,1,0:T(8,128)(2,1)}, bf16[39,288,256]{2,1,0:T(8,128)(2,1)}, bf16[1536,256]{1,0:T(8,128)(2,1)}) custom-call(bf16[20,48,512]{2,1,0:T(8,128)(2,1)} %bitcast.60, bf16[144,1536]{1,0:T(8,128)(2,1)} %bitcast.63, bf16[144,1536]{1,0:T(8,128)(2,1)} %bitcast.64, ...), custom_call_target="tpu_custom_call" | custom-call | tf_op jit(solution)/shard_map/chain/pallas_call | solution.py:605
  376.2 152.1 %reduce.23 = f32[48,10240]{1,0:T(8,128)} custom-call(bf16[4,288,1536]{2,1,0:T(8,128)(2,1)} %get-tuple-element.24.left_ref, bf16[39,288,256]{2,1,0:T(8,128)(2,1)} %get-tuple-element.25.right_ref, bf16[1536,256]{1,0:T(8,128)(2,1)} %get-tuple-element.26.small_ref), custom_call_target="tpu_custom_call" | custom-call | tf_op jit(solution)/shard_map/reduce/pallas_call | solution.py:865
  528.3 0.9 slice_reduce_fusion
  529.2 0.7 copy.66
  530.0 0.7 copy.67
  530.7 0.7 copy.68
  531.4 0.7 copy.70
  532.1 0.8 slice_reduce_fusion.1
  533.0 0.7 copy.69
  535.0 1.3 fusion.6
  536.3 1.3 fusion.7
  537.7 1.9 slice_bitcast_fusion.3
  539.6 2.4 slice_bitcast_fusion
  542.0 5.9 %fusion.5 = (bf16[32,1,72,1536]{3,2,1,0:T(8,128)(2,1)S(1)}, bf16[32,1,72,1536]{3,2,1,0:T(8,128)(2,1)S(1)}) fusion(bf16[32,2,72,1536]{3,2,1,0:T(8,128)(2,1)} %bitcast.59), kind=kLoop, calls=%fused_computation.36 | loop fusion | bytes 28311552 | tf_op jit(solution)/shard_map/slice | solution.py:899
  547.9 1.0 maximum_convert_fusion
  548.9 0.9 copy.81
  (36 shorter events, 2.8 us)
Async XLA Ops:
  7.2 0.7 copy-start
  7.2 365.7 %copy-start.2 = (s32[2,32]{1,0:T(2,128)S(1)}, s32[2,32]{1,0:T(2,128)}, u32[]{:S(2)}) copy-start(s32[2,32]{1,0:T(2,128)} %param.22) | copy-start | bytes 772
  7.2 534.7 %all-gather.3.cloned.1.call-start = ((), (), s32[]{:S(2)}) async-start(), calls=%async_computation | async-start | bytes 14598144 | tf_op jit(solution)/shard_map/all_gather | solution.py:897
  542.0 7.0 %copy-start.1 = (f32[144,1536]{1,0:T(8,128)S(1)}, f32[144,1536]{1,0:T(8,128)}, u32[]{:S(2)}) copy-start(f32[144,1536]{1,0:T(8,128)} %get-tuple-element.23) | copy-start | bytes 2654212
Sparse Core Ops, SparseCore 0:
  373.0 84.9 all-gather.2

commit v3 on v2

v3 whole, which is shorter than its diff:
```python
import jax
import jax.numpy as jnp
from jax import lax
from jax.experimental import pallas as pl
from jax.experimental.pallas import tpu as pltpu
from jax.sharding import PartitionSpec as P

MESH = pl.DeviceIdType.MESH
F32 = jnp.float32
BF16 = jnp.bfloat16
EPS = 1e-06
FLOOR = 0.01
PIECES = 20
PW = 512
TILE = 256
HALF = 144
ALL = 288
D = 1536
QUARTER = 384
VMEM_LIMIT = 63 * 2**20


def nn(a, b):
    return lax.dot_general(a, b, (((1,), (0,)), ((), ())), preferred_element_type=F32)


def nt(a, b):
    return lax.dot_general(a, b, (((1,), (1,)), ((), ())), preferred_element_type=F32)


def tn(a, b):
    return lax.dot_general(a, b, (((0,), (0,)), ((), ())), preferred_element_type=F32)


def gelu_parts(v):
    k = 0.7978845608028654
    th = jnp.tanh(k * (v + 0.044715 * v * v * v))
    half = 0.5 * (1.0 + th)
    slope = half + 0.5 * v * (1.0 - th * th) * (k * (1.0 + 0.134145 * v * v))
    return v * half, slope


def gelu(v):
    k = 0.7978845608028654
    return 0.5 * v * (1.0 + jnp.tanh(k * (v + 0.044715 * v * v * v)))


def sigmoid(v):
    return 1.0 / (1.0 + jnp.exp(-v))


def softplus(v):
    return jnp.maximum(v, 0.0) + jnp.log(1.0 + jnp.exp(-jnp.abs(v)))


def to_natural(v):
    return jnp.concatenate([v[0:72], v[144:216], v[72:144], v[216:288]], axis=0)


def to_exchange(v):
    return jnp.concatenate([v[0:72], v[144:216], v[72:144], v[216:288]], axis=0)


def down(v, k):
    return pltpu.roll(v, k, 0) if k else v


def up(v, k):
    return pltpu.roll(v, ALL - k, 0) if k else v


def scan_down(a, b):
    for s in (1, 2, 4, 8, 16, 32, 64):
        b = a * down(b, s) + b
        if s < 64:
            a = a * down(a, s)
    return b


def scan_up(a, b):
    for s in (1, 2, 4, 8, 16, 32, 64):
        b = a * up(b, s) + b
        if s < 64:
            a = a * up(a, s)
    return b


def iota(shape, dim):
    return lax.broadcasted_iota(jnp.int32, shape, dim)


def onehot(cond):
    return jnp.where(cond, 1.0, 0.0).astype(BF16)


class Ring:
    def __init__(self):
        dp = lax.axis_index("dp")
        c, z, x = dp % 2, (dp // 2) % 4, dp // 8
        self.dp, self.c, self.z, self.x = dp, c, z, x

        def at(dx, dz):
            return ((x + dx) % 4) * 8 + ((z + dz) % 4) * 2 + c

        self.ap, self.am = at(1 - c, c), at(3 * (1 - c), 3 * c)
        self.bp, self.bm = at(c, 1 - c), at(3 * c, 3 * (1 - c))
        self.sib = dp + 1 - 2 * c

    def by_colour(self, fn):
        @pl.when(self.c == 0)
        def _():
            fn(0)

        @pl.when(self.c == 1)
        def _():
            fn(1)


def by_parity(k, fn):
    @pl.when(k % 2 == 0)
    def _():
        fn(0)

    @pl.when(k % 2 == 1)
    def _():
        fn(1)


def go(src, dst, dev, ssem, rsem):
    return pltpu.make_async_remote_copy(
        src_ref=src, dst_ref=dst, send_sem=ssem, recv_sem=rsem, device_id=dev, device_id_type=MESH
    )


def gather_steps(ring, g_ref, sems):
    s1s, s1r, s2s, s2r, s3s, s3r = sems
    c, x, z = ring.c, ring.x, ring.z
    K = PIECES

    def send(r, dev, ssem, rsem):
        return go(r, r, {"dp": dev}, ssem, rsem)

    def one(k, j):
        return g_ref.at[k, (x + j * (1 - c)) % 4, (z + j * c) % 4, c]

    def p1(k, j, recv):
        if j == 0:
            return send(one(k, 3 if recv else 0), ring.ap, s1s.at[k, 0], s1r.at[k, 0])
        return send(one(k, 1 if recv else 0), ring.am, s1s.at[k, 1], s1r.at[k, 1])

    def p1f(k, par, recv):
        if par == 0:
            return send(one(k, 2 if recv else 3), ring.ap, s1s.at[k, 2], s1r.at[k, 2])
        return send(one(k, 2 if recv else 1), ring.am, s1s.at[k, 2], s1r.at[k, 2])

    def row(k, j, col):
        if col == 0:
            return g_ref.at[k, :, (z + j) % 4, 0]
        return g_ref.at[k, (x + j) % 4, :, 1]

    def p2(k, j, recv, col):
        if j == 0:
            return send(row(k, 3 if recv else 0, col), ring.bp, s2s.at[k, 0], s2r.at[k, 0])
        return send(row(k, 1 if recv else 0, col), ring.bm, s2s.at[k, 1], s2r.at[k, 1])

    def p2f(k, par, recv, col):
        if par == 0:
            return send(row(k, 2 if recv else 3, col), ring.bp, s2s.at[k, 2], s2r.at[k, 2])
        return send(row(k, 2 if recv else 1, col), ring.bm, s2s.at[k, 2], s2r.at[k, 2])

    def sb(k, j, col):
        return send(row(k, j, col), ring.sib, s3s.at[k, j], s3r.at[k, j])

    def step(t):
        @pl.when(t < K)
        def _():
            p1(t, 0, False).start()
            p1(t, 1, False).start()

        @pl.when(jnp.logical_and(t >= 1, t - 1 < K))
        def _():
            k = t - 1

            def f(par):
                p1(k, par, True).wait_recv()
                p1f(k, par, False).start()
                p1(k, 1 - par, True).wait_recv()

            by_parity(k, f)

        @pl.when(jnp.logical_and(t >= 2, t - 2 < K))
        def _():
            k = t - 2
            by_parity(k, lambda par: p1f(k, par, True).wait_recv())

            def f(col):
                p2(k, 0, False, col).start()
                p2(k, 1, False, col).start()
                sb(k, 0, col).start()

            ring.by_colour(f)

        @pl.when(jnp.logical_and(t >= 3, t - 3 < K))
        def _():
            k = t - 3

            def f(col):
                def h(par):
                    p2(k, par, True, col).wait_recv()
                    p2f(k, par, False, col).start()
                    p2(k, 1 - par, True, col).wait_recv()

                by_parity(k, h)
                sb(k, 1, col).start()
                sb(k, 3, col).start()

            ring.by_colour(f)

        @pl.when(t >= 4)
        def _():
            k = t - 4

            def f(col):
                by_parity(k, lambda par: p2f(k, par, True, col).wait_recv())
                sb(k, 2, col).start()

            ring.by_colour(f)

    def ready(k):
        def f(col):
            for j in range(4):
                send(row(k, j, 1 - col), ring.sib, s3s.at[k, j], s3r.at[k, j]).wait_recv()

        ring.by_colour(f)

    def finish(k, carry):
        p1(k, 0, False).wait_send()
        p1(k, 1, False).wait_send()
        by_parity(k, lambda par: p1f(k, par, False).wait_send())

        def f(col):
            p2(k, 0, False, col).wait_send()
            p2(k, 1, False, col).wait_send()
            by_parity(k, lambda par: p2f(k, par, False, col).wait_send())
            for j in range(4):
                sb(k, j, col).wait_send()

        ring.by_colour(f)
        return carry

    return step, ready, lambda: lax.fori_loop(0, K, finish, 0)


def deal_steps(ring, res, hid, sems):
    s1s, s1r, s2s, s2r, s3s, s3r, lsem = sems
    c, x, z = ring.c, ring.x, ring.z
    parts = (pl.ds(0, 80), pl.ds(80, 64))

    def send(r, dev, ssem, rsem):
        return go(r, r, {"dp": dev}, ssem, rsem)

    def one(j):
        return hid.at[(x + j * (1 - c)) % 4, (z + j * c) % 4, c]

    def row(j, col):
        if col == 0:
            return hid.at[:, (z + j) % 4, 0]
        return hid.at[(x + j) % 4, :, 1]

    def p1(i, recv):
        if i == 0:
            return send(one(3 if recv else 0), ring.ap, s1s.at[0], s1r.at[0])
        if i == 1:
            return send(one(1 if recv else 0), ring.am, s1s.at[1], s1r.at[1])
        if i == 2:
            return send(one(2 if recv else 3).at[parts[0]], ring.ap, s1s.at[2], s1r.at[2])
        return send(one(2 if recv else 1).at[parts[1]], ring.am, s1s.at[3], s1r.at[3])

    def p2(i, recv, col):
        if i == 0:
            return send(row(3 if recv else 0, col), ring.bp, s2s.at[0], s2r.at[0])
        if i == 1:
            return send(row(1 if recv else 0, col), ring.bm, s2s.at[1], s2r.at[1])
        if i == 2:
            return send(row(2 if recv else 3, col).at[:, parts[0]], ring.bp, s2s.at[2], s2r.at[2])
        return send(row(2 if recv else 1, col).at[:, parts[1]], ring.bm, s2s.at[3], s2r.at[3])

    def sb(j, col):
        return send(row(j, col), ring.sib, s3s.at[j], s3r.at[j])

    def step(t):
        if t == 0:
            local = pltpu.make_async_copy(res, one(0), lsem)
            local.start()
            local.wait()
            p1(0, False).start()
            p1(1, False).start()
        elif t == 1:
            p1(0, True).wait_recv()
            p1(2, False).start()
            p1(1, True).wait_recv()
            p1(3, False).start()
        elif t == 2:
            p1(2, True).wait_recv()
            p1(3, True).wait_recv()

            def f(col):
                p2(0, False, col).start()
                p2(1, False, col).start()
                sb(0, col).start()

            ring.by_colour(f)
        elif t == 3:
            def f(col):
                p2(0, True, col).wait_recv()
                p2(2, False, col).start()
                sb(3, col).start()
                p2(1, True, col).wait_recv()
                p2(3, False, col).start()
                sb(1, col).start()

            ring.by_colour(f)
        elif t == 4:
            def f(col):
                p2(2, True, col).wait_recv()
                p2(3, True, col).wait_recv()
                sb(2, col).start()

            ring.by_colour(f)
        else:
            for i in range(4):
                p1(i, False).wait_send()

            def f(col):
                for i in range(4):
                    p2(i, False, col).wait_send()
                    sb(i, col).wait_send()
                    send(row(i, 1 - col), ring.sib, s3s.at[i], s3r.at[i]).wait_recv()

            ring.by_colour(f)

    return step


def reduce_steps(ring, g_ref, left, right, leftt, pp, out_ref, stage, free, pack, sems):
    sbs, sbr, s1s, s1r, s2s, s2r, osem = sems
    c, x, z = ring.c, ring.x, ring.z
    K = PIECES

    def send(src, dst, dev, ssem, rsem):
        return go(src, dst, {"dp": dev}, ssem, rsem)

    def turn_left(li):
        def body(i, carry):
            cols = pl.ds(pl.multiple_of(i * 128, 128), 128)
            leftt[cols, :] = left[li, :, cols].T
            return carry
        lax.fori_loop(0, 12, body, 0)

    def one(k, j):
        return k, (x + j * (1 - c)) % 4, (z + j * c) % 4, 0

    def row(k, j, col):
        if col == 0:
            return k, slice(None), (z + j) % 4, 0
        return k, (x + j) % 4, slice(None), 0

    def sib(k, col):
        return send(pp.at[k % 2, :, :, 1 - col], g_ref.at[k, :, :, 0], ring.sib, sbs.at[k], sbr.at[k])

    def p1(k, i, j, dev, col):
        return send(g_ref.at[row(k, j, col)], g_ref.at[k, i, :, 1], dev, s1s.at[k, i], s1r.at[k, i])

    def p2(k, i, j, dev):
        return send(g_ref.at[one(k, j)], g_ref.at[k, 3, i, 1], dev, s2s.at[k, i], s2r.at[k, i])

    def add(a, b):
        return a.astype(F32) + b.astype(F32)

    def out_copy(k):
        return pltpu.make_async_copy(stage.at[k % 2], out_ref.at[k], osem.at[k % 2])

    def step(t, low, high):
        for li, when in ((3, 0), (2, 4), (1, 13), (0, 15), (3, 19)):
            if not low <= when <= high:
                continue

            @pl.when(t == when)
            def _(li=li):
                turn_left(li)

        for group, when in ((0, 0), (1, 4), (2, 13), (3, 15)):
            if not low <= when <= high:
                continue

            @pl.when(t == when)
            def _(group=group):
                pl.semaphore_wait(free.at[group], 5)

        @pl.when(t < K)
        def _():
            k = K - 1 - t

            @pl.when(t >= 2)
            def _():
                ring.by_colour(lambda col: sib(k + 2, col).wait_send())

            def body(xx, carry):
                rows = pl.ds(pl.multiple_of(xx * QUARTER, 16), QUARTER)
                part = nn(leftt[rows, :], right[k]).astype(BF16)
                pp[k % 2, xx] = part.reshape(4, 2, 48, PW)
                return carry

            lax.fori_loop(0, 4, body, 0)

            if high >= K - 1:
                pl.when(k == 0)(pack)

            ring.by_colour(lambda col: sib(k, col).start())

        @pl.when(jnp.logical_and(t >= 1, t - 1 < K))
        def _():
            k = K - t

            def f(col):
                sib(k, col).wait_recv()

                def body(xx, carry):
                    g_ref[k, xx, :, 0] = add(g_ref[k, xx, :, 0], pp[k % 2, xx, :, col]).astype(BF16)
                    return carry

                lax.fori_loop(0, 4, body, 0)

                def h(par):
                    if par == 0:
                        p1(k, 0, 2, ring.bp, col).start()
                        p1(k, 2, 3, ring.bm, col).start()
                    else:
                        p1(k, 0, 2, ring.bm, col).start()
                        p1(k, 1, 1, ring.bp, col).start()

                by_parity(k, h)

            ring.by_colour(f)

        @pl.when(jnp.logical_and(t >= 2, t - 2 < K))
        def _():
            k = K + 1 - t

            def f(col):
                def h(par):
                    j = 1 if par == 0 else 3
                    p1(k, 0, 2, ring.bp, col).wait_recv()
                    g_ref[row(k, j, col)] = add(g_ref[row(k, j, col)], g_ref[k, 0, :, 1]).astype(BF16)
                    if par == 0:
                        p1(k, 1, 1, ring.bp, col).start()
                    else:
                        p1(k, 2, 3, ring.bm, col).start()

                by_parity(k, h)

            ring.by_colour(f)

        @pl.when(jnp.logical_and(t >= 3, t - 3 < K))
        def _():
            k = K + 2 - t

            def f(col):
                p1(k, 1, 1, ring.bp, col).wait_recv()
                p1(k, 2, 3, ring.bm, col).wait_recv()
                mine = row(k, 0, col)
                g_ref[mine] = (add(g_ref[mine], g_ref[k, 1, :, 1]) + g_ref[k, 2, :, 1].astype(F32)).astype(BF16)

            ring.by_colour(f)

            def h(par):
                if par == 0:
                    p2(k, 0, 2, ring.ap).start()
                    p2(k, 2, 3, ring.am).start()
                else:
                    p2(k, 0, 2, ring.am).start()
                    p2(k, 1, 1, ring.ap).start()

            by_parity(k, h)

        @pl.when(jnp.logical_and(t >= 4, t - 4 < K))
        def _():
            k = K + 3 - t

            def h(par):
                j = 1 if par == 0 else 3
                p2(k, 0, 2, ring.ap).wait_recv()
                g_ref[one(k, j)] = add(g_ref[one(k, j)], g_ref[k, 3, 0, 1]).astype(BF16)
                if par == 0:
                    p2(k, 1, 1, ring.ap).start()
                else:
                    p2(k, 2, 3, ring.am).start()

            by_parity(k, h)

        @pl.when(t >= 5)
        def _():
            k = K + 4 - t
            p2(k, 1, 1, ring.ap).wait_recv()
            p2(k, 2, 3, ring.am).wait_recv()

            @pl.when(t >= 7)
            def _():
                out_copy(k + 2).wait()

            stage[k % 2] = add(g_ref[one(k, 0)], g_ref[k, 3, 1, 1]) + g_ref[k, 3, 2, 1].astype(F32)
            out_copy(k).start()

    def finish_one(k, carry):
        def f(col):
            @pl.when(k < 2)
            def _():
                sib(k, col).wait_send()
                out_copy(k).wait()

            for i in range(3):
                p1(k, i, 1, ring.bp, col).wait_send()

        ring.by_colour(f)
        for i in range(3):
            p2(k, i, 1, ring.ap).wait_send()
        return carry

    return step, lambda: lax.fori_loop(0, K, finish_one, 0)


def whole_kernel(
    gelu_ref, lru_ref, out_ref, gate_ref, up_ref, down_ref, small_ref, xin_ref, ein_ref, mask_ref,
    hid_out, grad_out, sums_out,
    g_ref, xb, left, right, pf, cv, rg, ig, st, mid, own, sb, rb, gmid, rw, vec, vgrad, gains, gsum, gpart, sgrad, acc,
    leftt, pp, stage, res,
    lsem, psem_s, psem_r, free, *more,
):
    sec = lax.axis_index("section")
    t = lax.axis_index("tensor")
    ring = Ring()
    barrier = pltpu.get_barrier_semaphore()
    others = [{"dp": d} for d in (ring.ap, ring.am, ring.bp, ring.bm, ring.sib)] + [{"tensor": 1 - t}, {"section": 1 - sec}]
    for dev in others:
        pl.semaphore_signal(barrier, inc=1, device_id=dev, device_id_type=MESH)
    loads = []

    def load(src, col, width, piece, lane):
        part = src.at[:, pl.ds(col, width)]
        to = g_ref.at[piece, ring.x, ring.z, ring.c, :, pl.ds(lane, width)]
        loads.append(pltpu.make_async_copy(part, to, lsem.at[len(loads)]))

    load(down_ref, 2048, 256, 0, 0)
    load(small_ref, 0, 256, 0, 256)
    for i in range(2):
        load(gelu_ref, i * 512, 512, 1 + i, 0)
        load(lru_ref, i * 512, 512, 3 + i, 0)
        load(out_ref, i * 512, 512, 5 + i, 0)
    for i in range(9):
        load(gate_ref, i * 256, 256, 7 + i, 0)
        load(up_ref, i * 256, 256, 7 + i, 256)
    for i in range(4):
        load(down_ref, i * 512, 512, 16 + i, 0)
    for copy in loads:
        copy.start()
    my = pl.ds(pl.multiple_of(t * HALF, 16), HALF)
    his = pl.ds(pl.multiple_of((1 - t) * HALF, 16), HALF)
    xcopy = pltpu.make_async_copy(xin_ref, xb, lsem.at[30])
    ecopy = pltpu.make_async_copy(ein_ref, left.at[3, my], lsem.at[31])

    @pl.when(sec == 0)
    def _():
        xcopy.start()

    @pl.when(sec == 1)
    def _():
        ecopy.start()

    pl.semaphore_wait(barrier, 7)
    for copy in loads:
        copy.wait()

    def pair(src, dst, i):
        return go(src, dst, {"tensor": 1 - t}, psem_s.at[i], psem_r.at[i])

    def share(li, i):
        return pair(left.at[li, my], left.at[li, my], i)

    def shared(li, i):
        return pair(left.at[li, his], left.at[li, his], i)

    def hand(src, dst, i):
        return go(src, dst, {"section": 1 - sec}, psem_s.at[i], psem_r.at[i])

    def back_piece(x):
        return hand(sb.at[x], left.at[3, my, pl.ds(x * QUARTER, QUARTER)], 22 + x)

    ag_step, ag_ready, ag_finish = gather_steps(ring, g_ref, more[0:6])
    deal = deal_steps(ring, res, hid_out, more[6:13])

    @pl.when(sec == 0)
    def _():
        def body(i, carry):
            ag_step(i)
            return carry
        lax.fori_loop(0, 5, body, 0)
        ag_ready(0)
        xcopy.wait()

    @pl.when(sec == 1)
    def _():
        ecopy.wait()
        share(3, 10).start()

        def body(i, carry):
            ag_step(i)
            return carry

        lax.fori_loop(0, PIECES + 4, body, 0)

        def await_piece(i, carry):
            ag_ready(i)
            return carry

        lax.fori_loop(0, PIECES, await_piece, 0)

    def beside(step, piece=None):
        @pl.when(sec == 0)
        def _():
            ag_step(step)
            if piece is not None:
                ag_ready(piece)

    def wt(piece, lane):
        return g_ref[piece, :, :, :, :, pl.ds(pl.multiple_of(lane, TILE), TILE)].reshape(D, TILE)

    def wc(piece):
        return g_ref[piece].reshape(D, PW)

    def wq(piece, x, width=PW):
        return g_ref[piece, x, :, :, :, 0:width].reshape(QUARTER, width)

    right[0] = jnp.zeros((ALL, PW), BF16)
    small = wt(0, TILE)

    def unpack(j, carry):
        ci, r = iota((128, D), 0), iota((128, D), 1)
        sel = onehot(r == (ci // 4) * 48 + j * 4 + ci % 4)
        rw[j] = nn(sel, small).astype(BF16)
        return carry

    lax.fori_loop(0, 8, unpack, 0)
    dpi, r = iota((32, D), 0), iota((32, D), 1)
    t32 = nn(onehot(r == dpi * 48 + 32), small).astype(BF16)
    d1 = onehot(iota((32, 128), 1) // 4 == iota((32, 128), 0))
    e1 = tn(t32, d1)
    e1 = jnp.where(iota((256, 128), 0) % 4 == iota((256, 128), 1) % 4, e1, 0.0).astype(BF16)
    v1 = nn(onehot(iota((64, 256), 1) // 4 == iota((64, 256), 0)), e1)
    for i in range(64):
        vec[i] = v1[i:i + 1, :]
    t33 = nn(onehot(r == dpi * 48 + 33), small).astype(BF16)
    d2 = onehot(jnp.logical_and(r >= dpi * 48, r < dpi * 48 + 48))
    e2 = tn(t33[:, 0:128], d2)
    within = iota((128, D), 1) % 48
    q = iota((128, D), 0)
    gains[0] = jnp.sum(jnp.where(q == within, e2, 0.0), axis=0, keepdims=True)
    gains[1] = jnp.sum(jnp.where(q == within + 48, e2, 0.0), axis=0, keepdims=True)

    @pl.when(sec == 1)
    def _():
        hand(xb, xb, 21).wait_recv()

    def rows16(i):
        return pl.ds(pl.multiple_of(i * 16, 16), 16)

    def myrows16(i):
        return pl.ds(pl.multiple_of(t * HALF + i * 16, 16), 16)

    def scale_of(v):
        return lax.rsqrt(jnp.mean(v * v, axis=1, keepdims=True) + EPS)

    def norm_one(i, carry):
        v = xb[rows16(i), :].astype(F32)
        left[0, myrows16(i), :] = (v * scale_of(v) * gains[0]).astype(BF16)
        return carry

    lax.fori_loop(0, 9, norm_one, 0)
    share(0, 0).start()

    def into_branches(rows, first):
        def body(i, carry):
            if first:
                beside(5 + i, 1 + i)
            else:
                pl.when(i < 2)(lambda: beside(9 + i, 5 + i))
            pf[i, rows, :] = nn(left[0, rows, :], wc(1 + i))
            return carry
        lax.fori_loop(0, 4, body, 0)

    into_branches(my, True)
    shared(0, 0).wait_recv()
    into_branches(his, False)

    def vrow(a, j):
        return vec[a * 8 + j]

    def lanes_of(i, h):
        return pl.ds(pl.multiple_of((i % 2) * 256 + h * 128, 128), 128)

    def mixer(i, carry):
        beside(11 + i, 7 + i)
        for h in range(2):
            j = i * 2 + h
            lanes = lanes_of(i, h)
            feature = to_natural(pf[2 + i // 2, :, lanes])
            filtered = vrow(7, j)
            for k in range(4):
                filtered = filtered + vrow(3 + k, j) * (down(feature, k) * mask_ref[k - 1] if k else feature)
            low = filtered.astype(BF16)
            cv[j] = low
            conv = low.astype(F32)
            pre = nn(low, rw[j])
            rate = sigmoid(pre[:, 0:128] + vrow(0, j))
            inp = sigmoid(pre[:, 128:256] + vrow(1, j))
            rg[j] = rate
            ig[j] = inp
            decay = jnp.exp(-8.0 * rate * softplus(-vrow(2, j)))
            scale_in = jnp.sqrt(jnp.maximum(1.0 - decay * decay, FLOOR))
            state = scan_down(decay * mask_ref[0], scale_in * inp * conv)
            st[j] = state
            right[5 + i // 2, :, lanes] = (to_exchange(state) * gelu(pf[i // 2, :, lanes])).astype(BF16)
        return carry

    lax.fori_loop(0, 4, mixer, 0)

    def reduce_out(pieces, base, turn, also):
        def body(x, carry):
            total = None
            for piece in pieces:
                width = PW if piece else TILE
                part = nt(right[piece, :, 0:width], wq(piece, x, width))
                total = part if total is None else total + part
            acc[...] = total
            sb[x] = acc[his, :].astype(BF16)
            pair(sb.at[x], rb.at[turn, x], base + x).start()
            own[x] = acc[my, :]
            also(x)
            return carry

        lax.fori_loop(0, 4, body, 0)

    def reduce_wait(base, turn):
        for x in range(4):
            pair(sb.at[x], rb.at[turn, x], base + x).wait()

    def summed(i, turn):
        rows = rows16(i)
        return jnp.concatenate([own[x, rows, :] + rb[turn, x, rows, :].astype(F32) for x in range(4)], axis=1)

    reduce_out((5, 6), 1, 0, lambda x: beside(15 + x, 11 + x))
    reduce_wait(1, 0)

    def norm_two(i, carry):
        v = xb[rows16(i), :].astype(F32) + summed(i, 0)
        mid[rows16(i), :] = v
        left[2, myrows16(i), :] = (v * scale_of(v) * gains[1]).astype(BF16)
        return carry

    lax.fori_loop(0, 9, norm_two, 0)
    share(2, 5).start()

    def hidden_at(i):
        return (16 + i // 2) % PIECES, pl.multiple_of((i % 2) * TILE, TILE)

    def feed(rows, first):
        def body(i, carry):
            if first:
                pl.when(i < 5)(lambda: beside(19 + i, 15 + i))
            both = nn(left[2, rows, :], wc(7 + i))
            pg, pu = both[:, 0:TILE], both[:, TILE:PW]
            right[7 + i, rows, :] = both.astype(BF16)
            piece, lane = hidden_at(i)
            right[piece, rows, pl.ds(lane, TILE)] = (gelu(pg) * pu).astype(BF16)
            return carry
        lax.fori_loop(0, 9, body, 0)

    feed(my, True)
    shared(2, 5).wait_recv()
    feed(his, False)
    reduce_out((16, 17, 18, 19, 0), 6, 1, lambda x: None)
    reduce_wait(6, 1)

    def finish_forward(i, carry):
        v = mid[rows16(i), :] + summed(i, 1)
        res[rows16(i), :] = v.astype(BF16)
        return carry

    lax.fori_loop(0, 9, finish_forward, 0)

    @pl.when(sec == 0)
    def _():
        hand(res, xb, 21).start()
        for i in range(5):
            deal(i)
        for x in range(4):
            back_piece(x).wait_recv()
        share(3, 10).start()

    def deal_beside(i):
        @pl.when(sec == 1)
        def _():
            deal(i)

    deal_beside(0)
    ag_finish()
    shared(3, 10).wait_recv()

    def feed_back(i, carry):
        piece, lane = hidden_at(i)
        gh = nn(left[3], wt(piece, lane))
        pg = right[7 + i, :, 0:TILE].astype(F32)
        pu = right[7 + i, :, TILE:PW].astype(F32)
        act, slope = gelu_parts(pg)
        right[7 + i, :, 0:TILE] = (gh * pu * slope).astype(BF16)
        right[7 + i, :, TILE:PW] = (gh * act).astype(BF16)
        return carry

    lax.fori_loop(0, 9, feed_back, 0)
    around = (ring.ap, ring.am, ring.bp, ring.bm, ring.sib)

    def release(group):
        for dev in around:
            pl.semaphore_signal(free.at[group], inc=1, device_id={"dp": dev}, device_id_type=MESH)

    rs_step, rs_finish = reduce_steps(ring, g_ref, left, right, leftt, pp, sums_out, stage, free, lambda: pack_small(), more[13:20])

    def sum_beside(i, low, high):
        @pl.when(sec == 0)
        def _():
            rs_step(i, low, high)

    release(0)
    deal_beside(1)
    reduce_out(tuple(range(7, 16)), 11, 0, lambda x: sum_beside(x, 0, 3))
    release(1)
    reduce_wait(11, 0)

    def eight(v):
        return v[0:8] + v[8:16]

    def middle_back(i, carry):
        ng = summed(i, 0)
        m = mid[rows16(i), :]
        sc = scale_of(m)
        u = ng * gains[1]
        gm = left[3, myrows16(i), :].astype(F32) + sc * u - m * (sc * sc * sc) * jnp.mean(u * m, axis=1, keepdims=True)
        gmid[rows16(i), :] = gm
        left[1, myrows16(i), :] = gm.astype(BF16)
        return carry + eight(ng * m * sc)

    gpart[1] = lax.fori_loop(0, 9, middle_back, jnp.zeros((8, D), F32))
    share(1, 15).start()
    deal_beside(2)
    sum_beside(4, 4, 4)
    shared(1, 15).wait_recv()

    def mixer_back(i, carry):
        gmix = nn(left[1], wt(5 + i // 2, (i % 2) * TILE))
        sum_beside(5 + i, 5, 8)
        for h in range(2):
            j = i * 2 + h
            lanes = lanes_of(i, h)
            gm = gmix[:, h * 128:h * 128 + 128]
            act, slope = gelu_parts(pf[i // 2, :, lanes])
            state = st[j]
            right[1 + i // 2, :, lanes] = (gm * to_exchange(state) * slope).astype(BF16)
            grad_state = to_natural(gm * act)
            rate, inp = rg[j], ig[j]
            conv = cv[j].astype(F32)
            forget = softplus(-vrow(2, j))
            decay = jnp.exp(-8.0 * rate * forget)
            spare = 1.0 - decay * decay
            scale_in = jnp.sqrt(jnp.maximum(spare, FLOOR))
            m1 = mask_ref[0]
            drive = scan_up(up(decay * m1, 1), grad_state)
            grad_spare = jnp.where(spare > FLOOR, 0.5 * (drive * inp * conv) / scale_in, 0.0)
            grad_decay = drive * down(state, 1) * m1 - 2.0 * decay * grad_spare
            grad_log = grad_decay * decay
            rate_low = (grad_log * (-8.0 * forget) * rate * (1.0 - rate)).astype(BF16)
            driven = drive * scale_in
            input_low = (driven * conv * inp * (1.0 - inp)).astype(BF16)
            both = jnp.concatenate([rate_low, input_low], axis=1)
            back = nt(both, rw[j])
            vgrad[0 * 8 + j] = jnp.sum(rate_low.astype(F32), axis=0, keepdims=True)
            vgrad[1 * 8 + j] = jnp.sum(input_low.astype(F32), axis=0, keepdims=True)
            grad_forget = jnp.sum(grad_log * (-8.0 * rate), axis=0, keepdims=True)
            vgrad[2 * 8 + j] = -grad_forget * sigmoid(-vrow(2, j))
            sgrad[j] = tn(cv[j], both).astype(BF16)
            grad_conv = driven * inp + back
            feature = to_natural(pf[2 + i // 2, :, lanes])
            grad_feature = None
            for k in range(4):
                masked = grad_conv * mask_ref[k - 1] if k else grad_conv
                vgrad[(3 + k) * 8 + j] = jnp.sum(masked * down(feature, k), axis=0, keepdims=True)
                term = up(masked, k) * vrow(3 + k, j)
                grad_feature = term if grad_feature is None else grad_feature + term
            vgrad[7 * 8 + j] = jnp.sum(grad_conv, axis=0, keepdims=True)
            right[3 + i // 2, :, lanes] = to_exchange(grad_feature).astype(BF16)
        return carry

    lax.fori_loop(0, 4, mixer_back, 0)
    release(2)
    deal_beside(3)
    reduce_out((1, 2, 3, 4), 16, 1, lambda x: sum_beside(9 + x, 9, 12))
    release(3)
    reduce_wait(16, 1)

    def first_back(i, carry):
        fg = summed(i, 1)
        v = xb[rows16(i), :].astype(F32)
        sc = scale_of(v)
        u = fg * gains[0]
        gv = gmid[rows16(i), :] + sc * u - v * (sc * sc * sc) * jnp.mean(u * v, axis=1, keepdims=True)
        mid[rows16(i), :] = gv
        for x in range(4):
            sb[x, rows16(i), :] = gv[:, x * QUARTER:(x + 1) * QUARTER].astype(BF16)
        return carry + eight(fg * v * sc)

    gpart[0] = lax.fori_loop(0, 9, first_back, jnp.zeros((8, D), F32))

    @pl.when(sec == 1)
    def _():
        for x in range(4):
            back_piece(x).start()

    pair(gpart, gsum, 20).start()
    grad_copy = pltpu.make_async_copy(mid, grad_out, lsem.at[0])
    grad_copy.start()
    deal_beside(4)

    v2 = jnp.concatenate([vgrad[i] for i in range(64)], axis=0).astype(BF16)
    e2 = nn(onehot(iota((256, 64), 0) // 4 == iota((256, 64), 1)), v2)
    e2 = jnp.where(iota((256, 128), 0) % 4 == iota((256, 128), 1) % 4, e2, 0.0).astype(BF16)
    t32 = nt(d1, e2).astype(BF16)
    pair(gpart, gsum, 20).wait()
    n1 = jnp.sum(gpart[0] + gsum[0], axis=0, keepdims=True)
    n2 = jnp.sum(gpart[1] + gsum[1], axis=0, keepdims=True)
    spread = jnp.where(q == within, n1, jnp.where(q == within + 48, n2, 0.0)).astype(BF16)
    t33 = nt(d2, spread).astype(BF16)
    t33 = jnp.concatenate([t33, jnp.zeros((32, 128), BF16)], axis=1)

    def pack_part(x, carry):
        r = iota((QUARTER, 128), 0) + x * QUARTER
        ci = iota((QUARTER, 128), 1)
        total = None
        for j in range(8):
            sel = onehot(r == (ci // 4) * 48 + j * 4 + ci % 4)
            part = nn(sel, sgrad[j])
            total = part if total is None else total + part
        r = iota((QUARTER, 32), 0) + x * QUARTER
        dpi = iota((QUARTER, 32), 1)
        total = total + nn(onehot(r == dpi * 48 + 32), t32) + nn(onehot(r == dpi * 48 + 33), t33)
        pp[0, x, :, :, :, TILE:PW] = total.astype(BF16).reshape(4, 2, 48, TILE)
        return carry

    def pack_small():
        lax.fori_loop(0, 4, pack_part, 0)

    def last(i, carry):
        rs_step(i, 0, PIECES + 4)
        return carry

    lax.fori_loop(jnp.where(sec == 0, 13, 0), PIECES + 5, last, 0)
    rs_finish()
    deal(5)
    for li, i in ((0, 0), (2, 5), (3, 10), (1, 15)):
        share(li, i).wait_send()

    @pl.when(sec == 0)
    def _():
        hand(res, xb, 21).wait_send()

    @pl.when(sec == 1)
    def _():
        for x in range(4):
            back_piece(x).wait_send()

    grad_copy.wait()


def whole(gelu, lru, out, gate, up_, down_, small, xin, ein, masks):
    K = PIECES
    dma = pltpu.SemaphoreType.DMA
    vmem = pl.BlockSpec(memory_space=pltpu.VMEM)
    hbm = pl.BlockSpec(memory_space=pl.ANY)
    sds = jax.ShapeDtypeStruct
    return pl.pallas_call(
        whole_kernel,
        name="whole",
        out_shape=(sds((4, 4, 2, HALF, D), BF16), sds((HALF, D), F32), sds((K, 48, PW), F32)),
        in_specs=[hbm] * 9 + [vmem],
        out_specs=(hbm, hbm, hbm),
        scratch_shapes=[
            pltpu.VMEM((K, 4, 4, 2, 48, PW), BF16),
            pltpu.VMEM((HALF, D), BF16),
            pltpu.VMEM((4, ALL, D), BF16),
            pltpu.VMEM((K, ALL, PW), BF16),
            pltpu.VMEM((4, ALL, PW), F32),
            pltpu.VMEM((8, ALL, 128), BF16),
            pltpu.VMEM((8, ALL, 128), F32),
            pltpu.VMEM((8, ALL, 128), F32),
            pltpu.VMEM((8, ALL, 128), F32),
            pltpu.VMEM((HALF, D), F32),
            pltpu.VMEM((4, HALF, QUARTER), F32),
            pltpu.VMEM((4, HALF, QUARTER), BF16),
            pltpu.VMEM((2, 4, HALF, QUARTER), BF16),
            pltpu.VMEM((HALF, D), F32),
            pltpu.VMEM((8, 128, 256), BF16),
            pltpu.VMEM((64, 1, 128), F32),
            pltpu.VMEM((64, 1, 128), F32),
            pltpu.VMEM((2, 1, D), F32),
            pltpu.VMEM((2, 8, D), F32),
            pltpu.VMEM((2, 8, D), F32),
            pltpu.VMEM((8, 128, 256), BF16),
            pltpu.VMEM((ALL, QUARTER), F32),
            pltpu.VMEM((D, ALL), BF16),
            pltpu.VMEM((2, 4, 4, 2, 48, PW), BF16),
            pltpu.VMEM((2, 48, PW), F32),
            pltpu.VMEM((HALF, D), BF16),
            dma((32,)), dma((26,)), dma((26,)), pltpu.SemaphoreType.REGULAR((4,)),
            dma((K, 3)), dma((K, 3)), dma((K, 3)), dma((K, 3)), dma((K, 4)), dma((K, 4)),
            dma((4,)), dma((4,)), dma((4,)), dma((4,)), dma((4,)), dma((4,)), dma(()),
            dma((K,)), dma((K,)), dma((K, 3)), dma((K, 3)), dma((K, 3)), dma((K, 3)), dma((2,)),
        ],
        compiler_params=pltpu.CompilerParams(
            collective_id=1, has_side_effects=True, vmem_limit_bytes=VMEM_LIMIT
        ),
    )(gelu, lru, out, gate, up_, down_, small, xin, ein, masks)


def document_masks(doc_lengths):
    ends = jnp.cumsum(doc_lengths, axis=-1, dtype=jnp.int32)
    position = jnp.arange(HALF, dtype=jnp.int32)
    ident = jnp.sum((position[None, :, None] >= ends[:, None, :]).astype(jnp.int32), axis=-1, dtype=jnp.int32)
    masks = []
    for offset in range(1, 4):
        before = jnp.pad(ident, ((0, 0), (offset, 0)), constant_values=-1)[:, :HALF]
        masks.append((before == ident).astype(F32).reshape(ALL, 1))
    return jnp.broadcast_to(jnp.stack(masks), (3, ALL, 128))


def pack_small_shard(rate_weight, input_weight, rate_bias, input_bias, decay_param, filter_taps, filter_bias, norm_first, norm_second):
    vectors = jnp.concatenate([v[0].reshape(-1) for v in (rate_bias, input_bias, decay_param, filter_taps, filter_bias)]).reshape(1, 256)
    gains = jnp.concatenate([norm_first[0], norm_second[0], jnp.zeros((160,), BF16)]).reshape(1, 256)
    gates = jnp.concatenate([rate_weight[0].reshape(32, 128), input_weight[0].reshape(32, 128)], axis=1)
    return jnp.concatenate([gates, vectors, gains, jnp.zeros((14, 256), BF16)], axis=0)


def shards(
    inputs, out_grad, lengths, order, gelu_weight, lru_weight, rate_weight, input_weight, rate_bias, input_bias,
    decay_param, filter_taps, filter_bias, out_weight, gate_weight, up_weight, down_weight, norm_first, norm_second
):
    group = lax.axis_index("dp")
    masks = document_masks(lax.dynamic_index_in_dim(lengths, group, 1, keepdims=False))
    small = pack_small_shard(rate_weight, input_weight, rate_bias, input_bias, decay_param, filter_taps, filter_bias, norm_first, norm_second)
    every, grad, sums = whole(
        gelu_weight[0], lru_weight[0], out_weight[0].T, gate_weight[0], up_weight[0], down_weight[0].T, small,
        inputs.reshape(HALF, D), out_grad.reshape(HALF, D), masks
    )
    slots = jnp.arange(32, dtype=jnp.int32)
    source = jnp.sum(jnp.where(order == group, slots[None, :], 0), axis=1, dtype=jnp.int32)
    every = every.reshape(32, 2, 72, D)
    hidden = jnp.stack(
        [lax.dynamic_index_in_dim(every[:, m], source[m], 0, keepdims=False) for m in range(2)]
    ).astype(F32)[None]
    input_grad = grad.reshape(1, 2, 72, D)

    def side(pieces):
        return jnp.concatenate(pieces, axis=1)

    tiny = sums[0, :, TILE:]
    vec = tiny[32].reshape(8, 8, 4)
    down_grad = side([sums[16], sums[17], sums[18], sums[19], sums[0, :, :TILE]])
    return (
        hidden, input_grad,
        side([sums[1], sums[2]])[None], side([sums[3], sums[4]])[None],
        tiny[0:32, 0:128].reshape(1, 8, 4, 128), tiny[0:32, 128:256].reshape(1, 8, 4, 128),
        vec[0][None], vec[1][None], vec[2][None], vec[3:7][None], vec[7][None],
        side([sums[5], sums[6]]).T[None],
        side([sums[7 + i, :, :TILE] for i in range(9)])[None], side([sums[7 + i, :, TILE:] for i in range(9)])[None],
        down_grad.T[None], tiny[33, 0:48][None], tiny[33, 48:96][None],
    )


def solution(mesh):
    rows = P(None, ("dp", "tensor"), None)
    tall = P("section", "dp", "tensor")
    wide = P("section", "tensor", "dp")
    block = P("section", "tensor", "dp", None)
    taps = P("section", None, "tensor", "dp")
    gain = P("section", "dp")
    params = (tall, tall, block, block, wide, wide, wide, taps, wide, wide, tall, tall, wide, gain, gain)
    out_rows = P("section", None, ("dp", "tensor"), None)
    return jax.shard_map(
        shards,
        mesh=mesh,
        in_specs=(rows, rows, P(), P()) + params,
        out_specs=(out_rows, out_rows) + params,
        check_vma=False,
    )
```

time: 558 us -> 467 us (0.84)
  Pallas kernels: 502 us -> 431 us
  between operations: 18 us -> 4.75 us
  local copies, waits for them, and re-layouts: 33.2 us -> 24.2 us
    pallas_call x2 -> x1, Pallas kernels: 502 us -> 431 us  [whole(): pl.pallas_call(whole_kernel, name='whole', out_shape=(sds((4, 4, 2, HALF,...]
    unnamed x22 -> x37, local copies, waits for them, and re-layouts: 13.4 us -> 8.28 us
  transfers between devices with their start and end apart: 1 -> 0, of which waited for: 0 -> 0; matrix products, arithmetic and copies ran while one was open for 2% -> 0% of each run, Pallas kernels for 27% -> 0%
where the time goes in v3:
time: 467 us; the launch traced here: 465 us
  Pallas kernels  431 us (92%)
  local copies, waits for them, and re-layouts  24.2 us (5%)
  other arithmetic  5.07 us (1%)
  between operations  4.75 us (1%)
    pallas_call x1, Pallas kernels, whole(): pl.pallas_call(whole_kernel, name='whole', out_shape=(sds((4, 4, 2, HALF,...  431 us
    slice x1, local copies, waits for them, and re-layouts, shards(): every[:, m]  10.3 us

profile of v3, /device:TPU:0, one launch (start us, length us, event | category | flops | bytes accessed | tf_op | source)
XLA Modules:
  0.0 465.1 jit_solution(10073763707353928747)
XLA Ops:
  0.7 0.8 pad_maximum_fusion
  1.4 0.8 copy.56
  2.3 0.8 copy.57
  3.2 0.8 copy.58
  4.0 0.8 copy.59
  4.8 0.1 reshape_squeeze.27
  4.9 0.8 copy.60
  5.8 0.1 concatenate.38
  6.0 1.4 maximum_maximum_fusion.small_ref
  7.4 0.2 dynamic-slice_reduce_fusion
  7.6 0.2 reduce_window_sum.14
  7.8 0.1 convert_reduce_fusion
  7.9 0.1 stack_reshape.14
  8.2 0.9 broadcast_in_dim.57.mask_ref
  9.2 431.0 %whole.1 = (bf16[4,4,2,144,1536]{4,3,2,1,0:T(8,128)(2,1)}, f32[144,1536]{1,0:T(8,128)}, f32[20,48,512]{2,1,0:T(8,128)}) custom-call(bf16[48,1024]{1,0:T(8,128)(2,1)} %bitcast.109, bf16[48,1024]{1,0:T(8,128)(2,1)} %bitcast.110, bf16[48,1024]{1,0:T(8,128)(2,1)} %bitcast.111, bf16[48,2304]{1,0:T(8,128)(2,1)} %bitcast.106, bf16[48,2304]{1,0:T(8,128)(2,1)} %bitcast.107, ...), custom_call_target="tpu_custom_call" | custom-call | tf_op jit(solution)/shard_map/whole/pallas_call | solution.py:997
  440.2 10.3 %fusion.1 = (bf16[32,1,72,1536]{3,2,1,0:T(8,128)(2,1)}, bf16[32,1,72,1536]{3,2,1,0:T(8,128)(2,1)}) fusion(bf16[32,2,72,1536]{3,2,1,0:T(8,128)(2,1)} %bitcast.102), kind=kLoop, calls=%fused_computation.52 | loop fusion | bytes 28311552 | tf_op jit(solution)/shard_map/slice | solution.py:1074
  450.5 0.1 fusion
  450.6 0.6 fusion.4
  455.1 1.1 constant_dynamic-slice_fusion
  456.2 1.0 maximum_convert_fusion
  457.2 0.8 maximum_bitcast_fusion
  458.0 0.6 fusion.3
  458.6 0.1 slice_reduce_fusion
  458.8 0.7 copy.64
  459.5 0.7 copy.65
  460.3 0.7 copy.66
  461.0 0.1 broadcast_in_dim.62
  461.1 0.7 copy.67
  461.9 0.7 copy.68
  462.5 0.7 maximum_bitcast_fusion.2
  463.5 0.7 fusion.2
  464.2 0.9 copy.90
  (47 shorter events, 1.3 us)
Async XLA Ops:
  0.7 6.7 %copy-start = (s32[2,32,4]{1,2,0:T(4,128)S(1)}, s32[2,32,4]{1,2,0:T(4,128)}, u32[]{:S(2)}) copy-start(s32[2,32,4]{1,2,0:T(4,128)} %param.21) | copy-start | bytes 3076
  440.2 10.3 %copy-start.6 = (s32[2,32]{1,0:T(2,128)S(1)}, s32[2,32]{1,0:T(2,128)}, u32[]{:S(2)}) copy-start(s32[2,32]{1,0:T(2,128)} %param.22) | copy-start | bytes 772
  450.5 6.7 %copy-start.1 = (f32[20,48,512]{2,1,0:T(8,128)S(1)}, f32[20,48,512]{2,1,0:T(8,128)}, u32[]{:S(2)}) copy-start(f32[20,48,512]{2,1,0:T(8,128)} %get-tuple-element.22) | copy-start | bytes 5898244
  457.2 7.0 %copy-start.2 = (f32[144,1536]{1,0:T(8,128)S(1)}, f32[144,1536]{1,0:T(8,128)}, u32[]{:S(2)}) copy-start(f32[144,1536]{1,0:T(8,128)} %get-tuple-element.21) | copy-start | bytes 2654212
  463.5 1.6 copy-start.3
  463.5 1.6 copy-start.4
  463.5 1.6 copy-start.5

commit v4 on v3

--- a/solution.py
+++ b/solution.py
@@ -17,6 +17,7 @@
 ALL = 288
 D = 1536
 QUARTER = 384
+LAG = 2
 VMEM_LIMIT = 63 * 2**20
 
 
@@ -342,7 +343,7 @@
     return step
 
 
-def reduce_steps(ring, g_ref, left, right, leftt, pp, out_ref, stage, free, pack, sems):
+def reduce_steps(ring, g_ref, left, right, leftt, pp, outs, stage, staget, free, pack, sems):
     sbs, sbr, s1s, s1r, s2s, s2r, osem = sems
     c, x, z = ring.c, ring.x, ring.z
     K = PIECES
@@ -377,8 +378,48 @@
     def add(a, b):
         return a.astype(F32) + b.astype(F32)
 
-    def out_copy(k):
-        return pltpu.make_async_copy(stage.at[k % 2], out_ref.at[k], osem.at[k % 2])
+    gelu_o, lru_o, out_o, gate_o, up_o, down_o, small_o = outs
+
+    def groups(k):
+        slot = k % 2
+
+        def flat(ref, first, width=PW, lane=0, sem=0):
+            to = ref.at[:, pl.ds(pl.multiple_of(first, 128), width)]
+            return pltpu.make_async_copy(stage.at[slot, :, pl.ds(lane, width)], to, osem.at[slot, sem])
+
+        def turned(ref, first, height=PW):
+            to = ref.at[pl.ds(pl.multiple_of(first, 128), height)]
+            return pltpu.make_async_copy(staget.at[slot, pl.ds(0, height)], to, osem.at[slot, 0])
+
+        def between(low, high):
+            return jnp.logical_and(k >= low, k <= high)
+
+        return (
+            (between(1, 2), False, lambda: (flat(gelu_o, (k - 1) * PW),)),
+            (between(3, 4), False, lambda: (flat(lru_o, (k - 3) * PW),)),
+            (between(5, 6), True, lambda: (turned(out_o, (k - 5) * PW),)),
+            (between(7, 15), False, lambda: (flat(gate_o, (k - 7) * TILE, TILE), flat(up_o, (k - 7) * TILE, TILE, TILE, 1))),
+            (between(16, 19), True, lambda: (turned(down_o, (k - 16) * PW),)),
+            (k == 0, None, lambda: (turned(down_o, 4 * PW, TILE), flat(small_o, 0, TILE, TILE, 1))),
+        )
+
+    def put(k, value):
+        for cond, turn, copies in groups(k):
+            @pl.when(cond)
+            def _(turn=turn, copies=copies):
+                if turn is not False:
+                    staget[k % 2] = value.T
+                if turn is not True:
+                    stage[k % 2] = value
+                for copy in copies():
+                    copy.start()
+
+    def put_wait(k):
+        for cond, _, copies in groups(k):
+            @pl.when(cond)
+            def _(copies=copies):
+                for copy in copies():
+                    copy.wait()
 
     def step(t, low, high):
         for li, when in ((3, 0), (2, 4), (1, 13), (0, 15), (3, 19)):
@@ -397,55 +438,58 @@
             def _(group=group):
                 pl.semaphore_wait(free.at[group], 5)
 
-        @pl.when(t < K)
-        def _():
-            k = K - 1 - t
-
-            @pl.when(t >= 2)
+        @pl.when(jnp.logical_and(t >= 5 * LAG, t - 5 * LAG < K))
+        def _():
+            k = K - 1 - t + 5 * LAG
+            p2(k, 1, 1, ring.ap).wait_recv()
+            p2(k, 2, 3, ring.am).wait_recv()
+
+            @pl.when(t >= 5 * LAG + 2)
             def _():
-                ring.by_colour(lambda col: sib(k + 2, col).wait_send())
-
-            def body(xx, carry):
-                rows = pl.ds(pl.multiple_of(xx * QUARTER, 16), QUARTER)
-                part = nn(leftt[rows, :], right[k]).astype(BF16)
-                pp[k % 2, xx] = part.reshape(4, 2, 48, PW)
-                return carry
-
-            lax.fori_loop(0, 4, body, 0)
-
-            if high >= K - 1:
-                pl.when(k == 0)(pack)
-
-            ring.by_colour(lambda col: sib(k, col).start())
-
-        @pl.when(jnp.logical_and(t >= 1, t - 1 < K))
-        def _():
-            k = K - t
+                put_wait(k + 2)
+
+            put(k, add(g_ref[one(k, 0)], g_ref[k, 3, 1, 1]) + g_ref[k, 3, 2, 1].astype(F32))
+
+        @pl.when(jnp.logical_and(t >= 4 * LAG, t - 4 * LAG < K))
+        def _():
+            k = K - 1 - t + 4 * LAG
+
+            def h(par):
+                j = 1 if par == 0 else 3
+                p2(k, 0, 2, ring.ap).wait_recv()
+                g_ref[one(k, j)] = add(g_ref[one(k, j)], g_ref[k, 3, 0, 1]).astype(BF16)
+                if par == 0:
+                    p2(k, 1, 1, ring.ap).start()
+                else:
+                    p2(k, 2, 3, ring.am).start()
+
+            by_parity(k, h)
+
+        @pl.when(jnp.logical_and(t >= 3 * LAG, t - 3 * LAG < K))
+        def _():
+            k = K - 1 - t + 3 * LAG
 
             def f(col):
-                sib(k, col).wait_recv()
-
-                def body(xx, carry):
-                    g_ref[k, xx, :, 0] = add(g_ref[k, xx, :, 0], pp[k % 2, xx, :, col]).astype(BF16)
-                    return carry
-
-                lax.fori_loop(0, 4, body, 0)
-
-                def h(par):
-                    if par == 0:
-                        p1(k, 0, 2, ring.bp, col).start()
-                        p1(k, 2, 3, ring.bm, col).start()
-                    else:
-                        p1(k, 0, 2, ring.bm, col).start()
-                        p1(k, 1, 1, ring.bp, col).start()
-
-                by_parity(k, h)
+                p1(k, 1, 1, ring.bp, col).wait_recv()
+                p1(k, 2, 3, ring.bm, col).wait_recv()
+                mine = row(k, 0, col)
+                g_ref[mine] = (add(g_ref[mine], g_ref[k, 1, :, 1]) + g_ref[k, 2, :, 1].astype(F32)).astype(BF16)
 
             ring.by_colour(f)
 
-        @pl.when(jnp.logical_and(t >= 2, t - 2 < K))
-        def _():
-            k = K + 1 - t
+            def h(par):
+                if par == 0:
+                    p2(k, 0, 2, ring.ap).start()
+                    p2(k, 2, 3, ring.am).start()
+                else:
+                    p2(k, 0, 2, ring.am).start()
+                    p2(k, 1, 1, ring.ap).start()
+
+            by_parity(k, h)
+
+        @pl.when(jnp.logical_and(t >= 2 * LAG, t - 2 * LAG < K))
+        def _():
+            k = K - 1 - t + 2 * LAG
 
             def f(col):
                 def h(par):
@@ -461,62 +505,58 @@
 
             ring.by_colour(f)
 
-        @pl.when(jnp.logical_and(t >= 3, t - 3 < K))
-        def _():
-            k = K + 2 - t
+        @pl.when(jnp.logical_and(t >= 1 * LAG, t - 1 * LAG < K))
+        def _():
+            k = K - 1 - t + 1 * LAG
 
             def f(col):
-                p1(k, 1, 1, ring.bp, col).wait_recv()
-                p1(k, 2, 3, ring.bm, col).wait_recv()
-                mine = row(k, 0, col)
-                g_ref[mine] = (add(g_ref[mine], g_ref[k, 1, :, 1]) + g_ref[k, 2, :, 1].astype(F32)).astype(BF16)
+                sib(k, col).wait_recv()
+
+                def body(xx, carry):
+                    g_ref[k, xx, :, 0] = add(g_ref[k, xx, :, 0], pp[k % 2, xx, :, col]).astype(BF16)
+                    return carry
+
+                lax.fori_loop(0, 4, body, 0)
+
+                def h(par):
+                    if par == 0:
+                        p1(k, 0, 2, ring.bp, col).start()
+                        p1(k, 2, 3, ring.bm, col).start()
+                    else:
+                        p1(k, 0, 2, ring.bm, col).start()
+                        p1(k, 1, 1, ring.bp, col).start()
+
+                by_parity(k, h)
 
             ring.by_colour(f)
 
-            def h(par):
-                if par == 0:
-                    p2(k, 0, 2, ring.ap).start()
-                    p2(k, 2, 3, ring.am).start()
-                else:
-                    p2(k, 0, 2, ring.am).start()
-                    p2(k, 1, 1, ring.ap).start()
-
-            by_parity(k, h)
-
-        @pl.when(jnp.logical_and(t >= 4, t - 4 < K))
-        def _():
-            k = K + 3 - t
-
-            def h(par):
-                j = 1 if par == 0 else 3
-                p2(k, 0, 2, ring.ap).wait_recv()
-                g_ref[one(k, j)] = add(g_ref[one(k, j)], g_ref[k, 3, 0, 1]).astype(BF16)
-                if par == 0:
-                    p2(k, 1, 1, ring.ap).start()
-                else:
-                    p2(k, 2, 3, ring.am).start()
-
-            by_parity(k, h)
-
-        @pl.when(t >= 5)
-        def _():
-            k = K + 4 - t
-            p2(k, 1, 1, ring.ap).wait_recv()
-            p2(k, 2, 3, ring.am).wait_recv()
-
-            @pl.when(t >= 7)
+        @pl.when(t < K)
+        def _():
+            k = K - 1 - t
+
+            @pl.when(t >= 2)
             def _():
-                out_copy(k + 2).wait()
-
-            stage[k % 2] = add(g_ref[one(k, 0)], g_ref[k, 3, 1, 1]) + g_ref[k, 3, 2, 1].astype(F32)
-            out_copy(k).start()
+                ring.by_colour(lambda col: sib(k + 2, col).wait_send())
+
+            def body(xx, carry):
+                rows = pl.ds(pl.multiple_of(xx * QUARTER, 16), QUARTER)
+                part = nn(leftt[rows, :], right[k]).astype(BF16)
+                pp[k % 2, xx] = part.reshape(4, 2, 48, PW)
+                return carry
+
+            lax.fori_loop(0, 4, body, 0)
+
+            if high >= K - 1:
+                pl.when(k == 0)(pack)
+
+            ring.by_colour(lambda col: sib(k, col).start())
 
     def finish_one(k, carry):
         def f(col):
             @pl.when(k < 2)
             def _():
                 sib(k, col).wait_send()
-                out_copy(k).wait()
+                put_wait(k)
 
             for i in range(3):
                 p1(k, i, 1, ring.bp, col).wait_send()
@@ -531,16 +571,16 @@
 
 def whole_kernel(
     gelu_ref, lru_ref, out_ref, gate_ref, up_ref, down_ref, small_ref, xin_ref, ein_ref, mask_ref,
-    hid_out, grad_out, sums_out,
-    g_ref, xb, left, right, pf, cv, rg, ig, st, mid, own, sb, rb, gmid, rw, vec, vgrad, gains, gsum, gpart, sgrad, acc,
-    leftt, pp, stage, res,
-    lsem, psem_s, psem_r, free, *more,
+    hid_out, grad_out, gelu_o, lru_o, out_o, gate_o, up_o, down_o, small_o,
+    g_ref, xall, left, right, pf, cv, rg, ig, st, mid, own, sb, rb, gmid, rw, vec, vgrad, gains, gsum, gpart, sgrad, acc,
+    leftt, pp, stage, staget, res,
+    lsem, psem_s, psem_r, free, hand_s, hand_r, back_s, back_r, *more,
 ):
     sec = lax.axis_index("section")
     t = lax.axis_index("tensor")
     ring = Ring()
     barrier = pltpu.get_barrier_semaphore()
-    others = [{"dp": d} for d in (ring.ap, ring.am, ring.bp, ring.bm, ring.sib)] + [{"tensor": 1 - t}, {"section": 1 - sec}]
+    others = [{"dp": d} for d in (ring.ap, ring.am, ring.bp, ring.bm, ring.sib)] + [{"tensor": 1 - t}, {"section": 1 - sec}, {"section": 1 - sec, "tensor": 1 - t}]
     for dev in others:
         pl.semaphore_signal(barrier, inc=1, device_id=dev, device_id_type=MESH)
     loads = []
@@ -565,7 +605,7 @@
         copy.start()
     my = pl.ds(pl.multiple_of(t * HALF, 16), HALF)
     his = pl.ds(pl.multiple_of((1 - t) * HALF, 16), HALF)
-    xcopy = pltpu.make_async_copy(xin_ref, xb, lsem.at[30])
+    xcopy = pltpu.make_async_copy(xin_ref, xall.at[t], lsem.at[30])
     ecopy = pltpu.make_async_copy(ein_ref, left.at[3, my], lsem.at[31])
 
     @pl.when(sec == 0)
@@ -576,7 +616,7 @@
     def _():
         ecopy.start()
 
-    pl.semaphore_wait(barrier, 7)
+    pl.semaphore_wait(barrier, 8)
     for copy in loads:
         copy.wait()
 
@@ -589,11 +629,27 @@
     def shared(li, i):
         return pair(left.at[li, his], left.at[li, his], i)
 
-    def hand(src, dst, i):
-        return go(src, dst, {"section": 1 - sec}, psem_s.at[i], psem_r.at[i])
-
-    def back_piece(x):
-        return hand(sb.at[x], left.at[3, my, pl.ds(x * QUARTER, QUARTER)], 22 + x)
+    def rows48(i):
+        return pl.ds(pl.multiple_of(i * 48, 16), 48)
+
+    def half48(h, i):
+        return pl.ds(pl.multiple_of(h * HALF + i * 48, 16), 48)
+
+    def hand(to, r):
+        dev = {"section": 1 - sec, "tensor": (t + to) % 2}
+        return go(res.at[rows48(r)], xall.at[t, rows48(r)], dev, hand_s.at[to, r], hand_r.at[t, r])
+
+    def handed(h, r):
+        to = xall.at[h, rows48(r)]
+        return go(to, to, {"section": 1 - sec}, hand_s.at[0, r], hand_r.at[h, r])
+
+    def hand_back(to, r):
+        dev = {"section": 1 - sec, "tensor": (t + to) % 2}
+        return go(res.at[rows48(r)], left.at[3, half48(t, r)], dev, back_s.at[to, r], back_r.at[t, r])
+
+    def handed_back(h, r):
+        to = left.at[3, half48(h, r)]
+        return go(to, to, {"section": 1 - sec}, back_s.at[0, r], back_r.at[h, r])
 
     ag_step, ag_ready, ag_finish = gather_steps(ring, g_ref, more[0:6])
     deal = deal_steps(ring, res, hid_out, more[6:13])
@@ -666,40 +722,45 @@
     gains[0] = jnp.sum(jnp.where(q == within, e2, 0.0), axis=0, keepdims=True)
     gains[1] = jnp.sum(jnp.where(q == within + 48, e2, 0.0), axis=0, keepdims=True)
 
-    @pl.when(sec == 1)
-    def _():
-        hand(xb, xb, 21).wait_recv()
-
-    def rows16(i):
-        return pl.ds(pl.multiple_of(i * 16, 16), 16)
-
-    def myrows16(i):
-        return pl.ds(pl.multiple_of(t * HALF + i * 16, 16), 16)
-
     def scale_of(v):
         return lax.rsqrt(jnp.mean(v * v, axis=1, keepdims=True) + EPS)
 
-    def norm_one(i, carry):
-        v = xb[rows16(i), :].astype(F32)
-        left[0, myrows16(i), :] = (v * scale_of(v) * gains[0]).astype(BF16)
-        return carry
-
-    lax.fori_loop(0, 9, norm_one, 0)
-    share(0, 0).start()
+    def norm_one(h, i):
+        v = xall[h, rows48(i), :].astype(F32)
+        left[0, half48(h, i), :] = (v * scale_of(v) * gains[0]).astype(BF16)
 
     def into_branches(rows, first):
         def body(i, carry):
             if first:
                 beside(5 + i, 1 + i)
-            else:
+            elif first is False:
                 pl.when(i < 2)(lambda: beside(9 + i, 5 + i))
             pf[i, rows, :] = nn(left[0, rows, :], wc(1 + i))
             return carry
         lax.fori_loop(0, 4, body, 0)
 
-    into_branches(my, True)
-    shared(0, 0).wait_recv()
-    into_branches(his, False)
+    @pl.when(sec == 0)
+    def _():
+        def body(i, carry):
+            norm_one(t, i)
+            return carry
+
+        lax.fori_loop(0, 3, body, 0)
+        share(0, 0).start()
+        into_branches(my, True)
+        shared(0, 0).wait_recv()
+        into_branches(his, False)
+
+    @pl.when(sec == 1)
+    def _():
+        def body(i, carry):
+            for h in range(2):
+                handed(h, i).wait_recv()
+                norm_one(h, i)
+            return carry
+
+        lax.fori_loop(0, 3, body, 0)
+        into_branches(slice(None), None)
 
     def vrow(a, j):
         return vec[a * 8 + j]
@@ -754,19 +815,19 @@
             pair(sb.at[x], rb.at[turn, x], base + x).wait()
 
     def summed(i, turn):
-        rows = rows16(i)
+        rows = rows48(i)
         return jnp.concatenate([own[x, rows, :] + rb[turn, x, rows, :].astype(F32) for x in range(4)], axis=1)
 
     reduce_out((5, 6), 1, 0, lambda x: beside(15 + x, 11 + x))
     reduce_wait(1, 0)
 
     def norm_two(i, carry):
-        v = xb[rows16(i), :].astype(F32) + summed(i, 0)
-        mid[rows16(i), :] = v
-        left[2, myrows16(i), :] = (v * scale_of(v) * gains[1]).astype(BF16)
+        v = xall[t, rows48(i), :].astype(F32) + summed(i, 0)
+        mid[rows48(i), :] = v
+        left[2, half48(t, i), :] = (v * scale_of(v) * gains[1]).astype(BF16)
         return carry
 
-    lax.fori_loop(0, 9, norm_two, 0)
+    lax.fori_loop(0, 3, norm_two, 0)
     share(2, 5).start()
 
     def hidden_at(i):
@@ -775,7 +836,9 @@
     def feed(rows, first):
         def body(i, carry):
             if first:
-                pl.when(i < 5)(lambda: beside(19 + i, 15 + i))
+                pl.when(i % 4 == 0)(lambda: beside(19 + i // 4, 15 + i // 4))
+            else:
+                pl.when(jnp.logical_or(i == 3, i == 7))(lambda: beside(22 + i // 7, 18 + i // 7))
             both = nn(left[2, rows, :], wc(7 + i))
             pg, pu = both[:, 0:TILE], both[:, TILE:PW]
             right[7 + i, rows, :] = both.astype(BF16)
@@ -791,20 +854,25 @@
     reduce_wait(6, 1)
 
     def finish_forward(i, carry):
-        v = mid[rows16(i), :] + summed(i, 1)
-        res[rows16(i), :] = v.astype(BF16)
+        v = mid[rows48(i), :] + summed(i, 1)
+        res[rows48(i), :] = v.astype(BF16)
+
+        @pl.when(sec == 0)
+        def _():
+            hand(0, i).start()
+            hand(1, i).start()
+
         return carry
 
-    lax.fori_loop(0, 9, finish_forward, 0)
+    lax.fori_loop(0, 3, finish_forward, 0)
 
     @pl.when(sec == 0)
     def _():
-        hand(res, xb, 21).start()
         for i in range(5):
             deal(i)
-        for x in range(4):
-            back_piece(x).wait_recv()
-        share(3, 10).start()
+        for h in range(2):
+            for r in range(3):
+                handed_back(h, r).wait_recv()
 
     def deal_beside(i):
         @pl.when(sec == 1)
@@ -813,7 +881,9 @@
 
     deal_beside(0)
     ag_finish()
-    shared(3, 10).wait_recv()
+    @pl.when(sec == 1)
+    def _():
+        shared(3, 10).wait_recv()
 
     def feed_back(i, carry):
         piece, lane = hidden_at(i)
@@ -832,7 +902,7 @@
         for dev in around:
             pl.semaphore_signal(free.at[group], inc=1, device_id={"dp": dev}, device_id_type=MESH)
 
-    rs_step, rs_finish = reduce_steps(ring, g_ref, left, right, leftt, pp, sums_out, stage, free, lambda: pack_small(), more[13:20])
+    rs_step, rs_finish = reduce_steps(ring, g_ref, left, right, leftt, pp, (gelu_o, lru_o, out_o, gate_o, up_o, down_o, small_o), stage, staget, free, lambda: pack_small(), more[13:20])
 
     def sum_beside(i, low, high):
         @pl.when(sec == 0)
@@ -846,19 +916,23 @@
     reduce_wait(11, 0)
 
     def eight(v):
-        return v[0:8] + v[8:16]
+        total = v[0:8]
+        for i in range(1, 6):
+            total = total + v[i * 8:i * 8 + 8]
+        return total
 
     def middle_back(i, carry):
         ng = summed(i, 0)
-        m = mid[rows16(i), :]
+        m = mid[rows48(i), :]
         sc = scale_of(m)
         u = ng * gains[1]
-        gm = left[3, myrows16(i), :].astype(F32) + sc * u - m * (sc * sc * sc) * jnp.mean(u * m, axis=1, keepdims=True)
-        gmid[rows16(i), :] = gm
-        left[1, myrows16(i), :] = gm.astype(BF16)
+        e = left[3, half48(t, i), :].astype(F32)
+        gm = e + sc * u - m * (sc * sc * sc) * jnp.mean(u * m, axis=1, keepdims=True)
+        gmid[rows48(i), :] = gm
+        left[1, half48(t, i), :] = gm.astype(BF16)
         return carry + eight(ng * m * sc)
 
-    gpart[1] = lax.fori_loop(0, 9, middle_back, jnp.zeros((8, D), F32))
+    gpart[1] = lax.fori_loop(0, 3, middle_back, jnp.zeros((8, D), F32))
     share(1, 15).start()
     deal_beside(2)
     sum_beside(4, 4, 4)
@@ -917,22 +991,21 @@
 
     def first_back(i, carry):
         fg = summed(i, 1)
-        v = xb[rows16(i), :].astype(F32)
+        v = xall[t, rows48(i), :].astype(F32)
         sc = scale_of(v)
         u = fg * gains[0]
-        gv = gmid[rows16(i), :] + sc * u - v * (sc * sc * sc) * jnp.mean(u * v, axis=1, keepdims=True)
-        mid[rows16(i), :] = gv
-        for x in range(4):
-            sb[x, rows16(i), :] = gv[:, x * QUARTER:(x + 1) * QUARTER].astype(BF16)
+        gv = gmid[rows48(i), :] + sc * u - v * (sc * sc * sc) * jnp.mean(u * v, axis=1, keepdims=True)
+        mid[rows48(i), :] = gv
+
+        @pl.when(sec == 1)
+        def _():
+            res[rows48(i), :] = gv.astype(BF16)
+            hand_back(0, i).start()
+            hand_back(1, i).start()
+
         return carry + eight(fg * v * sc)
 
-    gpart[0] = lax.fori_loop(0, 9, first_back, jnp.zeros((8, D), F32))
-
-    @pl.when(sec == 1)
-    def _():
-        for x in range(4):
-            back_piece(x).start()
-
+    gpart[0] = lax.fori_loop(0, 3, first_back, jnp.zeros((8, D), F32))
     pair(gpart, gsum, 20).start()
     grad_copy = pltpu.make_async_copy(mid, grad_out, lsem.at[0])
     grad_copy.start()
@@ -967,23 +1040,28 @@
         lax.fori_loop(0, 4, pack_part, 0)
 
     def last(i, carry):
-        rs_step(i, 0, PIECES + 4)
+        rs_step(i, 0, PIECES + 5 * LAG - 1)
         return carry
 
-    lax.fori_loop(jnp.where(sec == 0, 13, 0), PIECES + 5, last, 0)
+    lax.fori_loop(jnp.where(sec == 0, 13, 0), PIECES + 5 * LAG, last, 0)
     rs_finish()
     deal(5)
-    for li, i in ((0, 0), (2, 5), (3, 10), (1, 15)):
-        share(li, i).wait_send()
+    share(2, 5).wait_send()
+    share(1, 15).wait_send()
 
     @pl.when(sec == 0)
     def _():
-        hand(res, xb, 21).wait_send()
+        share(0, 0).wait_send()
+        for to in range(2):
+            for r in range(3):
+                hand(to, r).wait_send()
 
     @pl.when(sec == 1)
     def _():
-        for x in range(4):
-            back_piece(x).wait_send()
+        share(3, 10).wait_send()
+        for to in range(2):
+            for r in range(3):
+                hand_back(to, r).wait_send()
 
     grad_copy.wait()
 
@@ -997,12 +1075,16 @@
     return pl.pallas_call(
         whole_kernel,
         name="whole",
-        out_shape=(sds((4, 4, 2, HALF, D), BF16), sds((HALF, D), F32), sds((K, 48, PW), F32)),
+        out_shape=(
+            sds((4, 4, 2, HALF, D), BF16), sds((HALF, D), F32),
+            sds((48, 1024), F32), sds((48, 1024), F32), sds((1024, 48), F32),
+            sds((48, 2304), F32), sds((48, 2304), F32), sds((2304, 48), F32), sds((48, TILE), F32),
+        ),
         in_specs=[hbm] * 9 + [vmem],
-        out_specs=(hbm, hbm, hbm),
+        out_specs=(hbm,) * 9,
         scratch_shapes=[
             pltpu.VMEM((K, 4, 4, 2, 48, PW), BF16),
-            pltpu.VMEM((HALF, D), BF16),
+            pltpu.VMEM((2, HALF, D), BF16),
             pltpu.VMEM((4, ALL, D), BF16),
             pltpu.VMEM((K, ALL, PW), BF16),
             pltpu.VMEM((4, ALL, PW), F32),
@@ -1026,11 +1108,13 @@
             pltpu.VMEM((D, ALL), BF16),
             pltpu.VMEM((2, 4, 4, 2, 48, PW), BF16),
             pltpu.VMEM((2, 48, PW), F32),
+            pltpu.VMEM((2, PW, 48), F32),
             pltpu.VMEM((HALF, D), BF16),
-            dma((32,)), dma((26,)), dma((26,)), pltpu.SemaphoreType.REGULAR((4,)),
+            dma((32,)), dma((21,)), dma((21,)), pltpu.SemaphoreType.REGULAR((4,)),
+            dma((2, 3)), dma((2, 3)), dma((2, 3)), dma((2, 3)),
             dma((K, 3)), dma((K, 3)), dma((K, 3)), dma((K, 3)), dma((K, 4)), dma((K, 4)),
             dma((4,)), dma((4,)), dma((4,)), dma((4,)), dma((4,)), dma((4,)), dma(()),
-            dma((K,)), dma((K,)), dma((K, 3)), dma((K, 3)), dma((K, 3)), dma((K, 3)), dma((2,)),
+            dma((K,)), dma((K,)), dma((K, 3)), dma((K, 3)), dma((K, 3)), dma((K, 3)), dma((2, 2)),
         ],
         compiler_params=pltpu.CompilerParams(
             collective_id=1, has_side_effects=True, vmem_limit_bytes=VMEM_LIMIT
@@ -1063,7 +1147,7 @@
     group = lax.axis_index("dp")
     masks = document_masks(lax.dynamic_index_in_dim(lengths, group, 1, keepdims=False))
     small = pack_small_shard(rate_weight, input_weight, rate_bias, input_bias, decay_param, filter_taps, filter_bias, norm_first, norm_second)
-    every, grad, sums = whole(
+    every, grad, gelu_grad, lru_grad, out_wgrad, gate_grad, up_grad, down_grad, tiny = whole(
         gelu_weight[0], lru_weight[0], out_weight[0].T, gate_weight[0], up_weight[0], down_weight[0].T, small,
         inputs.reshape(HALF, D), out_grad.reshape(HALF, D), masks
     )
@@ -1075,20 +1159,13 @@
     ).astype(F32)[None]
     input_grad = grad.reshape(1, 2, 72, D)
 
-    def side(pieces):
-        return jnp.concatenate(pieces, axis=1)
-
-    tiny = sums[0, :, TILE:]
     vec = tiny[32].reshape(8, 8, 4)
-    down_grad = side([sums[16], sums[17], sums[18], sums[19], sums[0, :, :TILE]])
     return (
-        hidden, input_grad,
-        side([sums[1], sums[2]])[None], side([sums[3], sums[4]])[None],
+        hidden, input_grad, gelu_grad[None], lru_grad[None],
         tiny[0:32, 0:128].reshape(1, 8, 4, 128), tiny[0:32, 128:256].reshape(1, 8, 4, 128),
         vec[0][None], vec[1][None], vec[2][None], vec[3:7][None], vec[7][None],
-        side([sums[5], sums[6]]).T[None],
-        side([sums[7 + i, :, :TILE] for i in range(9)])[None], side([sums[7 + i, :, TILE:] for i in range(9)])[None],
-        down_grad.T[None], tiny[33, 0:48][None], tiny[33, 48:96][None],
+        out_wgrad[None], gate_grad[None], up_grad[None], down_grad[None],
+        tiny[33, 0:48][None], tiny[33, 48:96][None],
     )
 
 

time: 467 us -> 431 us (0.923)
  Pallas kernels: 431 us -> 390 us
  local copies, waits for them, and re-layouts: 24.2 us -> 31.9 us
    pallas_call x1, Pallas kernels: 431 us -> 390 us  [whole(): pl.pallas_call(whole_kernel, name='whole', out_shape=(sds((4, 4, 2, HALF,...]
    unnamed x37 -> x33, local copies, waits for them, and re-layouts: 8.28 us -> 15.6 us
where the time goes in v4:
time: 431 us
  Pallas kernels  390 us (90%)
  local copies, waits for them, and re-layouts  31.9 us (7%)
  between operations  4.65 us (1%)
    pallas_call x1, Pallas kernels, whole(): pl.pallas_call(whole_kernel, name='whole', out_shape=(sds((4, 4, 2, HALF,...  390 us
    unnamed x33, local copies, waits for them, and re-layouts  15.6 us
    slice x1, local copies, waits for them, and re-layouts, shards(): every[:, m]  10.8 us

profile of v4, /device:TPU:0, one launch (start us, length us, event | category | flops | bytes accessed | tf_op | source)
XLA Modules:
  0.0 430.5 jit_solution(15989694454683873853)
XLA Ops:
  0.7 0.7 copy-done
  1.3 0.2 dynamic-slice_reduce_fusion
  1.6 0.2 reduce_window_sum.14
  2.2 0.9 broadcast_in_dim.57.mask_ref
  3.1 0.8 copy.63
  3.9 0.1 reshape_squeeze.27
  4.1 0.8 copy.60
  4.9 0.8 copy.61
  5.8 0.8 copy.62
  6.6 0.8 copy.64
  7.6 0.8 pad_maximum_fusion
  8.4 1.4 maximum_maximum_fusion.small_ref
  9.8 390.4 %whole.1 = (bf16[4,4,2,144,1536]{4,3,2,1,0:T(8,128)(2,1)}, f32[144,1536]{1,0:T(8,128)}, f32[48,1024]{1,0:T(8,128)}, f32[48,1024]{1,0:T(8,128)}, f32[1024,48]{1,0...) custom-call(bf16[48,1024]{1,0:T(8,128)(2,1)} %bitcast.48, ...), custom_call_target="tpu_custom_call" | custom-call | tf_op jit(solution)/shard_map/whole/pallas_call | solution.py:1075
  400.3 10.8 %fusion.1 = (bf16[32,1,72,1536]{3,2,1,0:T(8,128)(2,1)}, bf16[32,1,72,1536]{3,2,1,0:T(8,128)(2,1)}) fusion(bf16[32,2,72,1536]{3,2,1,0:T(8,128)(2,1)} %bitcast.35), kind=kLoop, calls=%fused_computation.19 | loop fusion | bytes 28311552 | tf_op jit(solution)/shard_map/slice | solution.py:1158
  411.1 0.1 fusion
  411.2 0.6 fusion.4
  415.7 1.1 constant_dynamic-slice_fusion
  416.8 1.0 maximum_convert_fusion
  417.9 0.7 copy.68
  418.6 0.7 copy.69
  419.4 0.7 copy.70
  420.1 0.7 copy.72
  420.8 0.6 fusion.3
  421.4 0.6 fusion.2
  422.2 0.7 copy.71
  422.9 1.1 copy.74
  424.0 0.9 copy.73
  424.8 0.9 copy.80
  425.8 1.6 copy.81
  427.4 1.6 copy.82
  429.0 0.8 copy.83
  429.8 0.8 copy.84
  (38 shorter events, 1.6 us)
Async XLA Ops:
  0.7 0.7 copy-start
  400.2 10.9 %copy-start.7 = (s32[2,32]{1,0:T(2,128)S(1)}, s32[2,32]{1,0:T(2,128)}, u32[]{:S(2)}) copy-start(s32[2,32]{1,0:T(2,128)} %param.22) | copy-start | bytes 772
  400.2 17.5 %copy-start.6 = (f32[48,256]{1,0:T(8,128)S(1)}, f32[48,256]{1,0:T(8,128)}, u32[]{:S(2)}) copy-start(f32[48,256]{1,0:T(8,128)} %get-tuple-element.30) | copy-start | bytes 147460
  400.2 22.6 %copy-start.1 = (f32[2304,48]{1,0:T(8,128)S(1)}, f32[2304,48]{1,0:T(8,128)}, u32[]{:S(2)}) copy-start(f32[2304,48]{1,0:T(8,128)} %get-tuple-element.34) | copy-start | bytes 1327108
  400.2 23.7 %copy-start.3 = (f32[1024,48]{1,0:T(8,128)S(1)}, f32[1024,48]{1,0:T(8,128)}, u32[]{:S(2)}) copy-start(f32[1024,48]{1,0:T(8,128)} %get-tuple-element.31) | copy-start | bytes 589828
  400.2 24.6 %copy-start.2 = (f32[144,1536]{1,0:T(8,128)S(1)}, f32[144,1536]{1,0:T(8,128)}, u32[]{:S(2)}) copy-start(f32[144,1536]{1,0:T(8,128)} %get-tuple-element.27) | copy-start | bytes 2654212
  411.1 17.9 %copy-start.5 = (f32[48,2304]{1,0:T(8,128)S(1)}, f32[48,2304]{1,0:T(8,128)}, u32[]{:S(2)}) copy-start(f32[48,2304]{1,0:T(8,128)} %get-tuple-element.32) | copy-start | bytes 1327108
  411.1 18.7 %copy-start.4 = (f32[48,2304]{1,0:T(8,128)S(1)}, f32[48,2304]{1,0:T(8,128)}, u32[]{:S(2)}) copy-start(f32[48,2304]{1,0:T(8,128)} %get-tuple-element.33) | copy-start | bytes 1327108

commit v5 on v4

--- a/solution.py
+++ b/solution.py
@@ -18,6 +18,7 @@
 D = 1536
 QUARTER = 384
 LAG = 2
+SLACK = 2
 VMEM_LIMIT = 63 * 2**20
 
 
@@ -178,9 +179,9 @@
             p1(t, 0, False).start()
             p1(t, 1, False).start()
 
-        @pl.when(jnp.logical_and(t >= 1, t - 1 < K))
-        def _():
-            k = t - 1
+        @pl.when(jnp.logical_and(t >= SLACK, t - SLACK < K))
+        def _():
+            k = t - SLACK
 
             def f(par):
                 p1(k, par, True).wait_recv()
@@ -189,9 +190,9 @@
 
             by_parity(k, f)
 
-        @pl.when(jnp.logical_and(t >= 2, t - 2 < K))
-        def _():
-            k = t - 2
+        @pl.when(jnp.logical_and(t >= 2 * SLACK, t - 2 * SLACK < K))
+        def _():
+            k = t - 2 * SLACK
             by_parity(k, lambda par: p1f(k, par, True).wait_recv())
 
             def f(col):
@@ -201,9 +202,9 @@
 
             ring.by_colour(f)
 
-        @pl.when(jnp.logical_and(t >= 3, t - 3 < K))
-        def _():
-            k = t - 3
+        @pl.when(jnp.logical_and(t >= 3 * SLACK, t - 3 * SLACK < K))
+        def _():
+            k = t - 3 * SLACK
 
             def f(col):
                 def h(par):
@@ -217,9 +218,9 @@
 
             ring.by_colour(f)
 
-        @pl.when(t >= 4)
-        def _():
-            k = t - 4
+        @pl.when(t >= 4 * SLACK)
+        def _():
+            k = t - 4 * SLACK
 
             def f(col):
                 by_parity(k, lambda par: p2f(k, par, True, col).wait_recv())
@@ -343,7 +344,7 @@
     return step
 
 
-def reduce_steps(ring, g_ref, left, right, leftt, pp, outs, stage, staget, free, pack, sems):
+def reduce_steps(ring, g_ref, left, right, leftt, pp, outs, stage, free, pack, sems):
     sbs, sbr, s1s, s1r, s2s, s2r, osem = sems
     c, x, z = ring.c, ring.x, ring.z
     K = PIECES
@@ -387,35 +388,28 @@
             to = ref.at[:, pl.ds(pl.multiple_of(first, 128), width)]
             return pltpu.make_async_copy(stage.at[slot, :, pl.ds(lane, width)], to, osem.at[slot, sem])
 
-        def turned(ref, first, height=PW):
-            to = ref.at[pl.ds(pl.multiple_of(first, 128), height)]
-            return pltpu.make_async_copy(staget.at[slot, pl.ds(0, height)], to, osem.at[slot, 0])
-
         def between(low, high):
             return jnp.logical_and(k >= low, k <= high)
 
         return (
-            (between(1, 2), False, lambda: (flat(gelu_o, (k - 1) * PW),)),
-            (between(3, 4), False, lambda: (flat(lru_o, (k - 3) * PW),)),
-            (between(5, 6), True, lambda: (turned(out_o, (k - 5) * PW),)),
-            (between(7, 15), False, lambda: (flat(gate_o, (k - 7) * TILE, TILE), flat(up_o, (k - 7) * TILE, TILE, TILE, 1))),
-            (between(16, 19), True, lambda: (turned(down_o, (k - 16) * PW),)),
-            (k == 0, None, lambda: (turned(down_o, 4 * PW, TILE), flat(small_o, 0, TILE, TILE, 1))),
+            (between(1, 2), lambda: (flat(gelu_o, (k - 1) * PW),)),
+            (between(3, 4), lambda: (flat(lru_o, (k - 3) * PW),)),
+            (between(5, 6), lambda: (flat(out_o, (k - 5) * PW),)),
+            (between(7, 15), lambda: (flat(gate_o, (k - 7) * TILE, TILE), flat(up_o, (k - 7) * TILE, TILE, TILE, 1))),
+            (between(16, 19), lambda: (flat(down_o, (k - 16) * PW),)),
+            (k == 0, lambda: (flat(down_o, 4 * PW, TILE), flat(small_o, 0, TILE, TILE, 1))),
         )
 
     def put(k, value):
-        for cond, turn, copies in groups(k):
+        stage[k % 2] = value
+        for cond, copies in groups(k):
             @pl.when(cond)
-            def _(turn=turn, copies=copies):
-                if turn is not False:
-                    staget[k % 2] = value.T
-                if turn is not True:
-                    stage[k % 2] = value
+            def _(copies=copies):
                 for copy in copies():
                     copy.start()
 
     def put_wait(k):
-        for cond, _, copies in groups(k):
+        for cond, copies in groups(k):
             @pl.when(cond)
             def _(copies=copies):
                 for copy in copies():
@@ -573,7 +567,7 @@
     gelu_ref, lru_ref, out_ref, gate_ref, up_ref, down_ref, small_ref, xin_ref, ein_ref, mask_ref,
     hid_out, grad_out, gelu_o, lru_o, out_o, gate_o, up_o, down_o, small_o,
     g_ref, xall, left, right, pf, cv, rg, ig, st, mid, own, sb, rb, gmid, rw, vec, vgrad, gains, gsum, gpart, sgrad, acc,
-    leftt, pp, stage, staget, res,
+    leftt, pp, stage, res,
     lsem, psem_s, psem_r, free, hand_s, hand_r, back_s, back_r, *more,
 ):
     sec = lax.axis_index("section")
@@ -659,7 +653,7 @@
         def body(i, carry):
             ag_step(i)
             return carry
-        lax.fori_loop(0, 5, body, 0)
+        lax.fori_loop(0, 4 * SLACK + 1, body, 0)
         ag_ready(0)
         xcopy.wait()
 
@@ -672,7 +666,7 @@
             ag_step(i)
             return carry
 
-        lax.fori_loop(0, PIECES + 4, body, 0)
+        lax.fori_loop(0, PIECES + 4 * SLACK, body, 0)
 
         def await_piece(i, carry):
             ag_ready(i)
@@ -680,12 +674,11 @@
 
         lax.fori_loop(0, PIECES, await_piece, 0)
 
-    def beside(step, piece=None):
+    def beside(piece):
         @pl.when(sec == 0)
         def _():
-            ag_step(step)
-            if piece is not None:
-                ag_ready(piece)
+            ag_step(piece + 4 * SLACK)
+            ag_ready(piece)
 
     def wt(piece, lane):
         return g_ref[piece, :, :, :, :, pl.ds(pl.multiple_of(lane, TILE), TILE)].reshape(D, TILE)
@@ -732,9 +725,9 @@
     def into_branches(rows, first):
         def body(i, carry):
             if first:
-                beside(5 + i, 1 + i)
+                beside(1 + i)
             elif first is False:
-                pl.when(i < 2)(lambda: beside(9 + i, 5 + i))
+                pl.when(i < 2)(lambda: beside(5 + i))
             pf[i, rows, :] = nn(left[0, rows, :], wc(1 + i))
             return carry
         lax.fori_loop(0, 4, body, 0)
@@ -769,7 +762,7 @@
         return pl.ds(pl.multiple_of((i % 2) * 256 + h * 128, 128), 128)
 
     def mixer(i, carry):
-        beside(11 + i, 7 + i)
+        beside(7 + i)
         for h in range(2):
             j = i * 2 + h
             lanes = lanes_of(i, h)
@@ -818,7 +811,7 @@
         rows = rows48(i)
         return jnp.concatenate([own[x, rows, :] + rb[turn, x, rows, :].astype(F32) for x in range(4)], axis=1)
 
-    reduce_out((5, 6), 1, 0, lambda x: beside(15 + x, 11 + x))
+    reduce_out((5, 6), 1, 0, lambda x: beside(11 + x))
     reduce_wait(1, 0)
 
     def norm_two(i, carry):
@@ -836,9 +829,9 @@
     def feed(rows, first):
         def body(i, carry):
             if first:
-                pl.when(i % 4 == 0)(lambda: beside(19 + i // 4, 15 + i // 4))
+                pl.when(i % 4 == 0)(lambda: beside(15 + i // 4))
             else:
-                pl.when(jnp.logical_or(i == 3, i == 7))(lambda: beside(22 + i // 7, 18 + i // 7))
+                pl.when(jnp.logical_or(i == 3, i == 7))(lambda: beside(18 + i // 7))
             both = nn(left[2, rows, :], wc(7 + i))
             pg, pu = both[:, 0:TILE], both[:, TILE:PW]
             right[7 + i, rows, :] = both.astype(BF16)
@@ -902,7 +895,7 @@
         for dev in around:
             pl.semaphore_signal(free.at[group], inc=1, device_id={"dp": dev}, device_id_type=MESH)
 
-    rs_step, rs_finish = reduce_steps(ring, g_ref, left, right, leftt, pp, (gelu_o, lru_o, out_o, gate_o, up_o, down_o, small_o), stage, staget, free, lambda: pack_small(), more[13:20])
+    rs_step, rs_finish = reduce_steps(ring, g_ref, left, right, leftt, pp, (gelu_o, lru_o, out_o, gate_o, up_o, down_o, small_o), stage, free, lambda: pack_small(), more[13:20])
 
     def sum_beside(i, low, high):
         @pl.when(sec == 0)
@@ -1077,8 +1070,8 @@
         name="whole",
         out_shape=(
             sds((4, 4, 2, HALF, D), BF16), sds((HALF, D), F32),
-            sds((48, 1024), F32), sds((48, 1024), F32), sds((1024, 48), F32),
-            sds((48, 2304), F32), sds((48, 2304), F32), sds((2304, 48), F32), sds((48, TILE), F32),
+            sds((48, 1024), F32), sds((48, 1024), F32), sds((48, 1024), F32),
+            sds((48, 2304), F32), sds((48, 2304), F32), sds((48, 2304), F32), sds((48, TILE), F32),
         ),
         in_specs=[hbm] * 9 + [vmem],
         out_specs=(hbm,) * 9,
@@ -1108,7 +1101,6 @@
             pltpu.VMEM((D, ALL), BF16),
             pltpu.VMEM((2, 4, 4, 2, 48, PW), BF16),
             pltpu.VMEM((2, 48, PW), F32),
-            pltpu.VMEM((2, PW, 48), F32),
             pltpu.VMEM((HALF, D), BF16),
             dma((32,)), dma((21,)), dma((21,)), pltpu.SemaphoreType.REGULAR((4,)),
             dma((2, 3)), dma((2, 3)), dma((2, 3)), dma((2, 3)),
@@ -1120,6 +1112,37 @@
             collective_id=1, has_side_effects=True, vmem_limit_bytes=VMEM_LIMIT
         ),
     )(gelu, lru, out, gate, up_, down_, small, xin, ein, masks)
+
+
+def settle_kernel(source_ref, every, *refs):
+    ins, outs, (buf, sem, pick) = refs[0:7], refs[7:15], refs[15:18]
+    hid_o = outs[0]
+    picks = [pltpu.make_async_copy(every.at[source_ref[m]], buf.at[m], pick.at[m]) for m in range(2)]
+    for copy in picks:
+        copy.start()
+    copies = [pltpu.make_async_copy(a, b, sem.at[i]) for i, (a, b) in enumerate(zip(ins, outs[1:]))]
+    for copy in copies:
+        copy.start()
+    for copy in picks:
+        copy.wait()
+    hid_o[0:72, :] = buf[0].astype(F32)[0:72]
+    hid_o[72:144, :] = buf[1].astype(F32)[72:144]
+    for copy in copies:
+        copy.wait()
+
+
+def settle(source, every, *results):
+    vmem = pl.BlockSpec(memory_space=pltpu.VMEM)
+    hbm = pl.BlockSpec(memory_space=pl.ANY)
+    return pl.pallas_call(
+        settle_kernel,
+        name="settle",
+        out_shape=(jax.ShapeDtypeStruct((HALF, D), F32),) + tuple(jax.ShapeDtypeStruct(r.shape, F32) for r in results),
+        in_specs=[pl.BlockSpec(memory_space=pltpu.SMEM), hbm] + [vmem] * 7,
+        out_specs=(vmem,) + (hbm,) * 7,
+        scratch_shapes=[pltpu.VMEM((2, HALF, D), BF16), pltpu.SemaphoreType.DMA((7,)), pltpu.SemaphoreType.DMA((2,))],
+        compiler_params=pltpu.CompilerParams(vmem_limit_bytes=32 * 2**20),
+    )(source, every, *results)
 
 
 def document_masks(doc_lengths):
@@ -1153,18 +1176,17 @@
     )
     slots = jnp.arange(32, dtype=jnp.int32)
     source = jnp.sum(jnp.where(order == group, slots[None, :], 0), axis=1, dtype=jnp.int32)
-    every = every.reshape(32, 2, 72, D)
-    hidden = jnp.stack(
-        [lax.dynamic_index_in_dim(every[:, m], source[m], 0, keepdims=False) for m in range(2)]
-    ).astype(F32)[None]
+    hidden, grad, gelu_grad, lru_grad, out_wgrad, gate_grad, up_grad, down_grad = settle(
+        source, every.reshape(32, HALF, D), grad, gelu_grad, lru_grad, out_wgrad, gate_grad, up_grad, down_grad
+    )
+    hidden = hidden.reshape(1, 2, 72, D)
     input_grad = grad.reshape(1, 2, 72, D)
-
     vec = tiny[32].reshape(8, 8, 4)
     return (
         hidden, input_grad, gelu_grad[None], lru_grad[None],
         tiny[0:32, 0:128].reshape(1, 8, 4, 128), tiny[0:32, 128:256].reshape(1, 8, 4, 128),
         vec[0][None], vec[1][None], vec[2][None], vec[3:7][None], vec[7][None],
-        out_wgrad[None], gate_grad[None], up_grad[None], down_grad[None],
+        out_wgrad.T[None], gate_grad[None], up_grad[None], down_grad.T[None],
         tiny[33, 0:48][None], tiny[33, 48:96][None],
     )
 

time: 431 us -> 404 us (0.937)
  Pallas kernels: 390 us -> 376 us
  local copies, waits for them, and re-layouts: 31.9 us -> 23.1 us
    pallas_call x1, Pallas kernels: 390 us -> 373 us  [whole(): pl.pallas_call(whole_kernel, name='whole', out_shape=(sds((4, 4, 2, HALF,...]
    slice x2 -> x0, local copies, waits for them, and re-layouts: 11.4 us -> none  [the longest x1 10.8 us: shards(): every[:, m]]
    unnamed x33 -> x30, local copies, waits for them, and re-layouts: 15.6 us -> 19.2 us
where the time goes in v5:
time: 404 us; the launch traced here: 403 us
  Pallas kernels  376 us (93%)
  local copies, waits for them, and re-layouts  23.1 us (6%)
    pallas_call x1, Pallas kernels, whole(): pl.pallas_call(whole_kernel, name='whole', out_shape=(sds((4, 4, 2, HALF,...  373 us
    unnamed x30, local copies, waits for them, and re-layouts  19.2 us

profile of v5, /device:TPU:0, one launch (start us, length us, event | category | flops | bytes accessed | tf_op | source)
XLA Modules:
  0.0 403.3 jit_solution(2032357806711681855)
XLA Ops:
  0.7 0.8 fusion.source_ref
  1.5 0.2 dynamic-slice_reduce_fusion
  1.7 0.2 reduce_window_sum.14
  2.0 0.8 pad_maximum_fusion
  3.2 0.8 copy.56
  4.0 0.8 copy.57
  4.9 0.8 copy.58
  5.7 0.8 copy.60
  6.6 0.8 copy.59
  7.4 0.1 reshape_squeeze.27
  7.5 0.1 concatenate.13
  7.6 1.4 maximum_maximum_fusion.small_ref
  9.0 0.9 broadcast_in_dim.58.mask_ref
  10.0 372.6 %whole.1 = (bf16[4,4,2,144,1536]{4,3,2,1,0:T(8,128)(2,1)}, f32[144,1536]{1,0:T(8,128)}, f32[48,1024]{1,0:T(8,128)}, f32[48,1024]{1,0:T(8,128)}, f32[48,1024]{1,0...) custom-call(bf16[48,1024]{1,0:T(8,128)(2,1)} %bitcast.44, ...), custom_call_target="tpu_custom_call" | custom-call | tf_op jit(solution)/shard_map/whole/pallas_call | solution.py:1068
  382.6 5.0 %copy-done.1 = bf16[4,4,2,144,1536]{4,3,2,1,0:T(8,128)(2,1)S(1)} copy-done((bf16[4,4,2,144,1536]{4,3,2,1,0:T(8,128)(2,1)S(1)}, bf16[4,4,2,144,1536]{4,3,2,1,0:T(8,128)(2,1)}, u32[]{:S(2)}) %copy-start.1) | copy-done | bytes 14155800
  387.6 1.2 copy-done.2
  388.8 1.0 copy-done.3
  389.8 1.0 copy-done.4
  390.8 1.0 copy-done.5
  391.8 0.9 copy-done.6
  392.7 0.9 copy-done.7
  393.7 0.9 copy-done.8
  394.6 3.6 settle.1
  398.3 0.6 fusion.1
  398.8 0.1 slice_reduce_fusion
  398.9 0.6 fusion.2
  399.6 0.7 copy.68
  400.4 0.7 copy.66
  401.1 0.7 copy.65
  401.8 0.7 copy.64
  402.5 0.1 broadcast_in_dim.61
  402.6 0.7 copy.67
  (32 shorter events, 1.3 us)
Async XLA Ops:
  0.7 0.8 copy-start
  382.6 5.0 %copy-start.1 = (bf16[4,4,2,144,1536]{4,3,2,1,0:T(8,128)(2,1)S(1)}, bf16[4,4,2,144,1536]{4,3,2,1,0:T(8,128)(2,1)}, u32[]{:S(2)}) copy-start(bf16[4,4,2,144,1536]{4,3,2,1,0:T(8,128)(2,1)} %get-tuple-element.34) | copy-start | bytes 42467332
  387.6 1.2 copy-start.2
  388.8 1.0 copy-start.3
  389.8 1.0 copy-start.4
  390.8 1.0 copy-start.5
  391.8 0.9 copy-start.6
  392.7 0.9 copy-start.7
  393.7 0.9 copy-start.8
  394.6 3.6 copy-start.9

commit v6 on v5

--- a/solution.py
+++ b/solution.py
@@ -906,6 +906,7 @@
     deal_beside(1)
     reduce_out(tuple(range(7, 16)), 11, 0, lambda x: sum_beside(x, 0, 3))
     release(1)
+    sum_beside(4, 4, 4)
     reduce_wait(11, 0)
 
     def eight(v):
@@ -928,12 +929,13 @@
     gpart[1] = lax.fori_loop(0, 3, middle_back, jnp.zeros((8, D), F32))
     share(1, 15).start()
     deal_beside(2)
-    sum_beside(4, 4, 4)
+    sum_beside(5, 5, 5)
+    sum_beside(6, 6, 6)
     shared(1, 15).wait_recv()
 
     def mixer_back(i, carry):
         gmix = nn(left[1], wt(5 + i // 2, (i % 2) * TILE))
-        sum_beside(5 + i, 5, 8)
+        sum_beside(7 + i, 7, 10)
         for h in range(2):
             j = i * 2 + h
             lanes = lanes_of(i, h)
@@ -978,8 +980,10 @@
     lax.fori_loop(0, 4, mixer_back, 0)
     release(2)
     deal_beside(3)
-    reduce_out((1, 2, 3, 4), 16, 1, lambda x: sum_beside(9 + x, 9, 12))
+    reduce_out((1, 2, 3, 4), 16, 1, lambda x: sum_beside(11 + x, 11, 14))
     release(3)
+    sum_beside(15, 15, 15)
+    sum_beside(16, 16, 16)
     reduce_wait(16, 1)
 
     def first_back(i, carry):
@@ -1036,7 +1040,7 @@
         rs_step(i, 0, PIECES + 5 * LAG - 1)
         return carry
 
-    lax.fori_loop(jnp.where(sec == 0, 13, 0), PIECES + 5 * LAG, last, 0)
+    lax.fori_loop(jnp.where(sec == 0, 17, 0), PIECES + 5 * LAG, last, 0)
     rs_finish()
     deal(5)
     share(2, 5).wait_send()
@@ -1115,16 +1119,21 @@
 
 
 def settle_kernel(source_ref, every, *refs):
-    ins, outs, (buf, sem, pick) = refs[0:7], refs[7:15], refs[15:18]
+    ins, outs, held = refs[0:7], refs[7:15], refs[15:22]
+    buf, sem, back, pick = refs[22:26]
     hid_o = outs[0]
     picks = [pltpu.make_async_copy(every.at[source_ref[m]], buf.at[m], pick.at[m]) for m in range(2)]
     for copy in picks:
         copy.start()
-    copies = [pltpu.make_async_copy(a, b, sem.at[i]) for i, (a, b) in enumerate(zip(ins, outs[1:]))]
-    for copy in copies:
+    loads = [pltpu.make_async_copy(a, b, sem.at[i]) for i, (a, b) in enumerate(zip(ins, held))]
+    copies = [pltpu.make_async_copy(a, b, back.at[i]) for i, (a, b) in enumerate(zip(held, outs[1:]))]
+    for copy in loads:
         copy.start()
     for copy in picks:
         copy.wait()
+    for load, copy in zip(loads, copies):
+        load.wait()
+        copy.start()
     hid_o[0:72, :] = buf[0].astype(F32)[0:72]
     hid_o[72:144, :] = buf[1].astype(F32)[72:144]
     for copy in copies:
@@ -1138,10 +1147,11 @@
         settle_kernel,
         name="settle",
         out_shape=(jax.ShapeDtypeStruct((HALF, D), F32),) + tuple(jax.ShapeDtypeStruct(r.shape, F32) for r in results),
-        in_specs=[pl.BlockSpec(memory_space=pltpu.SMEM), hbm] + [vmem] * 7,
+        in_specs=[pl.BlockSpec(memory_space=pltpu.SMEM)] + [hbm] * 8,
         out_specs=(vmem,) + (hbm,) * 7,
-        scratch_shapes=[pltpu.VMEM((2, HALF, D), BF16), pltpu.SemaphoreType.DMA((7,)), pltpu.SemaphoreType.DMA((2,))],
-        compiler_params=pltpu.CompilerParams(vmem_limit_bytes=32 * 2**20),
+        scratch_shapes=[pltpu.VMEM(r.shape, F32) for r in results]
+        + [pltpu.VMEM((2, HALF, D), BF16)] + [pltpu.SemaphoreType.DMA((n,)) for n in (7, 7, 2)],
+        compiler_params=pltpu.CompilerParams(vmem_limit_bytes=60 * 2**20),
     )(source, every, *results)
 
 

time: 404 us -> 385 us (0.953)
  local copies, waits for them, and re-layouts: 23.1 us -> 11.1 us
  Pallas kernels: 376 us -> 369 us
    unnamed x30 -> x14, local copies, waits for them, and re-layouts: 19.2 us -> 7.23 us
    pallas_call x1, Pallas kernels: 373 us -> 363 us  [whole(): pl.pallas_call(whole_kernel, name='whole', out_shape=(sds((4, 4, 2, HALF,...]
where the time goes in v6:
time: 385 us; the launch traced here: 384 us
  Pallas kernels  369 us (96%)
  local copies, waits for them, and re-layouts  11.1 us (3%)
    pallas_call x1, Pallas kernels, whole(): pl.pallas_call(whole_kernel, name='whole', out_shape=(sds((4, 4, 2, HALF,...  363 us

profile of v6, /device:TPU:0, one launch (start us, length us, event | category | flops | bytes accessed | tf_op | source)
XLA Modules:
  0.0 384.2 jit_solution(3716127497629180625)
XLA Ops:
  0.7 1.3 fusion.source_ref
  2.0 0.2 dynamic-slice_reduce_fusion
  2.2 0.2 reduce_window_sum.14
  2.5 0.8 pad_maximum_fusion
  3.2 0.1 convert_reduce_fusion
  3.4 0.1 stack_reshape.12
  3.5 0.1 stack_reshape.14
  3.6 0.1 stack_reshape.13
  3.7 0.8 copy.56
  4.4 0.1 reshape_squeeze.24
  4.5 0.8 copy.57
  5.3 0.1 reshape_squeeze.25
  5.4 0.8 copy.58
  6.2 0.1 reshape_squeeze.26
  6.3 0.8 copy.60
  7.0 0.1 reshape_squeeze.28
  7.1 0.8 copy.59
  7.9 0.1 reshape_squeeze.27
  8.0 0.1 concatenate.13
  8.1 1.4 maximum_maximum_fusion.small_ref
  9.5 0.9 broadcast_in_dim.58.mask_ref
  10.5 363.2 %whole.1 = (bf16[4,4,2,144,1536]{4,3,2,1,0:T(8,128)(2,1)}, f32[144,1536]{1,0:T(8,128)}, f32[48,1024]{1,0:T(8,128)}, f32[48,1024]{1,0:T(8,128)}, f32[48,1024]{1,0...) custom-call(bf16[48,1024]{1,0:T(8,128)(2,1)} %bitcast.44, ...), custom_call_target="tpu_custom_call" | custom-call | tf_op jit(solution)/shard_map/whole/pallas_call | solution.py:1072
  373.7 5.4 %settle.1 = (f32[144,1536]{1,0:T(8,128)}, f32[144,1536]{1,0:T(8,128)}, f32[48,1024]{1,0:T(8,128)}, f32[48,1024]{1,0:T(8,128)}, f32[48,1024]{1,0:T(8,128)}, /*ind...) custom-call(s32[2]{0:T(128)} %fusion.source_ref, bf16[32,144,1536]{2,1,0:T(8,128)(2,1)} %bitcast.38, ...), custom_call_target="tpu_custom_call" | custom-call | tf_op jit(solution)/shard_map/settle/pallas_call | solution.py:1146
  379.2 0.6 fusion.1
  379.7 0.1 slice_reduce_fusion
  379.8 0.6 fusion.2
  380.5 0.7 copy.68
  381.3 0.7 copy.66
  382.0 0.7 copy.65
  382.7 0.7 copy.64
  383.4 0.1 broadcast_in_dim.61
  383.5 0.7 copy.67
  (16 shorter events, 0.6 us)
Async XLA Ops:
  0.7 1.3 copy-start
  373.7 5.4 %copy-start.1 = (f32[48,256]{1,0:T(8,128)S(1)}, f32[48,256]{1,0:T(8,128)}, u32[]{:S(2)}) copy-start(f32[48,256]{1,0:T(8,128)} %get-tuple-element.46) | copy-start | bytes 147460
